TPU v7x, 128 devices: a whole 4x4x4 slice. The times are simulated.
128 devices in a mesh: lat: 8 (over x, z_lo), lon: 16 (over z_hi, y, core).
Axes of the slice: x: 4, y: 4, z: 4 (z_hi: 2, z_lo: 2; z = z_hi * 2 + z_lo), core: 2. Of those that a mesh axis runs over, the one named last changes fastest.
Arguments:
- tokens: bfloat16 [192, 384, 2, 512], P('lat', 'lon'), may hold values from -6 to 6
- cotangent: bfloat16 [192, 384, 2, 512], P('lat', 'lon'), may hold values from -6 to 6
- norm_gain: float32 [512], replicated, may hold values from 0.5 to 1.5
- w_qkv: bfloat16 [512, 1536], replicated, may hold values from -0.25 to 0.25
- w_out: bfloat16 [512, 512], replicated, may hold values from -0.25 to 0.25
- mlp_gain: float32 [512], replicated, may hold values from 0.5 to 1.5
- w_up: bfloat16 [512, 2048], replicated, may hold values from -0.25 to 0.25
- w_down: bfloat16 [2048, 512], replicated, may hold values from -0.125 to 0.125
Outputs:
- output: bfloat16 [192, 384, 2, 512], P('lat', 'lon')
- grad_tokens: bfloat16 [192, 384, 2, 512], P('lat', 'lon')
- grad_norm_gain: float32 [512], replicated
- grad_qkv: float32 [512, 1536], replicated
- grad_out: float32 [512, 512], replicated
- grad_mlp_gain: float32 [512], replicated
- grad_up: float32 [512, 2048], replicated
- grad_down: float32 [2048, 512], replicated
All inputs are finite; a program needn't handle non-finite values.
Results may differ from a plain program's by a relative error of at most 0.02.
Values may be sent and summed in bfloat16 or wider, within the bound.
No kernel may reach another device: no remote copies, remote signals or barrier semaphores. Data moves between devices by JAX's collectives and lax.ppermute only.
A program may use at most 192 MiB of HBM per device.

v0:
```python
import jax
import jax.numpy as jnp
from jax import lax
from jax.sharding import PartitionSpec as P

HD = 64
WLAT = 6
WLON = 12


def shifted_2(block, axis, distance):
    devices = range(lax.axis_size(axis))
    route = [((i - distance) % len(devices), i) for i in devices]
    return lax.ppermute(block, axis, route)


def layer_norm(values, gain):
    mean = jnp.mean(values, axis=-1, keepdims=True)
    centred = values - mean
    var = jnp.mean(centred * centred, axis=-1, keepdims=True)
    return centred * lax.rsqrt(var + 1e-05) * gain


def windows(array):
    rows, cols, levels, width = array.shape
    split = array.reshape(rows // WLAT, WLAT, cols // WLON, WLON, levels, width)
    return split.transpose(0, 2, 1, 3, 4, 5).reshape(-1, WLAT * WLON * levels, width)


def unwindows(array, rows, cols, levels):
    width = array.shape[-1]
    split = array.reshape(rows // WLAT, cols // WLON, WLAT, WLON, levels, width)
    return split.transpose(0, 2, 1, 3, 4, 5).reshape(rows, cols, levels, width)


def block(shifted, norm_gain, w_qkv, w_out, mlp_gain, w_up, w_down, last_band):
    rows, cols, levels, width = shifted.shape
    heads = width // HD
    base = windows(shifted).astype(jnp.float32)
    count, size, _ = base.shape
    normed = layer_norm(base, norm_gain).astype(jnp.bfloat16)
    qkv = jnp.dot(normed.reshape(count * size, width), w_qkv, preferred_element_type=jnp.float32)
    qkv = qkv.astype(jnp.bfloat16).reshape(count, size, 3, heads, HD)
    scores = jnp.einsum(
        "wqhd,wkhd->whqk", qkv[:, :, 0], qkv[:, :, 1], preferred_element_type=jnp.float32
    )
    scores = scores * HD ** (-0.5)
    row_ids = lax.broadcasted_iota(jnp.int32, (rows, cols, levels, 1), 0)
    groups = jnp.where(last_band & (row_ids >= rows - WLAT // 2), 1, 0).astype(jnp.int32)
    group_w = windows(groups)[:, :, 0]
    allowed = group_w[:, None, :, None] == group_w[:, None, None, :]
    scores = jnp.where(allowed, scores, -1000000000.0)
    weights = jax.nn.softmax(scores, axis=-1).astype(jnp.bfloat16)
    attended = jnp.einsum(
        "whqk,wkhd->wqhd", weights, qkv[:, :, 2], preferred_element_type=jnp.float32
    )
    attended = attended.astype(jnp.bfloat16).reshape(count * size, width)
    projected = jnp.dot(attended, w_out, preferred_element_type=jnp.float32)
    mid = (base + projected.reshape(count, size, width)).astype(jnp.bfloat16)
    mid_f = mid.astype(jnp.float32)
    normed2 = layer_norm(mid_f, mlp_gain).astype(jnp.bfloat16).reshape(count * size, width)
    hidden = jax.nn.gelu(
        jnp.dot(normed2, w_up, preferred_element_type=jnp.float32), approximate=False
    )
    down = jnp.dot(hidden.astype(jnp.bfloat16), w_down, preferred_element_type=jnp.float32)
    result = (mid_f + down.reshape(count, size, width)).astype(jnp.bfloat16)
    return unwindows(result, rows, cols, levels)


def shards(tokens, cotangent, norm_gain, w_qkv, w_out, mlp_gain, w_up, w_down):
    half_lat = WLAT // 2
    half_lon = WLON // 2
    rim_tok, rim_cot = shifted_2((tokens[:half_lat], cotangent[:half_lat]), "lat", -1)
    shifted = jnp.concatenate([tokens[half_lat:], rim_tok], axis=0)
    pulled = jnp.concatenate([cotangent[half_lat:], rim_cot], axis=0)
    rim_tok, rim_cot = shifted_2((shifted[:, :half_lon], pulled[:, :half_lon]), "lon", -1)
    shifted = jnp.concatenate([shifted[:, half_lon:], rim_tok], axis=1)
    pulled = jnp.concatenate([pulled[:, half_lon:], rim_cot], axis=1)
    last_band = lax.axis_index("lat") == lax.axis_size("lat") - 1

    def forward(tile_in, gain1, wqkv, wout, gain2, wup, wdown):
        return block(tile_in, gain1, wqkv, wout, gain2, wup, wdown, last_band)

    result, pullback = jax.vjp(forward, shifted, norm_gain, w_qkv, w_out, mlp_gain, w_up, w_down)
    tail = shifted_2(result[-half_lat:], "lat", 1)
    moved = jnp.concatenate([tail, result[:-half_lat]], axis=0)
    tail = shifted_2(moved[:, -half_lon:], "lon", 1)
    output = jnp.concatenate([tail, moved[:, :-half_lon]], axis=1)
    grads = pullback(pulled)
    grad_shift = grads[0]
    tail = shifted_2(grad_shift[-half_lat:], "lat", 1)
    moved = jnp.concatenate([tail, grad_shift[:-half_lat]], axis=0)
    tail = shifted_2(moved[:, -half_lon:], "lon", 1)
    grad_tokens = jnp.concatenate([tail, moved[:, :-half_lon]], axis=1)
    partials = tuple((part.astype(jnp.float32) for part in grads[1:]))
    sums = lax.psum(partials, ("lat", "lon"))
    return (output, grad_tokens, sums[0], sums[1], sums[2], sums[3], sums[4], sums[5])


def solution(mesh):
    return jax.shard_map(
        shards,
        mesh=mesh,
        in_specs=(
            P("lat", "lon", None, None),
            P("lat", "lon", None, None),
            P(),
            P(),
            P(),
            P(),
            P(),
            P(),
        ),
        out_specs=(
            P("lat", "lon", None, None),
            P("lat", "lon", None, None),
            P(),
            P(),
            P(),
            P(),
            P(),
            P(),
        ),
        check_vma=False,
    )
```

profile of v0, /device:TPU:1, one launch (start us, length us, event | category | flops | bytes accessed | tf_op | source)
XLA Modules:
  0.0 463.6 jit_solution(17541241586837794466)
XLA Ops:
  9.0 4.7 %collective-permute-start.4 = (bf16[3,24,2,512]{3,2,1,0:T(2,128)(2,1)}, bf16[3,24,2,512]{3,2,1,0:T(2,128)(2,1)S(1)}, u32[]{:S(2)}, u32[]{:S(2)}) collective-permute-start(bf16[3,24,2,512]{3,2,1,0:T(2,128)(2,1)} %slice.69), channel_id=1, source_target_pairs={{16,0},{32,16},{48,32},{64,48},{80,64},{96,80},{112,96},{0,112},{1... | collective-permute-start | bytes 442376 | tf_op jit(solution)/shard_map/ppermute | solution.py:14
  24.3 4.7 %collective-permute-start.5 = (bf16[24,6,2,512]{3,2,1,0:T(2,128)(2,1)}, bf16[24,6,2,512]{3,2,1,0:T(2,128)(2,1)}, u32[]{:S(2)}, u32[]{:S(2)}) collective-permute-start(bf16[24,6,2,512]{3,2,1,0:T(2,128)(2,1)} %pad_maximum_fusion.5), channel_id=1, source_target_pairs={{1,0},{2,1},{3,2},{4,3},{5,4},{6,5},{7,6},{8,7},{9,8},{10,9},{11,1... | collective-permute-start | bytes 884744 | tf_op jit(solution)/shard_map/ppermute | solution.py:14
  57.6 6.0 %convolution_convert_fusion.1 = bf16[1152,1536]{1,0:T(8,128)(2,1)} fusion(bf16[512,1536]{1,0:T(8,128)(2,1)} %param.11, f32[1152,512]{1,0:T(8,128)} %reshape.246, f32[512]{0:T(512)S(1)} %copy-done.40, f32[1152]{0:T(1024)S(1)} %rsqrt.27, f32[1152]{0:T(1024)S(1)} %div.70), kind=kOutput, calls=%fused_computation.37 | convolution fusion | flops 1816068096 | bytes 7482368 | tf_op jit(solution)/shard_map/jvp()/dot_general | solution.py:42
  63.6 9.5 %reshape.258 = bf16[8,144,3,8,64]{4,3,2,1,0:T(8,128)(2,1)} reshape(bf16[1152,1536]{1,0:T(8,128)(2,1)} %convolution_convert_fusion.1) | data formatting | bytes 7077888 | tf_op jit(solution)/shard_map/jvp()/reshape | solution.py:43
  73.1 6.3 %fusion.82 = (bf16[8,144,1,8,64]{4,3,2,1,0:T(8,128)(2,1)}, bf16[8,144,1,8,64]{4,3,2,1,0:T(8,128)(2,1)}, bf16[8,144,1,8,64]{4,3,2,1,0:T(8,128)(2,1)}) fusion(bf16[8,144,3,8,64]{4,3,2,1,0:T(8,128)(2,1)} %reshape.258), kind=kLoop, calls=%fused_computation.146 | loop fusion | bytes 7077888 | tf_op jit(solution)/shard_map/jvp()/slice | solution.py:55
  79.4 4.5 copy.98
  83.9 4.5 copy.99
  88.3 4.5 copy.100
  92.8 7.4 %fusion.44 = f32[8,8,144,144]{2,3,1,0:T(8,128)} fusion(bf16[8,144,1,8,64]{1,4,3,0,2:T(8,128)(2,1)} %copy.100, bf16[8,144,1,8,64]{1,4,3,0,2:T(8,128)(2,1)} %copy.99), kind=kOutput, calls=%fused_computation.87 | convolution fusion | flops 169869312 | bytes 7667712 | tf_op jit(solution)/shard_map/jvp(wqhd,wkhd->whqk)/dot_general | solution.py:44
  100.3 10.1 %fusion.84 = (f32[8,8,144]{2,1,0:T(8,128)S(1)}, f32[8,8,144,144]{2,3,1,0:T(8,128)S(1)}) fusion(f32[8,8,144,144]{2,3,1,0:T(8,128)} %fusion.44, pred[8,144,144]{1,2,0:T(8,128)(4,1)S(1)} %copy-done.31), kind=kOutput, calls=%fused_computation.148 | output fusion | flops 7962767 | bytes 10819584 | tf_op jit(solution)/shard_map/jvp()/sub | solution.py:53
  120.7 24.7 %multiply_convert_fusion = (bf16[1152,2048]{1,0:T(8,128)(2,1)S(1)}, f32[1152,2048]{1,0:T(8,128)}, f32[1152,2048]{1,0:T(8,128)}) fusion(bf16[1152,512]{1,0:T(8,128)(2,1)S(1)} %bitcast.121, bf16[512,2048]{1,0:T(8,128)(2,1)S(1)} %copy-done), kind=kOutput, calls=%fused_computation.19 | convolution fusion | flops 2569273344 | bytes 26869760 | tf_op jit(solution)/shard_map/jvp()/dot_general | solution.py:63
  145.4 9.5 %fusion.5 = bf16[1152,2048]{1,0:T(8,128)(2,1)S(1)} fusion(f32[1152,2048]{1,0:T(8,128)} %get-tuple-element.19, f32[1152,2048]{1,0:T(8,128)} %get-tuple-element.36, bf16[1152,512]{1,0:T(8,128)(2,1)S(1)} %copy-done.26, bf16[2048,512]{1,0:T(8,128)(2,1)S(1)} %copy-done.42), kind=kOutput, calls=%fused_computation.10 | convolution fusion | flops 2453667840 | bytes 26869760 | tf_op jit(solution)/shard_map/transpose(jvp())/dot_general | solution.py:65
  186.4 6.1 %convert_bitcast_fusion.2 = bf16[8,144,1,8,64]{1,4,3,0,2:T(8,128)(2,1)} fusion(bf16[8,8,144,144]{2,3,1,0:T(8,128)(2,1)} %copy-done.2, bf16[8,8,64,144]{3,0,2,1:T(8,128)(2,1)} %bitcast.116), kind=kOutput, calls=%fused_computation.97 | convolution fusion | flops 170459136 | bytes 5013504 | tf_op jit(solution)/shard_map/transpose(jvp(whqk,wkhd->wqhd))/dot_general | solution.py:54
  192.5 6.5 %fusion.12 = (f32[8,8,144]{2,1,0:T(8,128)S(1)}, bf16[8,8,144,144]{2,3,1,0:T(8,128)(2,1)}) fusion(f32[8,8,144,144]{2,3,1,0:T(8,128)} %copy-done.3, f32[8,8,144]{2,1,0:T(8,128)S(1)} %multiply_divide_fusion, bf16[8,144,1,8,64]{1,4,3,0,2:T(8,128)(2,1)S(1)} %copy-done.6, bf16[8,8,64,144]{3,0,2,1:T(8,128)(2,1)S(1)} %bitcast.117), kind=kOutput, calls=%fused_computation.17 | convolution fusion | flops 176495616 | bytes 10395648 | tf_op jit(solution)/shard_map/transpose(jvp(whqk,wkhd->wqhd))/dot_general | solution.py:54
  199.0 9.6 %convert_bitcast_fusion = bf16[8,144,1,8,64]{1,4,3,0,2:T(8,128)(2,1)} fusion(bf16[8,144,1,8,64]{1,4,3,0,2:T(8,128)(2,1)} %copy.100, f32[8,8,144,144]{2,3,1,0:T(8,128)} %copy-done.3, bf16[8,8,144,144]{2,3,1,0:T(8,128)(2,1)} %get-tuple-element.38, f32[8,8,144]{2,1,0:T(8,128)S(1)} %neg.22, f32[8,8,144]{2,1,0:T(8,128)S(1)} %get-tuple-element.32, ...), kind=kOutput, calls=%fused_computation.95 | convolution fusion | flops 178421760 | bytes 10561536 | tf_op jit(solution)/shard_map/transpose(jvp(wqhd,wkhd->whqk))/dot_general | solution.py:44
  208.6 10.1 %convert_bitcast_fusion.1 = bf16[8,144,1,8,64]{1,4,3,0,2:T(8,128)(2,1)} fusion(bf16[8,144,1,8,64]{1,4,3,0,2:T(8,128)(2,1)} %copy.99, f32[8,8,144,144]{2,3,1,0:T(8,128)} %copy-done.3, bf16[8,8,144,144]{2,3,1,0:T(8,128)(2,1)} %get-tuple-element.38, f32[8,8,144]{2,1,0:T(8,128)S(1)} %neg.22, f32[8,8,144]{2,1,0:T(8,128)S(1)} %get-tuple-element.32, ...), kind=kOutput, calls=%fused_computation.96 | convolution fusion | flops 178421760 | bytes 10561536 | tf_op jit(solution)/shard_map/transpose(jvp(wqhd,wkhd->whqk))/dot_general | solution.py:44
  221.3 4.9 %reshape.244 = bf16[1152,512]{0,1:T(8,128)(2,1)} reshape(bf16[8,144,8,64]{1,0,3,2:T(8,128)(2,1)} %copy.87) | data formatting | bytes 2359296 | tf_op jit(solution)/shard_map/jvp()/reshape | solution.py:57
  232.5 7.2 %copy.78 = bf16[8,144,3,8,64]{1,0,4,3,2:T(8,128)(2,1)} copy(bf16[8,144,3,8,64]{1,4,3,0,2:T(8,128)(2,1)S(1)} %pad_add_fusion) | data formatting | bytes 7077888 | tf_op jit(solution)/shard_map/transpose(jvp())/add_any | solution.py:45
  239.7 10.4 %reshape.241 = bf16[1152,1536]{0,1:T(8,128)(2,1)} reshape(bf16[8,144,3,8,64]{1,0,4,3,2:T(8,128)(2,1)} %copy.78) | data formatting | bytes 7077888 | tf_op jit(solution)/shard_map/transpose(jvp())/reshape | solution.py:43
  250.1 5.5 %fusion.28 = f32[1152,512]{1,0:T(8,128)} fusion(bf16[1152,1536]{0,1:T(8,128)(2,1)} %reshape.241, bf16[512,1536]{1,0:T(8,128)(2,1)S(1)} %copy-done.43), kind=kOutput, calls=%fused_computation.56 | convolution fusion | flops 1813118976 | bytes 7471104 | tf_op jit(solution)/shard_map/transpose(jvp())/dot_general | solution.py:42
  259.7 5.5 %multiply_reduce_fusion = (f32[512]{0:T(512)S(1)}, f32[4,2,6,12,2]{4,3,2,1,0:T(8,128)S(1)}, bf16[4,2,6,12,2,512]{5,4,3,2,1,0:T(2,128)(2,1)S(1)}) fusion(f32[4,2,6,12,2,512]{5,4,3,2,1,0:T(2,128)} %reshape.250, f32[4,2,6,12,2]{4,3,2,1,0:T(8,128)} %get-tuple-element.28, f32[4,2,6,12,2]{4,3,2,1,0:T(8,128)S(1)} %copy-done.13, f32[512]{0:T(512)S(1)} %copy-done.41, ...), kind=kLoop, calls=%fused_computation.79 | loop fusion | flops 5896576 | bytes 4736512 | tf_op jit(solution)/shard_map/transpose(jvp())/reduce_sum | solution.py:21
  265.8 5.9 %fusion.27 = f32[512,1536]{1,0:T(8,128)} fusion(bf16[1152,512]{1,0:T(8,128)(2,1)S(1)} %convert_element_type.211, bf16[1152,1536]{0,1:T(8,128)(2,1)} %reshape.241), kind=kOutput, calls=%fused_computation.54 | convolution fusion | flops 1813512192 | bytes 7864320 | tf_op jit(solution)/shard_map/transpose(jvp())/dot_general | solution.py:42
  292.4 71.5 %all-reduce.3 = (f32[512]{0:T(512)}, f32[512]{0:T(512)}) all-reduce(f32[512]{0:T(512)S(1)} %get-tuple-element.8, f32[512]{0:T(512)S(1)} %get-tuple-element.10), channel_id=1, replica_groups=mesh['lat'=8,'lon'=16] {'lat','lon'}, use_global_device_ids=true, to_apply=%region_12.13 | all-reduce | flops 1024 | bytes 8192 | tf_op jit(solution)/shard_map/psum | solution.py:96
  370.5 75.4 %all-reduce.7.cloned.1.call-done = (f32[512,1536]{1,0:T(8,128)}, f32[512,512]{1,0:T(8,128)}, f32[512,2048]{1,0:T(8,128)}, f32[2048,512]{1,0:T(8,128)}) async-done(((f32[512,1536]{1,0:T(8,128)}, f32[512,512]{1,0:T(8,128)}, f32[512,2048]{1,0:T(8,128)}, f32[2048,512]{1,0:T(8,128)}), (f32[512,1536]{1,0:T(8,128)}, f32[512,512]{1,0:T(8,128)}, f32[512,2048]{1,0:T(8,128)}, ...) | async-done | bytes 12582928 | tf_op jit(solution)/shard_map/psum | solution.py:96
  (184 shorter events, 133.8 us)
Async XLA Ops:
  7.2 113.5 %copy-start = (bf16[512,2048]{1,0:T(8,128)(2,1)S(1)}, bf16[512,2048]{1,0:T(8,128)(2,1)}, u32[]{:S(2)}) copy-start(bf16[512,2048]{1,0:T(8,128)(2,1)} %param.14) | copy-start | bytes 6291460
  7.2 438.8 %all-reduce.7.cloned.1.call-start = ((), (), s32[]{:S(2)}) async-start(), calls=%async_computation | async-start | bytes 25165824 | tf_op jit(solution)/shard_map/psum | solution.py:96
  9.0 14.1 %collective-permute-start.4 = (bf16[3,24,2,512]{3,2,1,0:T(2,128)(2,1)}, bf16[3,24,2,512]{3,2,1,0:T(2,128)(2,1)S(1)}, u32[]{:S(2)}, u32[]{:S(2)}) collective-permute-start(bf16[3,24,2,512]{3,2,1,0:T(2,128)(2,1)} %slice.69), channel_id=1, source_target_pairs={{16,0},{32,16},{48,32},{64,48},{80,64},{96,80},{112,96},{0,112},{1... | collective-permute-start | bytes 442376 | tf_op jit(solution)/shard_map/ppermute | solution.py:14
  15.4 4.7 %collective-permute-start = (bf16[3,24,2,512]{3,2,1,0:T(2,128)(2,1)}, bf16[3,24,2,512]{3,2,1,0:T(2,128)(2,1)}, u32[]{:S(2)}, u32[]{:S(2)}) collective-permute-start(bf16[3,24,2,512]{3,2,1,0:T(2,128)(2,1)} %slice.58), channel_id=1, source_target_pairs={{16,0},{32,16},{48,32},{64,48},{80,64},{96,80},{112,96},{0,112},{1... | collective-permute-start | bytes 442376 | tf_op jit(solution)/shard_map/ppermute | solution.py:14
  21.2 11.0 %collective-permute-start.1 = (bf16[24,6,2,512]{3,2,1,0:T(2,128)(2,1)S(1)}, bf16[24,6,2,512]{3,2,1,0:T(2,128)(2,1)S(1)}, u32[]{:S(2)}, u32[]{:S(2)}) collective-permute-start(bf16[24,6,2,512]{3,2,1,0:T(2,128)(2,1)S(1)} %pad_maximum_fusion.7), channel_id=1, source_target_pairs={{1,0},{2,1},{3,2},{4,3},{5,4},{6,5},{7,6},{8,7},{9,8},{10,9},{11,1... | collective-permute-start | bytes 884744 | tf_op jit(solution)/shard_map/ppermute | solution.py:14
  24.3 26.4 %collective-permute-start.5 = (bf16[24,6,2,512]{3,2,1,0:T(2,128)(2,1)}, bf16[24,6,2,512]{3,2,1,0:T(2,128)(2,1)}, u32[]{:S(2)}, u32[]{:S(2)}) collective-permute-start(bf16[24,6,2,512]{3,2,1,0:T(2,128)(2,1)} %pad_maximum_fusion.5), channel_id=1, source_target_pairs={{1,0},{2,1},{3,2},{4,3},{5,4},{6,5},{7,6},{8,7},{9,8},{10,9},{11,1... | collective-permute-start | bytes 884744 | tf_op jit(solution)/shard_map/ppermute | solution.py:14
  34.8 5.6 %copy-start.12 = (f32[4,2,6,12,2]{4,3,2,1,0:T(8,128)}, f32[4,2,6,12,2]{4,3,2,1,0:T(8,128)S(1)}, u32[]{:S(2)}) copy-start(f32[4,2,6,12,2]{4,3,2,1,0:T(8,128)S(1)} %broadcast_multiply_fusion) | copy-start | bytes 13828
  40.6 17.0 %copy-start.35 = (f32[1152]{0:T(1024)}, f32[1152]{0:T(1024)S(1)}, u32[]{:S(2)}) copy-start(f32[1152]{0:T(1024)S(1)} %div.70) | copy-start | bytes 13828
  50.6 5.5 %copy-start.33 = (f32[1152]{0:T(1024)}, f32[1152]{0:T(1024)S(1)}, u32[]{:S(2)}) copy-start(f32[1152]{0:T(1024)S(1)} %add.55) | copy-start | bytes 13828
  50.6 7.0 %copy-start.37 = (f32[1152]{0:T(1024)}, f32[1152]{0:T(1024)S(1)}, u32[]{:S(2)}) copy-start(f32[1152]{0:T(1024)S(1)} %rsqrt.27) | copy-start | bytes 13828
  92.8 7.4 %copy-start.31 = (pred[8,144,144]{1,2,0:T(8,128)(4,1)S(1)}, pred[8,144,144]{1,2,0:T(8,128)(4,1)}, u32[]{:S(2)}) copy-start(pred[8,144,144]{1,2,0:T(8,128)(4,1)} %broadcast_compare_fusion) | copy-start | bytes 497668
  120.7 24.7 %copy-start.26 = (bf16[1152,512]{1,0:T(8,128)(2,1)S(1)}, bf16[1152,512]{1,0:T(8,128)(2,1)}, u32[]{:S(2)}) copy-start(bf16[1152,512]{1,0:T(8,128)(2,1)} %reshape.238) | copy-start | bytes 3538948
  120.7 24.7 %copy-start.42 = (bf16[2048,512]{1,0:T(8,128)(2,1)S(1)}, bf16[2048,512]{1,0:T(8,128)(2,1)}, u32[]{:S(2)}) copy-start(bf16[2048,512]{1,0:T(8,128)(2,1)} %param.15) | copy-start | bytes 6291460
  186.4 6.1 %copy-start.6 = (bf16[8,144,1,8,64]{1,4,3,0,2:T(8,128)(2,1)S(1)}, bf16[8,144,1,8,64]{1,4,3,0,2:T(8,128)(2,1)}, u32[]{:S(2)}) copy-start(bf16[8,144,1,8,64]{1,4,3,0,2:T(8,128)(2,1)} %copy.98) | copy-start | bytes 3538948
  186.4 6.1 %copy-start.10 = (bf16[8,144,8,64]{1,0,3,2:T(8,128)(2,1)S(1)}, bf16[8,144,8,64]{1,0,3,2:T(8,128)(2,1)}, u32[]{:S(2)}) copy-start(bf16[8,144,8,64]{1,0,3,2:T(8,128)(2,1)} %reshape.240) | copy-start | bytes 3538948
  192.5 6.5 %copy-start.32 = (pred[8,144,144]{1,2,0:T(8,128)(4,1)S(1)}, pred[8,144,144]{1,2,0:T(8,128)(4,1)}, u32[]{:S(2)}) copy-start(pred[8,144,144]{1,2,0:T(8,128)(4,1)} %broadcast_compare_fusion) | copy-start | bytes 497668
  208.6 10.1 %copy-start.8 = (bf16[8,8,64,144]{3,2,1,0:T(8,128)(2,1)S(1)}, bf16[8,8,64,144]{3,2,1,0:T(8,128)(2,1)}, u32[]{:S(2)}) copy-start(bf16[8,8,64,144]{3,2,1,0:T(8,128)(2,1)} %copy-done.7) | copy-start | bytes 3538948
  239.7 10.4 %copy-start.43 = (bf16[512,1536]{1,0:T(8,128)(2,1)S(1)}, bf16[512,1536]{1,0:T(8,128)(2,1)}, u32[]{:S(2)}) copy-start(bf16[512,1536]{1,0:T(8,128)(2,1)} %param.11) | copy-start | bytes 4718596
  276.2 6.2 %collective-permute-start.2 = (bf16[3,24,2,512]{3,2,1,0:T(2,128)(2,1)S(1)}, bf16[3,24,2,512]{3,2,1,0:T(2,128)(2,1)S(1)}, u32[]{:S(2)}, u32[]{:S(2)}) collective-permute-start(bf16[3,24,2,512]{3,2,1,0:T(2,128)(2,1)S(1)} %slice.81), channel_id=1, source_target_pairs={{112,0},{0,16},{16,32},{32,48},{48,64},{64,80},{80,96},{96,112},{1... | collective-permute-start | bytes 442376 | tf_op jit(solution)/shard_map/ppermute | solution.py:14
  276.9 6.7 %copy-start.19 = (bf16[8,144,512]{2,1,0:T(8,128)(2,1)S(1)}, bf16[8,144,512]{2,1,0:T(8,128)(2,1)}, u32[]{:S(2)}) copy-start(bf16[8,144,512]{2,1,0:T(8,128)(2,1)} %copy-done.17) | copy-start | bytes 3538948
  283.5 80.9 %collective-permute-start.3 = (bf16[24,6,2,512]{3,2,1,0:T(2,128)(2,1)}, bf16[24,6,2,512]{3,2,1,0:T(2,128)(2,1)}, u32[]{:S(2)}, u32[]{:S(2)}) collective-permute-start(bf16[24,6,2,512]{3,2,1,0:T(2,128)(2,1)} %pad_maximum_fusion.6), channel_id=1, source_target_pairs={{15,0},{0,1},{1,2},{2,3},{3,4},{4,5},{5,6},{6,7},{7,8},{8,9},{9,10... | collective-permute-start | bytes 884744 | tf_op jit(solution)/shard_map/ppermute | solution.py:14
  291.4 72.5 %collective-permute-start.6 = (bf16[3,24,2,512]{3,2,1,0:T(2,128)(2,1)S(1)}, bf16[3,24,2,512]{3,2,1,0:T(2,128)(2,1)S(1)}, u32[]{:S(2)}, u32[]{:S(2)}) collective-permute-start(bf16[3,24,2,512]{3,2,1,0:T(2,128)(2,1)S(1)} %slice.85), channel_id=1, source_target_pairs={{112,0},{0,16},{16,32},{32,48},{48,64},{64,80},{80,96},{96,112},{1... | collective-permute-start | bytes 442376 | tf_op jit(solution)/shard_map/ppermute | solution.py:14
  364.3 3.7 collective-permute-start.7
  450.8 5.7 %copy-start.1 = (bf16[512,2048]{1,0:T(8,128)(2,1)S(1)}, bf16[512,2048]{1,0:T(8,128)(2,1)}, u32[]{:S(2)}) copy-start(bf16[512,2048]{1,0:T(8,128)(2,1)} %param.14) | copy-start | bytes 6291460
  (29 other events, 91.8 us)
Sparse Core Ops, SparseCore 0:
  271.9 174.0 all-reduce.6
where the time goes:
time: 469 us; the launch traced here: 464 us
  matrix products  117 us (25%)
  local copies, waits for them, and re-layouts  108 us (23%)
  waiting for transfers between devices  78.1 us (17%)
  blocking collectives  71.5 us (15%)
  other arithmetic  62 us (13%)
  between operations  14.9 us (3%)
  starting transfers between devices  12.1 us (3%)
    psum x1, waiting for transfers between devices, shards(): sums = lax.psum(partials, ('lat', 'lon'))  75.4 us
    psum x1, blocking collectives, shards(): sums = lax.psum(partials, ('lat', 'lon'))  71.5 us
    dot_general x3, matrix products, block(): jnp.dot(normed2, w_up, preferred_element_type=jnp.float32)  32.8 us
    unnamed x95, local copies, waits for them, and re-layouts  28.6 us
    dot_general x3, matrix products, block(): jnp.einsum('wqhd,wkhd->whqk', qkv[:, :, 0], qkv[:, :, 1], preferred_eleme...  27.1 us
    reshape x2, local copies, waits for them, and re-layouts, block(): qkv = qkv.astype(jnp.bfloat16).reshape(count, size, 3, heads, HD)  19.9 us
    dot_general x3, matrix products, block(): jnp.dot(hidden.astype(jnp.bfloat16), w_down, preferred_element_type=jnp.f...  18 us
    dot_general x3, matrix products, block(): jnp.dot(normed.reshape(count * size, width), w_qkv, preferred_element_typ...  17.4 us
  transfers between devices with their start and end apart: 9, of which 4 were waited for; matrix products, arithmetic and copies ran while one was open for 11% of the time, Pallas kernels for 0%

commit v1 on v0

v1 whole, which is shorter than its diff:
```python
import functools

import jax
import jax.numpy as jnp
from jax import lax
from jax.experimental import pallas as pl
from jax.experimental.pallas import tpu as pltpu
from jax.sharding import PartitionSpec as P

HD = 64
WLAT = 6
WLON = 12
LEV = 2
WIN = WLAT * WLON * LEV
D = 512
FF = 2048
HALF_LAT = WLAT // 2
HALF_LON = WLON // 2
EPS = 1e-05
F32 = jnp.float32
BF16 = jnp.bfloat16
PAIR = 2 * HD
LIMIT = 56 * 1024 * 1024


def mm(a, b):
    return lax.dot_general(a, b, (((1,), (0,)), ((), ())), preferred_element_type=F32)


def mm_t(a, b):
    return lax.dot_general(a, b, (((1,), (1,)), ((), ())), preferred_element_type=F32)


def t_mm(a, b):
    return lax.dot_general(a, b, (((0,), (0,)), ((), ())), preferred_element_type=F32)


def normalised(values):
    mean = jnp.mean(values, axis=-1, keepdims=True)
    centred = values - mean
    var = jnp.mean(centred * centred, axis=-1, keepdims=True)
    scale = lax.rsqrt(var + EPS)
    return centred * scale, scale


def norm_pullback(xhat, scale, gain, grad):
    dxhat = grad * gain
    m1 = jnp.mean(dxhat, axis=-1, keepdims=True)
    m2 = jnp.mean(dxhat * xhat, axis=-1, keepdims=True)
    return scale * (dxhat - m1 - xhat * m2)


def gelu_parts(x):
    a = jnp.abs(x)
    t = 1.0 / (1.0 + (0.3275911 * 0.7071067811865476) * a)
    e = jnp.exp(-0.5 * x * x)
    poly = t * (0.127414796 + t * (-0.142248368 + t * (0.7107068705 + t * (-0.7265760135 + t * 0.5307027145))))
    tail = poly * e
    cdf = jnp.where(x >= 0.0, 1.0 - tail, tail)
    return cdf, 0.3989422804014327 * e


def front_kernel(flag_ref, x_ref, g1_ref, wqkv_ref, wout_ref, g2_ref,
                 n1_ref, qkv_ref, p_ref, att_ref, mid_ref, n2_ref):
    tokens = x_ref.shape[0]
    count = tokens // WIN
    per_row = count // 4
    gain1 = g1_ref[...]
    gain2 = g2_ref[...]

    @pl.loop(0, count)
    def _(w):
        rows = pl.ds(pl.multiple_of(w * WIN, WIN), WIN)
        xhat, _ = normalised(x_ref[rows, :].astype(F32))
        n1_ref[rows, :] = (xhat * gain1).astype(BF16)

    big = 2 * WIN

    @pl.loop(0, tokens // big)
    def _(b):
        rows = pl.ds(pl.multiple_of(b * big, big), big)
        n1 = n1_ref[rows, :]
        qkv_ref[rows, 0:D] = (mm(n1, wqkv_ref[:, 0:D]).astype(BF16) * 0.125).astype(BF16)
        qkv_ref[rows, D:2 * D] = mm(n1, wqkv_ref[:, D:2 * D]).astype(BF16)
        qkv_ref[rows, 2 * D:3 * D] = mm(n1, wqkv_ref[:, 2 * D:3 * D]).astype(BF16)

    key_group = lax.broadcasted_iota(jnp.int32, (WIN, WIN), 0) >= WIN // 2
    query_group = lax.broadcasted_iota(jnp.int32, (WIN, WIN), 1) >= WIN // 2
    split = key_group != query_group
    low = lax.broadcasted_iota(jnp.int32, (WIN, PAIR), 1) < HD

    @pl.loop(0, count)
    def _(w):
        rows = pl.ds(pl.multiple_of(w * WIN, WIN), WIN)
        cut = jnp.logical_and(flag_ref[0] == 1, w >= count - per_row)
        masked = jnp.logical_and(split, cut)
        for pair in range(D // PAIR):
            lanes = slice(pair * PAIR, (pair + 1) * PAIR)
            q = qkv_ref[rows, pair * PAIR:(pair + 1) * PAIR]
            k = qkv_ref[rows, D + pair * PAIR:D + (pair + 1) * PAIR]
            v = qkv_ref[rows, 2 * D + pair * PAIR:2 * D + (pair + 1) * PAIR]
            outs = []
            for h in range(2):
                mine = low if h == 0 else jnp.logical_not(low)
                kh = jnp.where(mine, k, jnp.zeros_like(k))
                s = mm_t(kh, q)
                s = jnp.where(masked, -1000000000.0, s)
                e = jnp.exp(s - jnp.max(s, axis=0, keepdims=True))
                p = (e * (1.0 / jnp.sum(e, axis=0, keepdims=True))).astype(BF16)
                p_ref[w, 2 * pair + h] = p
                outs.append(t_mm(p, v))
            att_ref[rows, lanes] = jnp.where(low, outs[0], outs[1]).astype(BF16)

    @pl.loop(0, tokens // big)
    def _(b):
        rows = pl.ds(pl.multiple_of(b * big, big), big)
        mid = (x_ref[rows, :].astype(F32) + mm(att_ref[rows, :], wout_ref[...])).astype(BF16)
        mid_ref[rows, :] = mid
        xhat, _ = normalised(mid.astype(F32))
        n2_ref[rows, :] = (xhat * gain2).astype(BF16)


def mlp_kernel(n2_ref, cot_ref, mid_ref, g2_ref, wup_ref, wdown_ref,
               res_ref, dmid_ref, dg2_ref, gup_ref, gdown_ref,
               down_acc, dn2_acc, hid_ref, du_ref):
    step = pl.program_id(0)
    tokens = n2_ref.shape[0]
    big = 2 * WIN

    @pl.when(step == 0)
    def _():
        down_acc[...] = jnp.zeros_like(down_acc)
        dn2_acc[...] = jnp.zeros_like(dn2_acc)

    @pl.loop(0, tokens // big)
    def _(b):
        rows = pl.ds(pl.multiple_of(b * big, big), big)
        up = mm(n2_ref[rows, :], wup_ref[...])
        cdf, pdf = gelu_parts(up)
        hid = (up * cdf).astype(BF16)
        hid_ref[rows, :] = hid
        dhid = mm_t(cot_ref[rows, :], wdown_ref[...]).astype(BF16).astype(F32)
        du = (dhid * (cdf + up * pdf)).astype(BF16)
        du_ref[rows, :] = du
        down_acc[rows, :] += mm(hid, wdown_ref[...])
        dn2_acc[rows, :] += mm_t(du, wup_ref[...])

    gdown_ref[...] = t_mm(hid_ref[...], cot_ref[...]).astype(BF16)
    gup_ref[...] = t_mm(n2_ref[...], du_ref[...]).astype(BF16)

    @pl.when(step == pl.num_programs(0) - 1)
    def _():
        gain2 = g2_ref[...]
        dg2_ref[...] = jnp.zeros_like(dg2_ref)

        @pl.loop(0, tokens // big)
        def _(b):
            rows = pl.ds(pl.multiple_of(b * big, big), big)
            mid = mid_ref[rows, :].astype(F32)
            res_ref[rows, :] = (mid + down_acc[rows, :]).astype(BF16)
            xhat, scale = normalised(mid)
            dn2 = dn2_acc[rows, :].astype(BF16).astype(F32)
            dg2_ref[...] += jnp.sum(dn2 * xhat, axis=0, keepdims=True)
            dmid = cot_ref[rows, :].astype(F32) + norm_pullback(xhat, scale, gain2, dn2)
            dmid_ref[rows, :] = dmid.astype(BF16)


def back_kernel(x_ref, dmid_ref, n1_ref, qkv_ref, p_ref, att_ref, g1_ref, wqkv_ref, wout_ref,
                dx_ref, dg1_ref, gqkv_ref, gout_ref, datt_ref, dqkv_ref):
    tokens = x_ref.shape[0]
    count = tokens // WIN
    gain1 = g1_ref[...]
    big = 2 * WIN

    gout_ref[...] = t_mm(att_ref[...], dmid_ref[...]).astype(BF16)

    @pl.loop(0, tokens // big)
    def _(b):
        rows = pl.ds(pl.multiple_of(b * big, big), big)
        datt_ref[rows, :] = mm_t(dmid_ref[rows, :], wout_ref[...]).astype(BF16)

    low = lax.broadcasted_iota(jnp.int32, (WIN, PAIR), 1) < HD

    @pl.loop(0, count)
    def _(w):
        rows = pl.ds(pl.multiple_of(w * WIN, WIN), WIN)
        for pair in range(D // PAIR):
            lanes = slice(pair * PAIR, (pair + 1) * PAIR)
            q = qkv_ref[rows, pair * PAIR:(pair + 1) * PAIR]
            k = qkv_ref[rows, D + pair * PAIR:D + (pair + 1) * PAIR]
            v = qkv_ref[rows, 2 * D + pair * PAIR:2 * D + (pair + 1) * PAIR]
            da = datt_ref[rows, lanes]
            dqs, dks, dvs = [], [], []
            for h in range(2):
                mine = low if h == 0 else jnp.logical_not(low)
                vh = jnp.where(mine, v, jnp.zeros_like(v))
                p = p_ref[w, 2 * pair + h]
                pf = p.astype(F32)
                dp = mm_t(vh, da).astype(BF16).astype(F32)
                ds = (pf * (dp - jnp.sum(dp * pf, axis=0, keepdims=True))).astype(BF16)
                dvs.append(mm(p, da))
                dks.append(mm(ds, q))
                dqs.append(t_mm(ds, k))
            dqkv_ref[rows, pair * PAIR:(pair + 1) * PAIR] = (jnp.where(low, dqs[0], dqs[1]) * 0.125).astype(BF16)
            dqkv_ref[rows, D + pair * PAIR:D + (pair + 1) * PAIR] = jnp.where(low, dks[0], dks[1]).astype(BF16)
            dqkv_ref[rows, 2 * D + pair * PAIR:2 * D + (pair + 1) * PAIR] = jnp.where(low, dvs[0], dvs[1]).astype(BF16)

    for part in range(3):
        gqkv_ref[:, part * D:(part + 1) * D] = t_mm(n1_ref[...], dqkv_ref[:, part * D:(part + 1) * D]).astype(BF16)

    dg1_ref[...] = jnp.zeros_like(dg1_ref)

    @pl.loop(0, tokens // big)
    def _(b):
        rows = pl.ds(pl.multiple_of(b * big, big), big)
        dn1 = mm_t(dqkv_ref[rows, :], wqkv_ref[...]).astype(BF16).astype(F32)
        xhat, scale = normalised(x_ref[rows, :].astype(F32))
        dg1_ref[...] += jnp.sum(dn1 * xhat, axis=0, keepdims=True)
        dx = dmid_ref[rows, :].astype(F32) + norm_pullback(xhat, scale, gain1, dn1)
        dx_ref[rows, :] = dx.astype(BF16)


def params():
    return pltpu.CompilerParams(vmem_limit_bytes=LIMIT)


def shape(dims, dtype=BF16):
    return jax.ShapeDtypeStruct(dims, dtype)


def front(flag, x, g1, wqkv, wout, g2):
    tokens = x.shape[0]
    count = tokens // WIN
    vm = pl.BlockSpec(memory_space=pltpu.VMEM)
    return pl.pallas_call(
        front_kernel,
        name="front",
        in_specs=[pl.BlockSpec(memory_space=pltpu.SMEM)] + [vm] * 5,
        out_specs=[vm] * 6,
        out_shape=[
            shape((tokens, D)),
            shape((tokens, 3 * D)),
            shape((count, D // HD, WIN, WIN)),
            shape((tokens, D)),
            shape((tokens, D)),
            shape((tokens, D)),
        ],
        compiler_params=params(),
    )(flag, x, g1, wqkv, wout, g2)


def mlp(n2, cot, mid, g2, wup, wdown, chunk=512):
    tokens = n2.shape[0]
    whole = pl.BlockSpec((tokens, D), lambda i: (0, 0))
    gain = pl.BlockSpec((1, D), lambda i: (0, 0))
    cols = pl.BlockSpec((D, chunk), lambda i: (0, i))
    rows = pl.BlockSpec((chunk, D), lambda i: (i, 0))
    return pl.pallas_call(
        mlp_kernel,
        name="mlp",
        grid=(FF // chunk,),
        in_specs=[whole, whole, whole, gain, cols, rows],
        out_specs=[whole, whole, gain, cols, rows],
        out_shape=[
            shape((tokens, D)),
            shape((tokens, D)),
            shape((1, D), F32),
            shape((D, FF)),
            shape((FF, D)),
        ],
        scratch_shapes=[
            pltpu.VMEM((tokens, D), F32),
            pltpu.VMEM((tokens, D), F32),
            pltpu.VMEM((tokens, chunk), BF16),
            pltpu.VMEM((tokens, chunk), BF16),
        ],
        compiler_params=params(),
    )(n2, cot, mid, g2, wup, wdown)


def back(x, dmid, n1, qkv, p, att, g1, wqkv, wout):
    tokens = x.shape[0]
    vm = pl.BlockSpec(memory_space=pltpu.VMEM)
    return pl.pallas_call(
        back_kernel,
        name="back",
        in_specs=[vm] * 9,
        out_specs=[vm] * 4,
        out_shape=[
            shape((tokens, D)),
            shape((1, D), F32),
            shape((D, 3 * D)),
            shape((D, D)),
        ],
        scratch_shapes=[
            pltpu.VMEM((tokens, D), BF16),
            pltpu.VMEM((tokens, 3 * D), BF16),
        ],
        compiler_params=params(),
    )(x, dmid, n1, qkv, p, att, g1, wqkv, wout)


def shifted_2(block, axis, distance):
    devices = range(lax.axis_size(axis))
    route = [((i - distance) % len(devices), i) for i in devices]
    return lax.ppermute(block, axis, route)


def windows(array):
    rows, cols, levels, width = array.shape
    split = array.reshape(rows // WLAT, WLAT, cols // WLON, WLON, levels, width)
    return split.transpose(0, 2, 1, 3, 4, 5).reshape(-1, width)


def unwindows(array, rows, cols, levels):
    width = array.shape[-1]
    split = array.reshape(rows // WLAT, cols // WLON, WLAT, WLON, levels, width)
    return split.transpose(0, 2, 1, 3, 4, 5).reshape(rows, cols, levels, width)


def pull_rims(block):
    rim = shifted_2(block[:HALF_LAT], "lat", -1)
    block = jnp.concatenate([block[HALF_LAT:], rim], axis=0)
    rim = shifted_2(block[:, :HALF_LON], "lon", -1)
    return jnp.concatenate([block[:, HALF_LON:], rim], axis=1)


def push_rims(block):
    tail = shifted_2(block[-HALF_LAT:], "lat", 1)
    moved = jnp.concatenate([tail, block[:-HALF_LAT]], axis=0)
    tail = shifted_2(moved[:, -HALF_LON:], "lon", 1)
    return jnp.concatenate([tail, moved[:, :-HALF_LON]], axis=1)


def shards(tokens, cotangent, norm_gain, w_qkv, w_out, mlp_gain, w_up, w_down):
    rows, cols, levels, _ = tokens.shape
    g1 = norm_gain.reshape(1, D)
    g2 = mlp_gain.reshape(1, D)
    x = windows(pull_rims(tokens))
    cot = windows(pull_rims(cotangent))
    last_band = lax.axis_index("lat") == lax.axis_size("lat") - 1
    flag = last_band.astype(jnp.int32).reshape(1)

    n1, qkv, p, att, mid, n2 = front(flag, x, g1, w_qkv, w_out, g2)
    res, dmid, dg2, gup, gdown = mlp(n2, cot, mid, g2, w_up, w_down)
    dx, dg1, gqkv, gout = back(x, dmid, n1, qkv, p, att, g1, w_qkv, w_out)

    output = push_rims(unwindows(res, rows, cols, levels))
    grad_tokens = push_rims(unwindows(dx, rows, cols, levels))
    sums = lax.psum((gup, gdown, gqkv, gout), ("lat", "lon"))
    gains = lax.psum(jnp.concatenate([dg1, dg2]), ("lat", "lon"))
    gup, gdown, gqkv, gout = (part.astype(F32) for part in sums)
    return (output, grad_tokens, gains[0], gqkv, gout, gains[1], gup, gdown)


def solution(mesh):
    field = P("lat", "lon", None, None)
    return jax.shard_map(
        shards,
        mesh=mesh,
        in_specs=(field, field, P(), P(), P(), P(), P(), P()),
        out_specs=(field, field, P(), P(), P(), P(), P(), P()),
        check_vma=False,
    )
```

time: 469 us -> 295 us (0.63); the launches traced: 464 us -> 295 us
  matrix products: 117 us -> 0 us
  local copies, waits for them, and re-layouts: 108 us -> 19.9 us
  Pallas kernels: 0 us -> 82.5 us
  other arithmetic: 62 us -> 21.4 us
    dot_general x18 -> x0, matrix products: 117 us -> none  [the longest x3 32.8 us: block(): jnp.dot(normed2, w_up, preferred_element_type=jnp.float32)]
    pallas_call x0 -> x3, Pallas kernels: none -> 82.5 us  [the longest x1 31.2 us: mlp(): pl.pallas_call(mlp_kernel, name='mlp', grid=(FF // chunk,), in_specs=[who...]
    reshape x6 -> x4, local copies, waits for them, and re-layouts: 32.9 us -> 4.55 us  [the longest x2 2.59 us: windows(): return split.transpose(0, 2, 1, 3, 4, 5).reshape(-1, width)]
    unnamed x95 -> x14, local copies, waits for them, and re-layouts: 28.6 us -> 1.32 us
    convert_element_type x7 -> x0, local copies, waits for them, and re-layouts: 20 us -> none  [the longest x2 8.02 us: block(): base = windows(shifted).astype(jnp.float32)]
    reduce_sum x7 -> x0, other arithmetic: 15.8 us -> none  [the longest x3 7.88 us: layer_norm(): return centred * lax.rsqrt(var + 1e-05) * gain]
    sub x1 -> x0, other arithmetic: 10.1 us -> none  [block(): weights = jax.nn.softmax(scores, axis=-1).astype(jnp.bfloat16)]
    add_any x1 -> x0, local copies, waits for them, and re-layouts: 7.21 us -> none  [block(): qkv[:, :, 0]]
  transfers between devices with their start and end apart: 9 -> 9, of which waited for: 4 -> 3; matrix products, arithmetic and copies ran while one was open for 11% -> 9% of each run, Pallas kernels for 0% -> 0%
where the time goes in v1:
time: 295 us
  Pallas kernels  82.5 us (28%)
  waiting for transfers between devices  74.3 us (25%)
  blocking collectives  69.8 us (24%)
  other arithmetic  21.4 us (7%)
  local copies, waits for them, and re-layouts  19.9 us (7%)
  between operations  14.3 us (5%)
  starting transfers between devices  12.4 us (4%)
    psum x1, waiting for transfers between devices, shards(): sums = lax.psum((gup, gdown, gqkv, gout), ('lat', 'lon'))  71 us
    psum x1, blocking collectives, shards(): gains = lax.psum(jnp.concatenate([dg1, dg2]), ('lat', 'lon'))  69.8 us
    pallas_call x1, Pallas kernels, mlp(): pl.pallas_call(mlp_kernel, name='mlp', grid=(FF // chunk,), in_specs=[who...  31.2 us
    pallas_call x1, Pallas kernels, back(): pl.pallas_call(back_kernel, name='back', in_specs=[vm] * 9, out_specs=[vm...  30 us
    pallas_call x1, Pallas kernels, front(): pl.pallas_call(front_kernel, name='front', in_specs=[pl.BlockSpec(memory_...  21.3 us
    ppermute x8, starting transfers between devices, shifted_2(): return lax.ppermute(block, axis, route)  12.3 us
    convert_element_type x4, other arithmetic, shards(): gup, gdown, gqkv, gout = (part.astype(F32) for part in sums)  9.48 us
  transfers between devices with their start and end apart: 9, of which 3 were waited for; matrix products, arithmetic and copies ran while one was open for 9% of the time, Pallas kernels for 0%

profile of v1, /device:TPU:1, one launch (start us, length us, event | category | flops | bytes accessed | tf_op | source)
XLA Modules:
  0.0 294.7 jit_solution(13610320561927183616)
XLA Ops:
  8.2 4.7 %collective-permute-start = (bf16[3,24,2,512]{3,2,1,0:T(2,128)(2,1)S(1)}, bf16[3,24,2,512]{3,2,1,0:T(2,128)(2,1)S(1)}, u32[]{:S(2)}, u32[]{:S(2)}) collective-permute-start(bf16[3,24,2,512]{3,2,1,0:T(2,128)(2,1)S(1)} %slice.55), channel_id=1, source_target_pairs={{16,0},{32,16},{48,32},{64,48},{80,64},{96,80},{112,96},{0,112},{1... | collective-permute-start | bytes 442376 | tf_op jit(solution)/shard_map/ppermute | solution.py:306
  14.2 2.1 slice.54
  19.1 5.5 %collective-permute-start.3 = (bf16[24,6,2,512]{3,2,1,0:T(2,128)(2,1)S(1)}, bf16[24,6,2,512]{3,2,1,0:T(2,128)(2,1)S(1)}, u32[]{:S(2)}, u32[]{:S(2)}) collective-permute-start(bf16[24,6,2,512]{3,2,1,0:T(2,128)(2,1)S(1)} %pad_maximum_fusion.6), channel_id=1, source_target_pairs={{1,0},{2,1},{3,2},{4,3},{5,4},{6,5},{7,6},{8,7},{9,8},{10,9},{11,1... | collective-permute-start | bytes 884744 | tf_op jit(solution)/shard_map/ppermute | solution.py:306
  25.7 1.2 fusion.2
  27.0 1.5 pad_maximum_fusion.2
  29.5 1.3 reshape.54.x_ref
  30.8 1.5 pad_maximum_fusion.3
  33.3 1.3 reshape.58.cot_ref
  34.6 21.3 %front.1 = (bf16[1152,512]{1,0:T(8,128)(2,1)}, bf16[1152,1536]{1,0:T(8,128)(2,1)}, bf16[8,8,144,144]{3,2,1,0:T(8,128)(2,1)}, bf16[1152,512]{1,0:T(8,128)(2,1)}, ...) custom-call(s32[1]{0:T(128)} %bitcast.flag_ref, bf16[1152,512]{1,0:T(8,128)(2,1)} %reshape.54.x_ref, ...), custom_call_target="tpu_custom_call" | custom-call | tf_op jit(solution)/shard_map/front/pallas_call | solution.py:235
  55.9 31.2 %mlp.1 = (bf16[1152,512]{1,0:T(8,128)(2,1)}, bf16[1152,512]{1,0:T(8,128)(2,1)}, f32[1,512]{1,0:T(1,128)}, bf16[512,2048]{1,0:T(8,128)(2,1)}, bf16[2048,512]{1,0:T(8,128)(2,1)}) custom-call(bf16[1152,512]{1,0:T(8,128)(2,1)} %get-tuple-element.23.n2_ref, bf16[1152,512]{1,0:T(8,128)(2,1)} %reshape.58.cot_ref, bf16[1152,512]{1,0:T(8,128)(2,1)} %get-tuple-element.24.mid_ref, ...), custom_call_target="tpu_custom_call" | custom-call | tf_op jit(solution)/shard_map/mlp/pallas_call | solution.py:258
  87.1 30.0 %back.1 = (bf16[1152,512]{1,0:T(8,128)(2,1)}, f32[1,512]{1,0:T(1,128)}, bf16[512,1536]{1,0:T(8,128)(2,1)}, bf16[512,512]{1,0:T(8,128)(2,1)}) custom-call(bf16[1152,512]{1,0:T(8,128)(2,1)} %reshape.54.x_ref, bf16[1152,512]{1,0:T(8,128)(2,1)} %get-tuple-element.26.dmid_ref, bf16[1152,512]{1,0:T(8,128)(2,1)} %get-tuple-element.27.n1_ref, ...), custom_call_target="tpu_custom_call" | custom-call | tf_op jit(solution)/shard_map/back/pallas_call | solution.py:284
  117.2 1.2 copy-done.3
  118.9 1.3 copy.18
  121.6 2.9 reshape.61
  124.4 1.2 copy.19
  127.7 69.8 %psum.35 = f32[2,512]{1,0:T(2,128)S(1)} all-reduce(f32[2,512]{1,0:T(2,128)S(1)} %pad_maximum_fusion.8), channel_id=1, replica_groups=mesh['lat'=8,'lon'=16] {'lat','lon'}, use_global_device_ids=true, to_apply=%region_0.0 | all-reduce | flops 1024 | bytes 8192 | tf_op jit(solution)/shard_map/psum | solution.py:351
  199.0 2.6 collective-permute-done.5
  201.6 2.5 fusion.1
  204.8 2.5 fusion
  207.3 71.0 %all-reduce.3.cloned.1.call-done = (bf16[512,1536]{1,0:T(8,128)(2,1)}, bf16[512,512]{1,0:T(8,128)(2,1)}, bf16[512,2048]{1,0:T(8,128)(2,1)}, bf16[2048,512]{1,0:T(8,128)(2,1)}) async-done(((bf16[512,1536]{1,0:T(8,128)(2,1)}, bf16[512,512]{1,0:T(8,128)(2,1)}, bf16[512,2048]{1,0:T(8,128)(2,1)}, bf16[2048,512]{1,0:T(8,128)(2,1)}), (bf16[512,1536]{1,0:T(8,128)(2,1)}, bf16[512,512]{1,0:T(8,128)(2,1)}, ...) | async-done | bytes 6291472 | tf_op jit(solution)/shard_map/psum | solution.py:350
  278.3 2.3 convert_element_type.14
  280.6 2.1 convert_element_type.13
  282.7 2.5 convert_element_type.15
  285.2 2.6 convert_element_type.16
  (45 shorter events, 14.3 us)
Async XLA Ops:
  7.2 271.1 %all-reduce.3.cloned.1.call-start = ((), (), s32[]{:S(2)}) async-start(), calls=%async_computation | async-start | bytes 12582912 | tf_op jit(solution)/shard_map/psum | solution.py:350
  8.2 8.0 %copy-start.4 = (bf16[24,24,2,512]{3,2,1,0:T(2,128)(2,1)S(1)}, bf16[24,24,2,512]{3,2,1,0:T(2,128)(2,1)}, u32[]{:S(2)}) copy-start(bf16[24,24,2,512]{3,2,1,0:T(2,128)(2,1)} %param.9) | copy-start | bytes 3538948
  8.2 8.9 %collective-permute-start = (bf16[3,24,2,512]{3,2,1,0:T(2,128)(2,1)S(1)}, bf16[3,24,2,512]{3,2,1,0:T(2,128)(2,1)S(1)}, u32[]{:S(2)}, u32[]{:S(2)}) collective-permute-start(bf16[3,24,2,512]{3,2,1,0:T(2,128)(2,1)S(1)} %slice.55), channel_id=1, source_target_pairs={{16,0},{32,16},{48,32},{64,48},{80,64},{96,80},{112,96},{0,112},{1... | collective-permute-start | bytes 442376 | tf_op jit(solution)/shard_map/ppermute | solution.py:306
  14.0 4.7 %collective-permute-start.2 = (bf16[3,24,2,512]{3,2,1,0:T(2,128)(2,1)S(1)}, bf16[3,24,2,512]{3,2,1,0:T(2,128)(2,1)S(1)}, u32[]{:S(2)}, u32[]{:S(2)}) collective-permute-start(bf16[3,24,2,512]{3,2,1,0:T(2,128)(2,1)S(1)} %slice.59), channel_id=1, source_target_pairs={{16,0},{32,16},{48,32},{64,48},{80,64},{96,80},{112,96},{0,112},{1... | collective-permute-start | bytes 442376 | tf_op jit(solution)/shard_map/ppermute | solution.py:306
  17.6 9.4 %collective-permute-start.1 = (bf16[24,6,2,512]{3,2,1,0:T(2,128)(2,1)S(1)}, bf16[24,6,2,512]{3,2,1,0:T(2,128)(2,1)S(1)}, u32[]{:S(2)}, u32[]{:S(2)}) collective-permute-start(bf16[24,6,2,512]{3,2,1,0:T(2,128)(2,1)S(1)} %pad_maximum_fusion.7), channel_id=1, source_target_pairs={{1,0},{2,1},{3,2},{4,3},{5,4},{6,5},{7,6},{8,7},{9,8},{10,9},{11,1... | collective-permute-start | bytes 884744 | tf_op jit(solution)/shard_map/ppermute | solution.py:306
  19.1 11.7 %collective-permute-start.3 = (bf16[24,6,2,512]{3,2,1,0:T(2,128)(2,1)S(1)}, bf16[24,6,2,512]{3,2,1,0:T(2,128)(2,1)S(1)}, u32[]{:S(2)}, u32[]{:S(2)}) collective-permute-start(bf16[24,6,2,512]{3,2,1,0:T(2,128)(2,1)S(1)} %pad_maximum_fusion.6), channel_id=1, source_target_pairs={{1,0},{2,1},{3,2},{4,3},{5,4},{6,5},{7,6},{8,7},{9,8},{10,9},{11,1... | collective-permute-start | bytes 884744 | tf_op jit(solution)/shard_map/ppermute | solution.py:306
  117.1 1.3 copy-start.3
  120.9 76.6 %collective-permute-start.4 = (bf16[3,24,2,512]{3,2,1,0:T(2,128)(2,1)}, bf16[3,24,2,512]{3,2,1,0:T(2,128)(2,1)S(1)}, u32[]{:S(2)}, u32[]{:S(2)}) collective-permute-start(bf16[3,24,2,512]{3,2,1,0:T(2,128)(2,1)} %slice.76), channel_id=1, source_target_pairs={{112,0},{0,16},{16,32},{32,48},{48,64},{64,80},{80,96},{96,112},{1... | collective-permute-start | bytes 442376 | tf_op jit(solution)/shard_map/ppermute | solution.py:306
  126.7 1.0 copy-start.5
  126.7 1.0 copy-start.6
  127.6 71.0 %collective-permute-start.6 = (bf16[3,24,2,512]{3,2,1,0:T(2,128)(2,1)S(1)}, bf16[3,24,2,512]{3,2,1,0:T(2,128)(2,1)S(1)}, u32[]{:S(2)}, u32[]{:S(2)}) collective-permute-start(bf16[3,24,2,512]{3,2,1,0:T(2,128)(2,1)S(1)} %slice.78), channel_id=1, source_target_pairs={{112,0},{0,16},{16,32},{32,48},{48,64},{64,80},{80,96},{96,112},{1... | collective-permute-start | bytes 442376 | tf_op jit(solution)/shard_map/ppermute | solution.py:306
  197.9 3.7 %collective-permute-start.5 = (bf16[24,6,2,512]{3,2,1,0:T(2,128)(2,1)S(1)}, bf16[24,6,2,512]{3,2,1,0:T(2,128)(2,1)S(1)}, u32[]{:S(2)}, u32[]{:S(2)}) collective-permute-start(bf16[24,6,2,512]{3,2,1,0:T(2,128)(2,1)S(1)} %pad_maximum_fusion.5), channel_id=1, source_target_pairs={{15,0},{0,1},{1,2},{2,3},{3,4},{4,5},{5,6},{6,7},{7,8},{8,9},{9,10... | collective-permute-start | bytes 884744 | tf_op jit(solution)/shard_map/ppermute | solution.py:306
  199.0 5.9 %collective-permute-start.7 = (bf16[24,6,2,512]{3,2,1,0:T(2,128)(2,1)S(1)}, bf16[24,6,2,512]{3,2,1,0:T(2,128)(2,1)S(1)}, u32[]{:S(2)}, u32[]{:S(2)}) collective-permute-start(bf16[24,6,2,512]{3,2,1,0:T(2,128)(2,1)S(1)} %pad_maximum_fusion.4), channel_id=1, source_target_pairs={{15,0},{0,1},{1,2},{2,3},{3,4},{4,5},{5,6},{6,7},{7,8},{8,9},{9,10... | collective-permute-start | bytes 884744 | tf_op jit(solution)/shard_map/ppermute | solution.py:306
  278.3 2.3 copy-start.2
  280.6 2.1 copy-start.1
  282.7 2.5 copy-start
Sparse Core Ops, SparseCore 0:
  117.3 160.9 all-reduce.2

commit v2 on v1

--- a/solution.py
+++ b/solution.py
@@ -60,8 +60,68 @@
     return cdf, 0.3989422804014327 * e
 
 
-def front_kernel(flag_ref, x_ref, g1_ref, wqkv_ref, wout_ref, g2_ref,
-                 n1_ref, qkv_ref, p_ref, att_ref, mid_ref, n2_ref):
+BANDS = 4
+SIDES = 2
+
+
+def strips():
+    for band in range(BANDS):
+        first = HALF_LAT + band * WLAT
+        last = band == BANDS - 1
+        across = [(0, WLAT, first, False)]
+        if last:
+            across = [(0, HALF_LAT, first, False), (HALF_LAT, HALF_LAT, 0, True)]
+        for side in range(SIDES):
+            left = HALF_LON + side * WLON
+            along = [(0, WLON, left, False)]
+            if side == SIDES - 1:
+                along = [(0, HALF_LON, left, False), (HALF_LON, HALF_LON, 0, True)]
+            for at_row, rows, row, far_row in across:
+                for at_col, cols, col, far_col in along:
+                    piece = 2 * far_row + far_col
+                    if far_row and not far_col:
+                        col -= HALF_LON
+                    if far_col and not far_row:
+                        row -= HALF_LAT
+                    yield (
+                        band, side, pl.ds(at_row, rows), pl.ds(at_col, cols),
+                        piece, pl.ds(row, rows), pl.ds(col, cols),
+                    )
+
+
+STRIPS = len(list(strips()))
+
+
+def gather_windows(which, field, rim_lon, rim_lat, corner, buffer, sems):
+    copies = []
+    for i, (band, side, to_rows, to_cols, piece, rows, cols) in enumerate(strips()):
+        source = field if piece == 0 else (None, rim_lon, rim_lat, corner)[piece].at[which]
+        copies.append(pltpu.make_async_copy(
+            source.at[rows, cols], buffer.at[band, side, to_rows, to_cols], sems.at[i]))
+    return copies
+
+
+def scatter_windows(which, buffer, field, rim_lon, rim_lat, corner, sems):
+    copies = []
+    for i, (band, side, to_rows, to_cols, piece, rows, cols) in enumerate(strips()):
+        target = field if piece == 0 else (None, rim_lon, rim_lat, corner)[piece].at[which]
+        copies.append(pltpu.make_async_copy(
+            buffer.at[band, side, to_rows, to_cols], target.at[rows, cols], sems.at[i]))
+    return copies
+
+
+def front_kernel(flag_ref, tok_ref, cot_ref, lon_ref, lat_ref, corner_ref, g1_ref, wqkv_ref, wout_ref, g2_ref,
+                 x_ref, cotw_ref, n1_ref, qkv_ref, p_ref, att_ref, mid_ref, n2_ref, tok_buf, cot_buf, sems):
+    tok_copies = gather_windows(0, tok_ref, lon_ref, lat_ref, corner_ref, tok_buf, sems.at[0])
+    cot_copies = gather_windows(1, cot_ref, lon_ref, lat_ref, corner_ref, cot_buf, sems.at[1])
+    for copy in tok_copies + cot_copies:
+        copy.start()
+    for copy in tok_copies:
+        copy.wait()
+    for band in range(BANDS):
+        for side in range(SIDES):
+            w = band * SIDES + side
+            x_ref[w * WIN:(w + 1) * WIN, :] = tok_buf[band, side].reshape(WIN, D)
     tokens = x_ref.shape[0]
     count = tokens // WIN
     per_row = count // 4
@@ -119,18 +179,17 @@
         xhat, _ = normalised(mid.astype(F32))
         n2_ref[rows, :] = (xhat * gain2).astype(BF16)
 
-
-def mlp_kernel(n2_ref, cot_ref, mid_ref, g2_ref, wup_ref, wdown_ref,
-               res_ref, dmid_ref, dg2_ref, gup_ref, gdown_ref,
-               down_acc, dn2_acc, hid_ref, du_ref):
-    step = pl.program_id(0)
+    for copy in cot_copies:
+        copy.wait()
+    for band in range(BANDS):
+        for side in range(SIDES):
+            w = band * SIDES + side
+            cotw_ref[w * WIN:(w + 1) * WIN, :] = cot_buf[band, side].reshape(WIN, D)
+
+
+def mlp_chunk(n2_ref, cot_ref, wup_ref, wdown_ref, gup_ref, gdown_ref, down_acc, dn2_acc, hid_ref, du_ref):
     tokens = n2_ref.shape[0]
     big = 2 * WIN
-
-    @pl.when(step == 0)
-    def _():
-        down_acc[...] = jnp.zeros_like(down_acc)
-        dn2_acc[...] = jnp.zeros_like(dn2_acc)
 
     @pl.loop(0, tokens // big)
     def _(b):
@@ -148,7 +207,34 @@
     gdown_ref[...] = t_mm(hid_ref[...], cot_ref[...]).astype(BF16)
     gup_ref[...] = t_mm(n2_ref[...], du_ref[...]).astype(BF16)
 
-    @pl.when(step == pl.num_programs(0) - 1)
+
+def mlp_send_kernel(me_ref, n2_ref, cot_ref, wup_ref, wdown_ref,
+                    down_acc, dn2_acc, gup_ref, gdown_ref, hid_ref, du_ref):
+    del me_ref
+
+    @pl.when(pl.program_id(0) == 0)
+    def _():
+        down_acc[...] = jnp.zeros_like(down_acc)
+        dn2_acc[...] = jnp.zeros_like(dn2_acc)
+
+    mlp_chunk(n2_ref, cot_ref, wup_ref, wdown_ref, gup_ref, gdown_ref, down_acc, dn2_acc, hid_ref, du_ref)
+
+
+def mlp_keep_kernel(me_ref, n2_ref, cot_ref, wup_ref, wdown_ref, mid_ref, g2_ref, down_in, dn2_in,
+                    res_ref, dmid_ref, dg2_ref, gup_ref, gdown_ref,
+                    down_acc, dn2_acc, hid_ref, du_ref):
+    del me_ref
+    tokens = n2_ref.shape[0]
+    big = 2 * WIN
+
+    @pl.when(pl.program_id(0) == 0)
+    def _():
+        down_acc[...] = down_in[...]
+        dn2_acc[...] = dn2_in[...]
+
+    mlp_chunk(n2_ref, cot_ref, wup_ref, wdown_ref, gup_ref, gdown_ref, down_acc, dn2_acc, hid_ref, du_ref)
+
+    @pl.when(pl.program_id(0) == pl.num_programs(0) - 1)
     def _():
         gain2 = g2_ref[...]
         dg2_ref[...] = jnp.zeros_like(dg2_ref)
@@ -165,14 +251,46 @@
             dmid_ref[rows, :] = dmid.astype(BF16)
 
 
-def back_kernel(x_ref, dmid_ref, n1_ref, qkv_ref, p_ref, att_ref, g1_ref, wqkv_ref, wout_ref,
-                dx_ref, dg1_ref, gqkv_ref, gout_ref, datt_ref, dqkv_ref):
-    tokens = x_ref.shape[0]
+HALF = D // 2
+SLOTS = 72
+CHIPS_N = 64
+
+
+def att_grads(half, n1_ref, dqkv_ref, att_ref, dmid_ref, dg1, dg2, out_ref):
+    per = D // (CHIPS_N // 4)
+    lanes = pl.ds(pl.multiple_of(half * HALF, HALF), HALF)
+    for part in range(4):
+        if part < 3:
+            part_lanes = pl.ds(pl.multiple_of(part * D + half * HALF, HALF), HALF)
+            grad = t_mm(n1_ref[...], dqkv_ref[:, part_lanes])
+        else:
+            grad = t_mm(att_ref[...], dmid_ref[:, lanes])
+        grad = grad.astype(BF16)
+        first = part * (CHIPS_N // 4)
+        for block in range(2):
+            piece = grad[:, block * 128:(block + 1) * 128].reshape(CHIPS_N // 4, per, 128)
+            out_ref[first:first + CHIPS_N // 4, block * per:(block + 1) * per, :] = piece
+    out_ref[:, 2 * per:, :] = jnp.zeros((CHIPS_N, SLOTS - 2 * per, 128), BF16)
+    gain = jnp.where(half == 0, dg1, dg2)
+    for block in range(D // 128):
+        row = jnp.broadcast_to(gain[:, block * 128:(block + 1) * 128], (SLOTS - 2 * per, 128))
+        out_ref[block, 2 * per:, :] = row.astype(BF16)
+
+
+def back_kernel(me_ref, dmid_ref, n1_ref, qkv_ref, p_ref, att_ref, x_ref, g1_ref, wqkv_ref, wout_ref, dg2_ref, res_ref,
+                out_ref, grad_ref, lon_ref, lat_ref, corner_ref, dqkv_ref, dg1_ref, send_ref,
+                datt_ref, dx_ref, res_buf, dx_buf, sems):
+    for band in range(BANDS):
+        for side in range(SIDES):
+            w = band * SIDES + side
+            res_buf[band, side] = res_ref[w * WIN:(w + 1) * WIN, :].reshape(WLAT, WLON, LEV, D)
+    res_copies = scatter_windows(0, res_buf, out_ref, lon_ref, lat_ref, corner_ref, sems.at[0])
+    for copy in res_copies:
+        copy.start()
+    tokens = dmid_ref.shape[0]
     count = tokens // WIN
     gain1 = g1_ref[...]
     big = 2 * WIN
-
-    gout_ref[...] = t_mm(att_ref[...], dmid_ref[...]).astype(BF16)
 
     @pl.loop(0, tokens // big)
     def _(b):
@@ -205,9 +323,6 @@
             dqkv_ref[rows, D + pair * PAIR:D + (pair + 1) * PAIR] = jnp.where(low, dks[0], dks[1]).astype(BF16)
             dqkv_ref[rows, 2 * D + pair * PAIR:2 * D + (pair + 1) * PAIR] = jnp.where(low, dvs[0], dvs[1]).astype(BF16)
 
-    for part in range(3):
-        gqkv_ref[:, part * D:(part + 1) * D] = t_mm(n1_ref[...], dqkv_ref[:, part * D:(part + 1) * D]).astype(BF16)
-
     dg1_ref[...] = jnp.zeros_like(dg1_ref)
 
     @pl.loop(0, tokens // big)
@@ -219,25 +334,146 @@
         dx = dmid_ref[rows, :].astype(F32) + norm_pullback(xhat, scale, gain1, dn1)
         dx_ref[rows, :] = dx.astype(BF16)
 
+    for band in range(BANDS):
+        for side in range(SIDES):
+            w = band * SIDES + side
+            dx_buf[band, side] = dx_ref[w * WIN:(w + 1) * WIN, :].reshape(WLAT, WLON, LEV, D)
+    dx_copies = scatter_windows(1, dx_buf, grad_ref, lon_ref, lat_ref, corner_ref, sems.at[1])
+    for copy in dx_copies:
+        copy.start()
+    att_grads(1 - me_ref[0], n1_ref, dqkv_ref, att_ref, dmid_ref, dg1_ref[...], dg2_ref[...], send_ref)
+    for copy in res_copies + dx_copies:
+        copy.wait()
+
+
+def keep_kernel(me_ref, n1_ref, dqkv_ref, att_ref, dmid_ref, dg1_ref, dg2_ref, keep_ref):
+    att_grads(me_ref[0], n1_ref, dqkv_ref, att_ref, dmid_ref, dg1_ref[...], dg2_ref[...], keep_ref)
+
+
+def share_kernel(in_ref, out_ref):
+    total = in_ref[0].astype(F32)
+    for chip in range(1, in_ref.shape[0]):
+        total += in_ref[chip].astype(F32)
+    total = total.astype(BF16)
+    for chip in range(in_ref.shape[0]):
+        out_ref[chip] = total
+
+
+def unpack_mlp_kernel(me_ref, mine_ref, theirs_ref, gup_ref, gdown_ref):
+    wide = FF // 2
+    for ref, half in ((mine_ref, me_ref[0]), (theirs_ref, 1 - me_ref[0])):
+        for block in range(2):
+            lanes = pl.ds(pl.multiple_of(half * wide + block * D, D), D)
+            gup_ref[:, lanes] = ref[block * D:(block + 1) * D, :].astype(F32)
+        gdown_ref[pl.ds(pl.multiple_of(half * wide, wide), wide), :] = ref[2 * D:, :].astype(F32)
+
+
+def unpack_att_kernel(me_ref, mine_ref, theirs_ref, gqkv_ref, gout_ref, gains_ref):
+    quarter = CHIPS_N // 4
+    per = D // quarter
+    for ref, half in ((mine_ref, me_ref[0]), (theirs_ref, 1 - me_ref[0])):
+        for part in range(4):
+            for block in range(2):
+                piece = ref[part * quarter:(part + 1) * quarter, block * per:(block + 1) * per, :]
+                piece = piece.reshape(D, 128).astype(F32)
+                out, first = (gqkv_ref, part * D) if part < 3 else (gout_ref, 0)
+                out[:, pl.ds(pl.multiple_of(half * HALF + (first + block * 128), 128), 128)] = piece
+        for block in range(D // 128):
+            gains_ref[pl.ds(pl.multiple_of(half * 8, 8), 8), block * 128:(block + 1) * 128] = ref[block, 2 * per:, :].astype(F32)
+
+
+def pack_kernel(tok_ref, cot_ref, lon_ref, lat_ref, corner_ref, sems):
+    copies = []
+    for which, ref in enumerate((tok_ref, cot_ref)):
+        below, right = pl.ds(HALF_LAT, ref.shape[0] - HALF_LAT), pl.ds(HALF_LON, ref.shape[1] - HALF_LON)
+        top, left = pl.ds(0, HALF_LAT), pl.ds(0, HALF_LON)
+        for i, (rows, cols, out) in enumerate(((below, left, lon_ref), (top, right, lat_ref), (top, left, corner_ref))):
+            copies.append(pltpu.make_async_copy(ref.at[rows, cols], out.at[which], sems.at[which, i]))
+    for copy in copies:
+        copy.start()
+    for copy in copies:
+        copy.wait()
+
+
+def place_kernel(out_in, grad_in, lon_ref, lat_ref, corner_ref, out_ref, grad_ref, sems):
+    del out_in, grad_in
+    copies = []
+    for which, ref in enumerate((out_ref, grad_ref)):
+        below, right = pl.ds(HALF_LAT, ref.shape[0] - HALF_LAT), pl.ds(HALF_LON, ref.shape[1] - HALF_LON)
+        top, left = pl.ds(0, HALF_LAT), pl.ds(0, HALF_LON)
+        for i, (rows, cols, rim) in enumerate(((below, left, lon_ref), (top, right, lat_ref), (top, left, corner_ref))):
+            copies.append(pltpu.make_async_copy(rim.at[which], ref.at[rows, cols], sems.at[which, i]))
+    for copy in copies:
+        copy.start()
+    for copy in copies:
+        copy.wait()
+
 
 def params():
     return pltpu.CompilerParams(vmem_limit_bytes=LIMIT)
 
 
+def cost(flops, moved):
+    return pl.CostEstimate(flops=flops, bytes_accessed=moved, transcendentals=0)
+
+
 def shape(dims, dtype=BF16):
     return jax.ShapeDtypeStruct(dims, dtype)
 
 
-def front(flag, x, g1, wqkv, wout, g2):
-    tokens = x.shape[0]
+SM = pl.BlockSpec(memory_space=pltpu.SMEM)
+VM = pl.BlockSpec(memory_space=pltpu.VMEM)
+
+
+ANY = pl.BlockSpec(memory_space=pl.ANY)
+
+
+def rim_shapes(rows, cols, levels):
+    return [
+        shape((2, rows - HALF_LAT, HALF_LON, levels, D)),
+        shape((2, HALF_LAT, cols - HALF_LON, levels, D)),
+        shape((2, HALF_LAT, HALF_LON, levels, D)),
+    ]
+
+
+def pack(tokens, cotangent):
+    return pl.pallas_call(
+        pack_kernel,
+        name="pack",
+        in_specs=[ANY] * 2,
+        out_specs=[ANY] * 3,
+        out_shape=rim_shapes(*tokens.shape[:3]),
+        scratch_shapes=[pltpu.SemaphoreType.DMA((2, 3))],
+    )(tokens, cotangent)
+
+
+def place(output, grad, lon, lat, corner):
+    return pl.pallas_call(
+        place_kernel,
+        name="place",
+        in_specs=[ANY] * 5,
+        out_specs=[ANY] * 2,
+        out_shape=[shape(output.shape), shape(grad.shape)],
+        input_output_aliases={0: 0, 1: 1},
+        scratch_shapes=[pltpu.SemaphoreType.DMA((2, 3))],
+        cost_estimate=cost(10**9, 2**21),
+    )(output, grad, lon, lat, corner)
+
+
+WINDOWED = (BANDS, SIDES, WLAT, WLON, LEV, D)
+
+
+def front(flag, tok, cot, lon, lat, corner, g1, wqkv, wout, g2):
+    tokens = tok.size // D
     count = tokens // WIN
-    vm = pl.BlockSpec(memory_space=pltpu.VMEM)
     return pl.pallas_call(
         front_kernel,
         name="front",
-        in_specs=[pl.BlockSpec(memory_space=pltpu.SMEM)] + [vm] * 5,
-        out_specs=[vm] * 6,
+        in_specs=[SM] + [ANY] * 5 + [VM] * 4,
+        out_specs=[VM] * 8,
         out_shape=[
+            shape((tokens, D)),
+            shape((tokens, D)),
             shape((tokens, D)),
             shape((tokens, 3 * D)),
             shape((count, D // HD, WIN, WIN)),
@@ -245,116 +481,218 @@
             shape((tokens, D)),
             shape((tokens, D)),
         ],
+        scratch_shapes=[
+            pltpu.VMEM(WINDOWED, BF16),
+            pltpu.VMEM(WINDOWED, BF16),
+            pltpu.SemaphoreType.DMA((2, STRIPS)),
+        ],
         compiler_params=params(),
-    )(flag, x, g1, wqkv, wout, g2)
-
-
-def mlp(n2, cot, mid, g2, wup, wdown, chunk=512):
+        cost_estimate=cost(20 * 10**9, 10 * 2**20),
+    )(flag, tok, cot, lon, lat, corner, g1, wqkv, wout, g2)
+
+
+def mlp_specs(tokens, chunk):
+    steps = FF // chunk // 2
+    specs = {
+        "whole": pl.BlockSpec((tokens, D), lambda i, me: (0, 0)),
+        "gain": pl.BlockSpec((1, D), lambda i, me: (0, 0)),
+        "out": pl.BlockSpec((chunk, D), lambda i, me: (i, 0)),
+    }
+    for name, other in (("send", 1), ("keep", 0)):
+        def place(i, me, other=other):
+            return (me[0] if other == 0 else 1 - me[0]) * steps + i
+        specs[name] = [
+            pl.BlockSpec((D, chunk), lambda i, me, place=place: (0, place(i, me))),
+            pl.BlockSpec((chunk, D), lambda i, me, place=place: (place(i, me), 0)),
+        ]
+    return specs, steps
+
+
+def mlp_send(me, n2, cot, wup, wdown, chunk=512):
     tokens = n2.shape[0]
-    whole = pl.BlockSpec((tokens, D), lambda i: (0, 0))
-    gain = pl.BlockSpec((1, D), lambda i: (0, 0))
-    cols = pl.BlockSpec((D, chunk), lambda i: (0, i))
-    rows = pl.BlockSpec((chunk, D), lambda i: (i, 0))
-    return pl.pallas_call(
-        mlp_kernel,
-        name="mlp",
-        grid=(FF // chunk,),
-        in_specs=[whole, whole, whole, gain, cols, rows],
-        out_specs=[whole, whole, gain, cols, rows],
+    specs, steps = mlp_specs(tokens, chunk)
+    whole, out = specs["whole"], specs["out"]
+    return pl.pallas_call(
+        mlp_send_kernel,
+        name="mlp_send",
+        grid_spec=pltpu.PrefetchScalarGridSpec(
+            num_scalar_prefetch=1,
+            grid=(steps,),
+            in_specs=[whole, whole] + specs["send"],
+            out_specs=[whole, whole, out, out],
+            scratch_shapes=[pltpu.VMEM((tokens, chunk), BF16), pltpu.VMEM((tokens, chunk), BF16)],
+        ),
+        out_shape=[shape((tokens, D), F32), shape((tokens, D), F32), shape((FF // 2, D)), shape((FF // 2, D))],
+        compiler_params=params(),
+        cost_estimate=cost(16 * 10**9, 10 * 2**20),
+    )(me, n2, cot, wup, wdown)
+
+
+def mlp_keep(me, n2, cot, wup, wdown, mid, g2, down, dn2, chunk=512):
+    tokens = n2.shape[0]
+    specs, steps = mlp_specs(tokens, chunk)
+    whole, out, gain = specs["whole"], specs["out"], specs["gain"]
+    return pl.pallas_call(
+        mlp_keep_kernel,
+        name="mlp_keep",
+        grid_spec=pltpu.PrefetchScalarGridSpec(
+            num_scalar_prefetch=1,
+            grid=(steps,),
+            in_specs=[whole, whole] + specs["keep"] + [whole, gain, whole, whole],
+            out_specs=[whole, whole, gain, out, out],
+            scratch_shapes=[
+                pltpu.VMEM((tokens, D), F32),
+                pltpu.VMEM((tokens, D), F32),
+                pltpu.VMEM((tokens, chunk), BF16),
+                pltpu.VMEM((tokens, chunk), BF16),
+            ],
+        ),
         out_shape=[
             shape((tokens, D)),
             shape((tokens, D)),
             shape((1, D), F32),
-            shape((D, FF)),
-            shape((FF, D)),
-        ],
-        scratch_shapes=[
-            pltpu.VMEM((tokens, D), F32),
-            pltpu.VMEM((tokens, D), F32),
-            pltpu.VMEM((tokens, chunk), BF16),
-            pltpu.VMEM((tokens, chunk), BF16),
+            shape((FF // 2, D)),
+            shape((FF // 2, D)),
         ],
         compiler_params=params(),
-    )(n2, cot, mid, g2, wup, wdown)
-
-
-def back(x, dmid, n1, qkv, p, att, g1, wqkv, wout):
+        cost_estimate=cost(16 * 10**9, 10 * 2**20),
+    )(me, n2, cot, wup, wdown, mid, g2, down, dn2)
+
+
+def back(me, dmid, n1, qkv, p, att, x, g1, wqkv, wout, dg2, res, field):
     tokens = x.shape[0]
-    vm = pl.BlockSpec(memory_space=pltpu.VMEM)
     return pl.pallas_call(
         back_kernel,
         name="back",
-        in_specs=[vm] * 9,
-        out_specs=[vm] * 4,
-        out_shape=[
-            shape((tokens, D)),
+        in_specs=[SM] + [VM] * 11,
+        out_specs=[ANY] * 5 + [VM] * 3,
+        out_shape=[shape(field), shape(field)] + rim_shapes(*field[:3]) + [
+            shape((tokens, 3 * D)),
             shape((1, D), F32),
-            shape((D, 3 * D)),
-            shape((D, D)),
+            shape((CHIPS_N, SLOTS, 128)),
         ],
         scratch_shapes=[
             pltpu.VMEM((tokens, D), BF16),
-            pltpu.VMEM((tokens, 3 * D), BF16),
+            pltpu.VMEM((tokens, D), BF16),
+            pltpu.VMEM(WINDOWED, BF16),
+            pltpu.VMEM(WINDOWED, BF16),
+            pltpu.SemaphoreType.DMA((2, STRIPS)),
         ],
         compiler_params=params(),
-    )(x, dmid, n1, qkv, p, att, g1, wqkv, wout)
-
-
-def shifted_2(block, axis, distance):
-    devices = range(lax.axis_size(axis))
-    route = [((i - distance) % len(devices), i) for i in devices]
-    return lax.ppermute(block, axis, route)
-
-
-def windows(array):
-    rows, cols, levels, width = array.shape
-    split = array.reshape(rows // WLAT, WLAT, cols // WLON, WLON, levels, width)
-    return split.transpose(0, 2, 1, 3, 4, 5).reshape(-1, width)
-
-
-def unwindows(array, rows, cols, levels):
-    width = array.shape[-1]
-    split = array.reshape(rows // WLAT, cols // WLON, WLAT, WLON, levels, width)
-    return split.transpose(0, 2, 1, 3, 4, 5).reshape(rows, cols, levels, width)
-
-
-def pull_rims(block):
-    rim = shifted_2(block[:HALF_LAT], "lat", -1)
-    block = jnp.concatenate([block[HALF_LAT:], rim], axis=0)
-    rim = shifted_2(block[:, :HALF_LON], "lon", -1)
-    return jnp.concatenate([block[:, HALF_LON:], rim], axis=1)
-
-
-def push_rims(block):
-    tail = shifted_2(block[-HALF_LAT:], "lat", 1)
-    moved = jnp.concatenate([tail, block[:-HALF_LAT]], axis=0)
-    tail = shifted_2(moved[:, -HALF_LON:], "lon", 1)
-    return jnp.concatenate([tail, moved[:, :-HALF_LON]], axis=1)
+        cost_estimate=cost(30 * 10**9, 10 * 2**20),
+    )(me, dmid, n1, qkv, p, att, x, g1, wqkv, wout, dg2, res)
+
+
+def keep_grads(me, n1, dqkv, att, dmid, dg1, dg2):
+    return pl.pallas_call(
+        keep_kernel,
+        name="keep",
+        in_specs=[SM] + [VM] * 6,
+        out_specs=VM,
+        out_shape=shape((CHIPS_N, SLOTS, 128)),
+        compiler_params=params(),
+        cost_estimate=cost(4 * 10**9, 4 * 2**20),
+    )(me, n1, dqkv, att, dmid, dg1, dg2)
+
+
+def unpack_mlp(me, mine, theirs):
+    return pl.pallas_call(
+        unpack_mlp_kernel,
+        name="unpack_mlp",
+        in_specs=[SM, VM, VM],
+        out_specs=[VM, VM],
+        out_shape=[shape((D, FF), F32), shape((FF, D), F32)],
+        compiler_params=params(),
+        cost_estimate=cost(10**9, 12 * 2**20),
+    )(me, mine, theirs)
+
+
+def unpack_att(me, mine, theirs):
+    return pl.pallas_call(
+        unpack_att_kernel,
+        name="unpack_att",
+        in_specs=[SM, VM, VM],
+        out_specs=[VM] * 3,
+        out_shape=[shape((D, 3 * D), F32), shape((D, D), F32), shape((16, D), F32)],
+        compiler_params=params(),
+        cost_estimate=cost(10**9, 6 * 2**20),
+    )(me, mine, theirs)
+
+
+LAT = ("x", "zl")
+LON = ("zh", "y", "c")
+CHIPS = ("x", "zl", "zh", "y")
+
+
+def send_rims(lon, lat, corner, distance):
+    lats, lons = lax.axis_size(LAT), lax.axis_size(LON)
+    moved = []
+    for block, down, across in ((lon, 0, distance), (lat, distance, 0), (corner, distance, distance)):
+        route = [
+            (i * lons + j, (i + down) % lats * lons + (j + across) % lons)
+            for i in range(lats) for j in range(lons)
+        ]
+        moved.append(lax.ppermute(block, LAT + LON, route))
+    return moved
+
+
+def other_core(block):
+    return lax.ppermute(block, "c", [(0, 1), (1, 0)])
+
+
+def exchange(parts):
+    return lax.all_to_all(parts, CHIPS, 0, 0, tiled=True)
+
+
+def add_cores(keep, got):
+    return (keep.astype(F32) + got.astype(F32)).astype(BF16)
+
+
+def shared(parts):
+    return pl.pallas_call(
+        share_kernel,
+        name="share",
+        in_specs=[VM],
+        out_specs=VM,
+        out_shape=shape(parts.shape),
+        compiler_params=params(),
+        cost_estimate=cost(10**9, 2 * parts.size * 2),
+    )(parts)
 
 
 def shards(tokens, cotangent, norm_gain, w_qkv, w_out, mlp_gain, w_up, w_down):
-    rows, cols, levels, _ = tokens.shape
     g1 = norm_gain.reshape(1, D)
     g2 = mlp_gain.reshape(1, D)
-    x = windows(pull_rims(tokens))
-    cot = windows(pull_rims(cotangent))
-    last_band = lax.axis_index("lat") == lax.axis_size("lat") - 1
+    last_band = lax.axis_index(LAT) == lax.axis_size(LAT) - 1
     flag = last_band.astype(jnp.int32).reshape(1)
-
-    n1, qkv, p, att, mid, n2 = front(flag, x, g1, w_qkv, w_out, g2)
-    res, dmid, dg2, gup, gdown = mlp(n2, cot, mid, g2, w_up, w_down)
-    dx, dg1, gqkv, gout = back(x, dmid, n1, qkv, p, att, g1, w_qkv, w_out)
-
-    output = push_rims(unwindows(res, rows, cols, levels))
-    grad_tokens = push_rims(unwindows(dx, rows, cols, levels))
-    sums = lax.psum((gup, gdown, gqkv, gout), ("lat", "lon"))
-    gains = lax.psum(jnp.concatenate([dg1, dg2]), ("lat", "lon"))
-    gup, gdown, gqkv, gout = (part.astype(F32) for part in sums)
-    return (output, grad_tokens, gains[0], gqkv, gout, gains[1], gup, gdown)
+    me = lax.axis_index("c").astype(jnp.int32).reshape(1)
+
+    rims = send_rims(*pack(tokens, cotangent), -1)
+    x, cot, n1, qkv, p, att, mid, n2 = front(flag, tokens, cotangent, *rims, g1, w_qkv, w_out, g2)
+    down, dn2, gup, gdown = mlp_send(me, n2, cot, w_up, w_down)
+    got = other_core(jnp.concatenate([gup, gdown]))
+    res, dmid, dg2, gup, gdown = mlp_keep(me, n2, cot, w_up, w_down, mid, g2, down, dn2)
+    mlp_part = add_cores(jnp.concatenate([gup, gdown]), got).reshape(CHIPS_N, -1, D)
+    mlp_part = exchange(mlp_part)
+    output, grad_tokens, lon, lat, corner, dqkv, dg1, send = back(
+        me, dmid, n1, qkv, p, att, x, g1, w_qkv, w_out, dg2, res, tokens.shape)
+    got = other_core(send)
+    rims = send_rims(lon, lat, corner, 1)
+    keep = keep_grads(me, n1, dqkv, att, dmid, dg1, dg2)
+    att_part = exchange(add_cores(keep, got))
+    output, grad_tokens = place(output, grad_tokens, *rims)
+    mlp_mine = exchange(shared(mlp_part)).reshape(-1, D)
+    att_part, output, grad_tokens = lax.optimization_barrier((att_part, output, grad_tokens))
+    att_mine = exchange(shared(att_part))
+    gup, gdown = unpack_mlp(me, mlp_mine, other_core(mlp_mine))
+    att_mine, gup, gdown = lax.optimization_barrier((att_mine, gup, gdown))
+    gqkv, gout, gains = unpack_att(me, att_mine, other_core(att_mine))
+    return (output, grad_tokens, gains[0], gqkv, gout, gains[8], gup, gdown)
 
 
 def solution(mesh):
-    field = P("lat", "lon", None, None)
+    field = P(LAT, LON, None, None)
+    mesh = jax.sharding.Mesh(mesh.devices.reshape(4, 2, 2, 4, 2), ("x", "zl", "zh", "y", "c"))
     return jax.shard_map(
         shards,
         mesh=mesh,

time: 295 us -> 302 us (1.024)
  Pallas kernels: 82.5 us -> 164 us
  waiting for transfers between devices: 74.3 us -> 41.1 us
  starting transfers between devices: 12.4 us -> 44.6 us
  blocking collectives: 69.8 us -> 39.6 us
  other arithmetic: 21.4 us -> 6.44 us
  local copies, waits for them, and re-layouts: 19.9 us -> 4.94 us
  between operations: 14.3 us -> 0.76 us
    pallas_call x3 -> x11, Pallas kernels: 82.5 us -> 164 us  [the longest x1 31.2 us: back(): pl.pallas_call(back_kernel, name='back', in_specs=[SM] + [VM] * 11, out_s...]
    psum x1 -> x0, waiting for transfers between devices: 71 us -> none  [shards(): sums = lax.psum((gup, gdown, gqkv, gout), ('lat', 'lon'))]
    psum x1 -> x0, blocking collectives: 69.8 us -> none  [shards(): gains = lax.psum(jnp.concatenate([dg1, dg2]), ('lat', 'lon'))]
    all_to_all x0 -> x1, blocking collectives: none -> 39.6 us  [exchange(): return lax.all_to_all(parts, CHIPS, 0, 0, tiled=True)]
    ppermute x8 -> x10, waiting for transfers between devices: 3.33 us -> 27.8 us  [the longest x6 25.3 us: send_rims(): moved.append(lax.ppermute(block, LAT + LON, route))]
    all_to_all x0 -> x3, starting transfers between devices: none -> 23.3 us  [exchange(): return lax.all_to_all(parts, CHIPS, 0, 0, tiled=True)]
    all_to_all x0 -> x3, waiting for transfers between devices: none -> 13.3 us  [exchange(): return lax.all_to_all(parts, CHIPS, 0, 0, tiled=True)]
    concatenate x9 -> x1, other arithmetic: 11.1 us -> 1.68 us  [shards(): got = other_core(jnp.concatenate([gup, gdown]))]
  transfers between devices with their start and end apart: 9 -> 13, of which waited for: 3 -> 4; matrix products, arithmetic and copies ran while one was open for 9% -> 1% of each run, Pallas kernels for 0% -> 30%
where the time goes in v2:
time: 302 us
  Pallas kernels  164 us (54%)
  starting transfers between devices  44.6 us (15%)
  waiting for transfers between devices  41.1 us (14%)
  blocking collectives  39.6 us (13%)
  other arithmetic  6.44 us (2%)
  local copies, waits for them, and re-layouts  4.94 us (2%)
    all_to_all x1, blocking collectives, exchange(): return lax.all_to_all(parts, CHIPS, 0, 0, tiled=True)  39.6 us
    pallas_call x1, Pallas kernels, back(): pl.pallas_call(back_kernel, name='back', in_specs=[SM] + [VM] * 11, out_s...  31.2 us
    pallas_call x1, Pallas kernels, pack(): pl.pallas_call(pack_kernel, name='pack', in_specs=[ANY] * 2, out_specs=[A...  25.7 us
    pallas_call x1, Pallas kernels, place(): pl.pallas_call(place_kernel, name='place', in_specs=[ANY] * 5, out_specs=...  25.7 us
    ppermute x6, waiting for transfers between devices, send_rims(): moved.append(lax.ppermute(block, LAT + LON, route))  25.3 us
    pallas_call x1, Pallas kernels, front(): pl.pallas_call(front_kernel, name='front', in_specs=[SM] + [ANY] * 5 + [V...  23.9 us
    all_to_all x3, starting transfers between devices, exchange(): return lax.all_to_all(parts, CHIPS, 0, 0, tiled=True)  23.3 us
    pallas_call x1, Pallas kernels, mlp_keep(): pl.pallas_call(mlp_keep_kernel, name='mlp_keep', grid_spec=pltpu.Prefetch...  20.2 us
  transfers between devices with their start and end apart: 13, of which 4 were waited for; matrix products, arithmetic and copies ran while one was open for 1% of the time, Pallas kernels for 30%

profile of v2, /device:TPU:1, one launch (start us, length us, event | category | flops | bytes accessed | tf_op | source)
XLA Modules:
  0.0 301.6 jit_solution(16660811080988215617)
XLA Ops:
  0.6 25.7 %pack.1 = (bf16[2,21,6,2,512]{4,3,2,1,0:T(2,128)(2,1)}, bf16[2,3,18,2,512]{4,3,2,1,0:T(2,128)(2,1)}, bf16[2,3,6,2,512]{4,3,2,1,0:T(2,128)(2,1)}) custom-call(bf16[24,24,2,512]{3,2,1,0:T(2,128)(2,1)} %tok_ref.3, bf16[24,24,2,512]{3,2,1,0:T(2,128)(2,1)} %cot_ref.3), custom_call_target="tpu_custom_call" | custom-call | tf_op jit(solution)/shard_map/pack/pallas_call | solution.py:440
  27.9 3.9 %collective-permute-start.1 = (bf16[2,3,18,2,512]{4,3,2,1,0:T(2,128)(2,1)}, bf16[2,3,18,2,512]{4,3,2,1,0:T(2,128)(2,1)S(1)}, u32[]{:S(2)}, u32[]{:S(2)}) collective-permute-start(bf16[2,3,18,2,512]{4,3,2,1,0:T(2,128)(2,1)} %get-tuple-element.50), channel_id=1, source_target_pairs={{0,112},{1,113},{2,114},{3,115},{4,116},{5,117},{6,118},{7,119},{8... | collective-permute-start | bytes 663560 | tf_op jit(solution)/shard_map/ppermute | solution.py:635
  31.8 5.8 %collective-permute-start.2 = (bf16[2,3,6,2,512]{4,3,2,1,0:T(2,128)(2,1)}, bf16[2,3,6,2,512]{4,3,2,1,0:T(2,128)(2,1)S(1)}, u32[]{:S(2)}, u32[]{:S(2)}) collective-permute-start(bf16[2,3,6,2,512]{4,3,2,1,0:T(2,128)(2,1)} %get-tuple-element.51), channel_id=1, source_target_pairs={{0,127},{1,112},{2,113},{3,114},{4,115},{5,116},{6,117},{7,118},{8... | collective-permute-start | bytes 221192 | tf_op jit(solution)/shard_map/ppermute | solution.py:635
  37.5 2.3 collective-permute-done.2.corner_ref
  40.7 23.9 %front.1 = (bf16[1152,512]{1,0:T(8,128)(2,1)}, bf16[1152,512]{1,0:T(8,128)(2,1)}, bf16[1152,512]{1,0:T(8,128)(2,1)}, bf16[1152,1536]{1,0:T(8,128)(2,1)}, bf16[8,...) custom-call(s32[1]{0:T(128)} %bitcast.1.flag_ref, ...), custom_call_target="tpu_custom_call" | custom-call | flops 20000000000 | bytes 10485760 | tf_op jit(solution)/shard_map/front/pallas_call | solution.py:469
  64.7 15.7 %mlp_send.1 = (f32[1152,512]{1,0:T(8,128)}, f32[1152,512]{1,0:T(8,128)}, bf16[1024,512]{1,0:T(8,128)(2,1)}, bf16[1024,512]{1,0:T(8,128)(2,1)}) custom-call(s32[1]{0:T(128)} %bitcast.me_ref, bf16[1152,512]{1,0:T(8,128)(2,1)} %get-tuple-element.53.n2_ref, bf16[1152,512]{1,0:T(8,128)(2,1)} %get-tuple-element.54.cot_ref, bf16[512,2048]{1,0:T(8,128)(2,1)} %wup_ref.3, ...), custom_call_target="tpu_custom_call" | custom-call | flops 16000000000 | bytes 10485760 | tf_op jit(solution)/shard_map/mlp_send/pallas_call | solution.py:515
  82.0 3.1 %collective-permute-start.7 = (bf16[2048,512]{1,0:T(8,128)(2,1)S(1)}, bf16[2048,512]{1,0:T(8,128)(2,1)S(1)}, u32[]{:S(2)}, u32[]{:S(2)}) collective-permute-start(bf16[2048,512]{1,0:T(8,128)(2,1)S(1)} %pad_maximum_fusion), channel_id=1, source_target_pairs={{0,1},{1,0},{2,3},{3,2},{4,5},{5,4},{6,7},{7,6},{8,9},{9,8},{10,11... | collective-permute-start | bytes 6291464 | tf_op jit(solution)/shard_map/ppermute | solution.py:640
  85.1 20.2 %mlp_keep.1 = (bf16[1152,512]{1,0:T(8,128)(2,1)}, bf16[1152,512]{1,0:T(8,128)(2,1)}, f32[1,512]{1,0:T(1,128)}, bf16[1024,512]{1,0:T(8,128)(2,1)}, bf16[1024,512]{1,0:T(8,128)(2,1)}) custom-call(s32[1]{0:T(128)} %bitcast.me_ref, bf16[1152,512]{1,0:T(8,128)(2,1)} %get-tuple-element.53.n2_ref, bf16[1152,512]{1,0:T(8,128)(2,1)} %get-tuple-element.54.cot_ref, ...), custom_call_target="tpu_custom_call" | custom-call | flops 16000000000 | bytes 10485760 | tf_op jit(solution)/shard_map/mlp_keep/pallas_call | solution.py:535
  105.3 2.1 add_convert_fusion
  107.5 39.6 %all_to_all.20.in_ref = bf16[64,32,512]{2,1,0:T(8,128)(2,1)} all-to-all(bf16[64,32,512]{2,1,0:T(8,128)(2,1)S(1)} %bitcast.8), channel_id=1, replica_groups=mesh['x'=4,'zl'=2,'zh'=2,'y'=4,'c'=2] {'x','zl','zh','y'}, dimensions={0} | all-to-all | bytes 4194304 | tf_op jit(solution)/shard_map/all_to_all | solution.py:644
  147.1 3.4 %share.3 = bf16[64,32,512]{2,1,0:T(8,128)(2,1)} custom-call(bf16[64,32,512]{2,1,0:T(8,128)(2,1)} %all_to_all.20.in_ref), custom_call_target="tpu_custom_call" | custom-call | flops 1000000000 | bytes 4194304 | tf_op jit(solution)/shard_map/share/pallas_call | solution.py:652
  150.4 6.0 %all-to-all-start.3 = ((bf16[64,32,512]{2,1,0:T(8,128)(2,1)}), bf16[64,32,512]{2,1,0:T(8,128)(2,1)S(1)}, u32[]{:S(2)}, u32[]{:S(2)}) async-start(bf16[64,32,512]{2,1,0:T(8,128)(2,1)} %share.3), calls=%async_computation.3 | async-start | bytes 4194304 | tf_op jit(solution)/shard_map/all_to_all | solution.py:644
  156.5 31.2 %back.1 = (bf16[24,24,2,512]{3,2,1,0:T(2,128)(2,1)}, bf16[24,24,2,512]{3,2,1,0:T(2,128)(2,1)}, bf16[2,21,6,2,512]{4,3,2,1,0:T(2,128)(2,1)}, bf16[2,3,18,2,512]{4...) custom-call(s32[1]{0:T(128)} %bitcast.me_ref, ...), custom_call_target="tpu_custom_call" | custom-call | flops 30000001024 | bytes 10485760 | tf_op jit(solution)/shard_map/back/pallas_call | solution.py:564
  189.3 5.6 %keep.1 = bf16[64,72,128]{2,1,0:T(8,128)(2,1)} custom-call(s32[1]{0:T(128)} %bitcast.me_ref, bf16[1152,512]{1,0:T(8,128)(2,1)} %get-tuple-element.52.n1_ref, bf16[1152,1536]{1,0:T(8,128)(2,1)} %get-tuple-element.65.dqkv_ref, bf16[1152,512]{1,0:T(8,128)(2,1)} %get-tuple-element.61.att_ref, bf16[1152,512]{1,0:T(8,128)(2,1)} %get-tuple-element.58.dmid_ref, ...), custom_call_target="tpu_custom_call" | custom-call | flops 4000000000 | bytes 4194304 | tf_op jit(solution)/shard_map/keep/pallas_call | solution.py:587
  194.9 2.6 add_convert_fusion.1
  197.5 10.0 %all-to-all-start = ((bf16[64,72,128]{2,1,0:T(8,128)(2,1)}), bf16[64,72,128]{2,1,0:T(8,128)(2,1)S(1)}, u32[]{:S(2)}, u32[]{:S(2)}) async-start(bf16[64,72,128]{2,1,0:T(8,128)(2,1)} %add_convert_fusion.1), calls=%async_computation | async-start | bytes 2359296 | tf_op jit(solution)/shard_map/all_to_all | solution.py:644
  212.0 23.0 %collective-permute-done.6.corner_ref = bf16[2,3,6,2,512]{4,3,2,1,0:T(2,128)(2,1)S(1)} collective-permute-done((bf16[2,3,6,2,512]{4,3,2,1,0:T(2,128)(2,1)}, bf16[2,3,6,2,512]{4,3,2,1,0:T(2,128)(2,1)S(1)}, u32[]{:S(2)}, u32[]{:S(2)}) %collective-permute-start.6) | collective-permute-done | bytes 73760 | tf_op jit(solution)/shard_map/ppermute | solution.py:635
  235.7 25.7 %place.1 = (bf16[24,24,2,512]{3,2,1,0:T(2,128)(2,1)}, bf16[24,24,2,512]{3,2,1,0:T(2,128)(2,1)}) custom-call(bf16[24,24,2,512]{3,2,1,0:T(2,128)(2,1)} %get-tuple-element.68.out_in, bf16[24,24,2,512]{3,2,1,0:T(2,128)(2,1)} %get-tuple-element.69.grad_in, ...), custom_call_target="tpu_custom_call", output_to_operand_aliasing={{0}: (0, {}), {1}: (1, {})} | custom-call | flops 1000000000 | bytes 2097152 | tf_op jit(solution)/shard_map/place/pallas_call | solution.py:451
  262.5 2.5 share.2
  265.0 7.2 %all-to-all-start.1 = ((bf16[64,72,128]{2,1,0:T(8,128)(2,1)}), bf16[64,72,128]{2,1,0:T(8,128)(2,1)S(1)}, u32[]{:S(2)}, u32[]{:S(2)}) async-start(bf16[64,72,128]{2,1,0:T(8,128)(2,1)} %share.2), calls=%async_computation.1 | async-start | bytes 2359296 | tf_op jit(solution)/shard_map/all_to_all | solution.py:644
  272.3 6.0 %unpack_mlp.1 = (f32[512,2048]{1,0:T(8,128)}, f32[2048,512]{1,0:T(8,128)}) custom-call(s32[1]{0:T(128)} %bitcast.me_ref, bf16[2048,512]{1,0:T(8,128)(2,1)} %bitcast.10, bf16[2048,512]{1,0:T(8,128)(2,1)} %collective-permute-done.8.theirs_ref), custom_call_target="tpu_custom_call" | custom-call | flops 1000000000 | bytes 12582912 | tf_op jit(solution)/shard_map/unpack_mlp/pallas_call | solution.py:599
  278.3 13.3 %all-to-all-done.1.mine_ref = bf16[64,72,128]{2,1,0:T(8,128)(2,1)S(1)} async-done(((bf16[64,72,128]{2,1,0:T(8,128)(2,1)}), bf16[64,72,128]{2,1,0:T(8,128)(2,1)S(1)}, u32[]{:S(2)}, u32[]{:S(2)}) %all-to-all-start.1) | async-done | bytes 1179680 | tf_op jit(solution)/shard_map/all_to_all | solution.py:644
  292.6 2.5 collective-permute-done.9.theirs_ref
  296.1 4.1 %unpack_att.1 = (f32[512,1536]{1,0:T(8,128)}, f32[512,512]{1,0:T(8,128)}, f32[16,512]{1,0:T(8,128)}) custom-call(s32[1]{0:T(128)} %bitcast.me_ref, bf16[64,72,128]{2,1,0:T(8,128)(2,1)} %copy-done.2, bf16[64,72,128]{2,1,0:T(8,128)(2,1)} %copy-done.3), custom_call_target="tpu_custom_call" | custom-call | flops 1000000000 | bytes 6291456 | tf_op jit(solution)/shard_map/unpack_att/pallas_call | solution.py:611
  (38 shorter events, 15.1 us)
Async XLA Ops:
  26.4 13.5 %collective-permute-start = (bf16[2,21,6,2,512]{4,3,2,1,0:T(2,128)(2,1)}, bf16[2,21,6,2,512]{4,3,2,1,0:T(2,128)(2,1)S(1)}, u32[]{:S(2)}, u32[]{:S(2)}) collective-permute-start(bf16[2,21,6,2,512]{4,3,2,1,0:T(2,128)(2,1)} %get-tuple-element.49), channel_id=1, source_target_pairs={{0,15},{1,0},{2,1},{3,2},{4,3},{5,4},{6,5},{7,6},{8,7},{9,8},{10,9... | collective-permute-start | bytes 1548296 | tf_op jit(solution)/shard_map/ppermute | solution.py:635
  27.9 12.0 %collective-permute-start.1 = (bf16[2,3,18,2,512]{4,3,2,1,0:T(2,128)(2,1)}, bf16[2,3,18,2,512]{4,3,2,1,0:T(2,128)(2,1)S(1)}, u32[]{:S(2)}, u32[]{:S(2)}) collective-permute-start(bf16[2,3,18,2,512]{4,3,2,1,0:T(2,128)(2,1)} %get-tuple-element.50), channel_id=1, source_target_pairs={{0,112},{1,113},{2,114},{3,115},{4,116},{5,117},{6,118},{7,119},{8... | collective-permute-start | bytes 663560 | tf_op jit(solution)/shard_map/ppermute | solution.py:635
  31.8 8.1 %collective-permute-start.2 = (bf16[2,3,6,2,512]{4,3,2,1,0:T(2,128)(2,1)}, bf16[2,3,6,2,512]{4,3,2,1,0:T(2,128)(2,1)S(1)}, u32[]{:S(2)}, u32[]{:S(2)}) collective-permute-start(bf16[2,3,6,2,512]{4,3,2,1,0:T(2,128)(2,1)} %get-tuple-element.51), channel_id=1, source_target_pairs={{0,127},{1,112},{2,113},{3,114},{4,115},{5,116},{6,117},{7,118},{8... | collective-permute-start | bytes 221192 | tf_op jit(solution)/shard_map/ppermute | solution.py:635
  39.9 0.6 copy-start.8
  39.9 0.7 copy-start.5
  39.9 0.9 copy-start.4
  82.0 23.3 %collective-permute-start.7 = (bf16[2048,512]{1,0:T(8,128)(2,1)S(1)}, bf16[2048,512]{1,0:T(8,128)(2,1)S(1)}, u32[]{:S(2)}, u32[]{:S(2)}) collective-permute-start(bf16[2048,512]{1,0:T(8,128)(2,1)S(1)} %pad_maximum_fusion), channel_id=1, source_target_pairs={{0,1},{1,0},{2,3},{3,2},{4,5},{5,4},{6,7},{7,6},{8,9},{9,8},{10,11... | collective-permute-start | bytes 6291464 | tf_op jit(solution)/shard_map/ppermute | solution.py:640
  150.4 47.1 %all-to-all-start.3 = ((bf16[64,32,512]{2,1,0:T(8,128)(2,1)}), bf16[64,32,512]{2,1,0:T(8,128)(2,1)S(1)}, u32[]{:S(2)}, u32[]{:S(2)}) async-start(bf16[64,32,512]{2,1,0:T(8,128)(2,1)} %share.3), calls=%async_computation.3 | async-start | bytes 4194304 | tf_op jit(solution)/shard_map/all_to_all | solution.py:644
  187.7 7.2 %collective-permute-start.3 = (bf16[64,72,128]{2,1,0:T(8,128)(2,1)}, bf16[64,72,128]{2,1,0:T(8,128)(2,1)S(1)}, u32[]{:S(2)}, u32[]{:S(2)}) collective-permute-start(bf16[64,72,128]{2,1,0:T(8,128)(2,1)} %get-tuple-element.67), channel_id=1, source_target_pairs={{0,1},{1,0},{2,3},{3,2},{4,5},{5,4},{6,7},{7,6},{8,9},{9,8},{10,11... | collective-permute-start | bytes 3538952 | tf_op jit(solution)/shard_map/ppermute | solution.py:640
  194.9 14.3 %copy-start.6 = (bf16[2,3,18,2,512]{4,3,2,1,0:T(2,128)(2,1)S(1)}, bf16[2,3,18,2,512]{4,3,2,1,0:T(2,128)(2,1)}, u32[]{:S(2)}) copy-start(bf16[2,3,18,2,512]{4,3,2,1,0:T(2,128)(2,1)} %get-tuple-element.71) | copy-start | bytes 663556
  197.5 63.9 %copy-start = (bf16[64,32,512]{2,1,0:T(8,128)(2,1)}, bf16[64,32,512]{2,1,0:T(8,128)(2,1)S(1)}, u32[]{:S(2)}) copy-start(bf16[64,32,512]{2,1,0:T(8,128)(2,1)S(1)} %all-to-all-done.3) | copy-start | bytes 6291460
  197.5 63.9 %all-to-all-start = ((bf16[64,72,128]{2,1,0:T(8,128)(2,1)}), bf16[64,72,128]{2,1,0:T(8,128)(2,1)S(1)}, u32[]{:S(2)}, u32[]{:S(2)}) async-start(bf16[64,72,128]{2,1,0:T(8,128)(2,1)} %add_convert_fusion.1), calls=%async_computation | async-start | bytes 2359296 | tf_op jit(solution)/shard_map/all_to_all | solution.py:644
  207.6 64.7 %collective-permute-start.8 = (bf16[2048,512]{1,0:T(8,128)(2,1)S(1)}, bf16[2048,512]{1,0:T(8,128)(2,1)}, u32[]{:S(2)}, u32[]{:S(2)}) collective-permute-start(bf16[2048,512]{1,0:T(8,128)(2,1)S(1)} %bitcast.9), channel_id=1, source_target_pairs={{0,1},{1,0},{2,3},{3,2},{4,5},{5,4},{6,7},{7,6},{8,9},{9,8},{10,11... | collective-permute-start | bytes 6291464 | tf_op jit(solution)/shard_map/ppermute | solution.py:640
  208.0 27.8 %collective-permute-start.4 = (bf16[2,21,6,2,512]{4,3,2,1,0:T(2,128)(2,1)}, bf16[2,21,6,2,512]{4,3,2,1,0:T(2,128)(2,1)}, u32[]{:S(2)}, u32[]{:S(2)}) collective-permute-start(bf16[2,21,6,2,512]{4,3,2,1,0:T(2,128)(2,1)} %get-tuple-element.70), channel_id=1, source_target_pairs={{0,1},{1,2},{2,3},{3,4},{4,5},{5,6},{6,7},{7,8},{8,9},{9,10},{10,1... | collective-permute-start | bytes 1548296 | tf_op jit(solution)/shard_map/ppermute | solution.py:635
  209.2 25.8 %collective-permute-start.5 = (bf16[2,3,18,2,512]{4,3,2,1,0:T(2,128)(2,1)S(1)}, bf16[2,3,18,2,512]{4,3,2,1,0:T(2,128)(2,1)S(1)}, u32[]{:S(2)}, u32[]{:S(2)}) collective-permute-start(bf16[2,3,18,2,512]{4,3,2,1,0:T(2,128)(2,1)S(1)} %copy-done.6), channel_id=1, source_target_pairs={{0,16},{1,17},{2,18},{3,19},{4,20},{5,21},{6,22},{7,23},{8,24},{9,... | collective-permute-start | bytes 663560 | tf_op jit(solution)/shard_map/ppermute | solution.py:635
  210.4 24.6 %collective-permute-start.6 = (bf16[2,3,6,2,512]{4,3,2,1,0:T(2,128)(2,1)}, bf16[2,3,6,2,512]{4,3,2,1,0:T(2,128)(2,1)S(1)}, u32[]{:S(2)}, u32[]{:S(2)}) collective-permute-start(bf16[2,3,6,2,512]{4,3,2,1,0:T(2,128)(2,1)} %get-tuple-element.72), channel_id=1, source_target_pairs={{0,17},{1,18},{2,19},{3,20},{4,21},{5,22},{6,23},{7,24},{8,25},{9,... | collective-permute-start | bytes 221192 | tf_op jit(solution)/shard_map/ppermute | solution.py:635
  235.0 0.7 copy-start.9
  235.0 0.7 copy-start.7
  261.5 1.0 copy-start.1
  265.0 26.6 %all-to-all-start.1 = ((bf16[64,72,128]{2,1,0:T(8,128)(2,1)}), bf16[64,72,128]{2,1,0:T(8,128)(2,1)S(1)}, u32[]{:S(2)}, u32[]{:S(2)}) async-start(bf16[64,72,128]{2,1,0:T(8,128)(2,1)} %share.2), calls=%async_computation.1 | async-start | bytes 2359296 | tf_op jit(solution)/shard_map/all_to_all | solution.py:644
  291.6 3.5 %copy-start.2 = (bf16[64,72,128]{2,1,0:T(8,128)(2,1)}, bf16[64,72,128]{2,1,0:T(8,128)(2,1)S(1)}, u32[]{:S(2)}) copy-start(bf16[64,72,128]{2,1,0:T(8,128)(2,1)S(1)} %all-to-all-done.1.mine_ref) | copy-start | bytes 3538948
  291.6 3.5 %collective-permute-start.9 = (bf16[64,72,128]{2,1,0:T(8,128)(2,1)S(1)}, bf16[64,72,128]{2,1,0:T(8,128)(2,1)S(1)}, u32[]{:S(2)}, u32[]{:S(2)}) collective-permute-start(bf16[64,72,128]{2,1,0:T(8,128)(2,1)S(1)} %all-to-all-done.1.mine_ref), channel_id=1, source_target_pairs={{0,1},{1,0},{2,3},{3,2},{4,5},{5,4},{6,7},{7,6},{8,9},{9,8},{10,11... | collective-permute-start | bytes 3538952 | tf_op jit(solution)/shard_map/ppermute | solution.py:640
  295.1 1.0 copy-start.3

commit v3 on v2

--- a/solution.py
+++ b/solution.py
@@ -20,7 +20,6 @@
 F32 = jnp.float32
 BF16 = jnp.bfloat16
 PAIR = 2 * HD
-LIMIT = 56 * 1024 * 1024
 
 
 def mm(a, b):
@@ -89,6 +88,7 @@
                     )
 
 
+SAVES = 6
 STRIPS = len(list(strips()))
 
 
@@ -110,11 +110,22 @@
     return copies
 
 
-def front_kernel(flag_ref, tok_ref, cot_ref, lon_ref, lat_ref, corner_ref, g1_ref, wqkv_ref, wout_ref, g2_ref,
-                 x_ref, cotw_ref, n1_ref, qkv_ref, p_ref, att_ref, mid_ref, n2_ref, tok_buf, cot_buf, sems):
+def front_kernel(flag_ref, tok_ref, cot_ref, lon_ref, lat_ref, corner_ref, g1_ref, wqkv_hbm, wout_hbm, g2_ref,
+                 x_out, n1_out, qkv_out, p_out, att_out, mid_out, cot_out, cotw_ref, n2_ref,
+                 tok_buf, cot_buf, x_ref, n1_ref, qkv_ref, p_ref, att_ref, mid_ref, wqkv_ref, wout_ref,
+                 sems, out_sems, w_sems):
+    wqkv_copy = pltpu.make_async_copy(wqkv_hbm, wqkv_ref, w_sems.at[0])
+    wout_copy = pltpu.make_async_copy(wout_hbm, wout_ref, w_sems.at[1])
+    saves = []
+
+    def save(source, target):
+        copy = pltpu.make_async_copy(source, target, out_sems.at[len(saves)])
+        copy.start()
+        saves.append(copy)
+
     tok_copies = gather_windows(0, tok_ref, lon_ref, lat_ref, corner_ref, tok_buf, sems.at[0])
     cot_copies = gather_windows(1, cot_ref, lon_ref, lat_ref, corner_ref, cot_buf, sems.at[1])
-    for copy in tok_copies + cot_copies:
+    for copy in tok_copies + [wqkv_copy, wout_copy] + cot_copies:
         copy.start()
     for copy in tok_copies:
         copy.wait()
@@ -122,6 +133,7 @@
         for side in range(SIDES):
             w = band * SIDES + side
             x_ref[w * WIN:(w + 1) * WIN, :] = tok_buf[band, side].reshape(WIN, D)
+    save(x_ref, x_out)
     tokens = x_ref.shape[0]
     count = tokens // WIN
     per_row = count // 4
@@ -134,7 +146,9 @@
         xhat, _ = normalised(x_ref[rows, :].astype(F32))
         n1_ref[rows, :] = (xhat * gain1).astype(BF16)
 
-    big = 2 * WIN
+    wqkv_copy.wait()
+
+    big = ROWS
 
     @pl.loop(0, tokens // big)
     def _(b):
@@ -143,6 +157,9 @@
         qkv_ref[rows, 0:D] = (mm(n1, wqkv_ref[:, 0:D]).astype(BF16) * 0.125).astype(BF16)
         qkv_ref[rows, D:2 * D] = mm(n1, wqkv_ref[:, D:2 * D]).astype(BF16)
         qkv_ref[rows, 2 * D:3 * D] = mm(n1, wqkv_ref[:, 2 * D:3 * D]).astype(BF16)
+
+    save(n1_ref, n1_out)
+    save(qkv_ref, qkv_out)
 
     key_group = lax.broadcasted_iota(jnp.int32, (WIN, WIN), 0) >= WIN // 2
     query_group = lax.broadcasted_iota(jnp.int32, (WIN, WIN), 1) >= WIN // 2
@@ -170,6 +187,10 @@
                 p_ref[w, 2 * pair + h] = p
                 outs.append(t_mm(p, v))
             att_ref[rows, lanes] = jnp.where(low, outs[0], outs[1]).astype(BF16)
+        pltpu.make_async_copy(p_ref.at[w], p_out.at[w], out_sems.at[SAVES + w]).start()
+
+    save(att_ref, att_out)
+    wout_copy.wait()
 
     @pl.loop(0, tokens // big)
     def _(b):
@@ -179,76 +200,83 @@
         xhat, _ = normalised(mid.astype(F32))
         n2_ref[rows, :] = (xhat * gain2).astype(BF16)
 
+    save(mid_ref, mid_out)
     for copy in cot_copies:
         copy.wait()
     for band in range(BANDS):
         for side in range(SIDES):
             w = band * SIDES + side
             cotw_ref[w * WIN:(w + 1) * WIN, :] = cot_buf[band, side].reshape(WIN, D)
-
-
-def mlp_chunk(n2_ref, cot_ref, wup_ref, wdown_ref, gup_ref, gdown_ref, down_acc, dn2_acc, hid_ref, du_ref):
-    tokens = n2_ref.shape[0]
-    big = 2 * WIN
-
-    @pl.loop(0, tokens // big)
+    save(cotw_ref, cot_out)
+    for copy in saves:
+        copy.wait()
+    for w in range(count):
+        pltpu.make_async_copy(p_ref.at[w], p_out.at[w], out_sems.at[SAVES + w]).wait()
+
+
+CHUNK = 512
+ROWS = 4 * WIN
+
+
+def mlp_chunk(chunk, n2_ref, cot_ref, wup_ref, wdown_ref, down_in, dn2_in, down_out, dn2_out, hid_ref, du_ref):
+    at = pl.ds(pl.multiple_of(chunk * CHUNK, CHUNK), CHUNK)
+
+    @pl.loop(0, n2_ref.shape[0] // ROWS)
     def _(b):
-        rows = pl.ds(pl.multiple_of(b * big, big), big)
-        up = mm(n2_ref[rows, :], wup_ref[...])
+        rows = pl.ds(pl.multiple_of(b * ROWS, ROWS), ROWS)
+        up = mm(n2_ref[rows, :], wup_ref[:, at])
         cdf, pdf = gelu_parts(up)
         hid = (up * cdf).astype(BF16)
         hid_ref[rows, :] = hid
-        dhid = mm_t(cot_ref[rows, :], wdown_ref[...]).astype(BF16).astype(F32)
+        dhid = mm_t(cot_ref[rows, :], wdown_ref[at, :]).astype(BF16).astype(F32)
         du = (dhid * (cdf + up * pdf)).astype(BF16)
         du_ref[rows, :] = du
-        down_acc[rows, :] += mm(hid, wdown_ref[...])
-        dn2_acc[rows, :] += mm_t(du, wup_ref[...])
-
-    gdown_ref[...] = t_mm(hid_ref[...], cot_ref[...]).astype(BF16)
-    gup_ref[...] = t_mm(n2_ref[...], du_ref[...]).astype(BF16)
-
-
-def mlp_send_kernel(me_ref, n2_ref, cot_ref, wup_ref, wdown_ref,
-                    down_acc, dn2_acc, gup_ref, gdown_ref, hid_ref, du_ref):
-    del me_ref
-
-    @pl.when(pl.program_id(0) == 0)
-    def _():
-        down_acc[...] = jnp.zeros_like(down_acc)
-        dn2_acc[...] = jnp.zeros_like(dn2_acc)
-
-    mlp_chunk(n2_ref, cot_ref, wup_ref, wdown_ref, gup_ref, gdown_ref, down_acc, dn2_acc, hid_ref, du_ref)
-
-
-def mlp_keep_kernel(me_ref, n2_ref, cot_ref, wup_ref, wdown_ref, mid_ref, g2_ref, down_in, dn2_in,
-                    res_ref, dmid_ref, dg2_ref, gup_ref, gdown_ref,
-                    down_acc, dn2_acc, hid_ref, du_ref):
-    del me_ref
-    tokens = n2_ref.shape[0]
-    big = 2 * WIN
-
-    @pl.when(pl.program_id(0) == 0)
-    def _():
-        down_acc[...] = down_in[...]
-        dn2_acc[...] = dn2_in[...]
-
-    mlp_chunk(n2_ref, cot_ref, wup_ref, wdown_ref, gup_ref, gdown_ref, down_acc, dn2_acc, hid_ref, du_ref)
-
-    @pl.when(pl.program_id(0) == pl.num_programs(0) - 1)
-    def _():
-        gain2 = g2_ref[...]
-        dg2_ref[...] = jnp.zeros_like(dg2_ref)
-
-        @pl.loop(0, tokens // big)
-        def _(b):
-            rows = pl.ds(pl.multiple_of(b * big, big), big)
-            mid = mid_ref[rows, :].astype(F32)
-            res_ref[rows, :] = (mid + down_acc[rows, :]).astype(BF16)
-            xhat, scale = normalised(mid)
-            dn2 = dn2_acc[rows, :].astype(BF16).astype(F32)
-            dg2_ref[...] += jnp.sum(dn2 * xhat, axis=0, keepdims=True)
-            dmid = cot_ref[rows, :].astype(F32) + norm_pullback(xhat, scale, gain2, dn2)
-            dmid_ref[rows, :] = dmid.astype(BF16)
+        down = mm(hid, wdown_ref[at, :])
+        dn2 = mm_t(du, wup_ref[:, at])
+        if down_in is None:
+            down_out[rows, :] = down
+            dn2_out[rows, :] = dn2
+        else:
+            down_out[rows, :] = down_in[rows, :] + down
+            dn2_out[rows, :] = dn2_in[rows, :] + dn2
+
+    return t_mm(n2_ref[...], du_ref[...]).astype(BF16), t_mm(hid_ref[...], cot_ref[...]).astype(BF16)
+
+
+def send_kernel(me_ref, n2_ref, cot_ref, wup_ref, wdown_ref, down_ref, dn2_ref, grads_ref, hid_ref, du_ref):
+    for i in range(2):
+        carried = (down_ref, dn2_ref) if i else (None, None)
+        grads = mlp_chunk((1 - me_ref[0]) * 2 + i, n2_ref, cot_ref, wup_ref, wdown_ref,
+                          *carried, down_ref, dn2_ref, hid_ref, du_ref)
+        for part, grad in enumerate(grads):
+            grads_ref[(2 * part + i) * CHUNK:(2 * part + i + 1) * CHUNK, :] = grad
+
+
+def keep_first_kernel(me_ref, n2_ref, cot_ref, wup_ref, wdown_ref, down_in, dn2_in,
+                      down_ref, dn2_ref, early_ref, hid_ref, du_ref):
+    grads = mlp_chunk(me_ref[0] * 2, n2_ref, cot_ref, wup_ref, wdown_ref,
+                      down_in, dn2_in, down_ref, dn2_ref, hid_ref, du_ref)
+    for part, grad in enumerate(grads):
+        early_ref[part * CHUNK:(part + 1) * CHUNK, :] = grad
+
+
+def keep_second_kernel(me_ref, n2_ref, cot_ref, wup_ref, wdown_ref, down_in, dn2_in, early_ref, got_ref,
+                       down_hbm, dn2_hbm, grads_ref, hid_ref, du_ref, down_ref, dn2_ref, sems):
+    grads = mlp_chunk(me_ref[0] * 2 + 1, n2_ref, cot_ref, wup_ref, wdown_ref,
+                      down_in, dn2_in, down_ref, dn2_ref, hid_ref, du_ref)
+    copies = [
+        pltpu.make_async_copy(down_ref, down_hbm, sems.at[0]),
+        pltpu.make_async_copy(dn2_ref, dn2_hbm, sems.at[1]),
+    ]
+    for copy in copies:
+        copy.start()
+    for part, grad in enumerate(grads):
+        for i in range(2):
+            rows = slice((2 * part + i) * CHUNK, (2 * part + i + 1) * CHUNK)
+            mine = grad if i else early_ref[part * CHUNK:(part + 1) * CHUNK, :]
+            grads_ref[rows, :] = (mine.astype(F32) + got_ref[rows, :].astype(F32)).astype(BF16)
+    for copy in copies:
+        copy.wait()
 
 
 HALF = D // 2
@@ -277,29 +305,10 @@
         out_ref[block, 2 * per:, :] = row.astype(BF16)
 
 
-def back_kernel(me_ref, dmid_ref, n1_ref, qkv_ref, p_ref, att_ref, x_ref, g1_ref, wqkv_ref, wout_ref, dg2_ref, res_ref,
-                out_ref, grad_ref, lon_ref, lat_ref, corner_ref, dqkv_ref, dg1_ref, send_ref,
-                datt_ref, dx_ref, res_buf, dx_buf, sems):
-    for band in range(BANDS):
-        for side in range(SIDES):
-            w = band * SIDES + side
-            res_buf[band, side] = res_ref[w * WIN:(w + 1) * WIN, :].reshape(WLAT, WLON, LEV, D)
-    res_copies = scatter_windows(0, res_buf, out_ref, lon_ref, lat_ref, corner_ref, sems.at[0])
-    for copy in res_copies:
-        copy.start()
-    tokens = dmid_ref.shape[0]
-    count = tokens // WIN
-    gain1 = g1_ref[...]
-    big = 2 * WIN
-
-    @pl.loop(0, tokens // big)
-    def _(b):
-        rows = pl.ds(pl.multiple_of(b * big, big), big)
-        datt_ref[rows, :] = mm_t(dmid_ref[rows, :], wout_ref[...]).astype(BF16)
-
+def att_back(first, last, datt_ref, qkv_ref, p_ref, dqkv_ref):
     low = lax.broadcasted_iota(jnp.int32, (WIN, PAIR), 1) < HD
 
-    @pl.loop(0, count)
+    @pl.loop(first, last)
     def _(w):
         rows = pl.ds(pl.multiple_of(w * WIN, WIN), WIN)
         for pair in range(D // PAIR):
@@ -323,11 +332,66 @@
             dqkv_ref[rows, D + pair * PAIR:D + (pair + 1) * PAIR] = jnp.where(low, dks[0], dks[1]).astype(BF16)
             dqkv_ref[rows, 2 * D + pair * PAIR:2 * D + (pair + 1) * PAIR] = jnp.where(low, dvs[0], dvs[1]).astype(BF16)
 
+
+def back_kernel(me_ref, cot_hbm, mid_hbm, down_hbm, dn2_hbm, wout_hbm, qkv_hbm, p_hbm, wqkv_hbm, x_hbm, att_hbm, n1_hbm,
+                g1_ref, g2_ref,
+                out_ref, grad_ref, lon_ref, lat_ref, corner_ref,
+                att_ref, n1_ref, dmid_ref, dqkv_ref, dg1_ref, dg2_ref, send_ref,
+                cot_ref, mid_ref, down_ref, dn2_ref, wout_ref, qkv_ref, p_ref, wqkv_ref, x_ref,
+                datt_ref, dx_ref, res_ref, res_buf, dx_buf, in_sems, sems):
+    loads = {}
+    for i, (name, source, target) in enumerate((
+        ("cot", cot_hbm, cot_ref), ("mid", mid_hbm, mid_ref), ("down", down_hbm, down_ref), ("dn2", dn2_hbm, dn2_ref),
+        ("wout", wout_hbm, wout_ref), ("qkv", qkv_hbm, qkv_ref), ("p", p_hbm, p_ref), ("wqkv", wqkv_hbm, wqkv_ref),
+        ("x", x_hbm, x_ref), ("att", att_hbm, att_ref), ("n1", n1_hbm, n1_ref),
+    )):
+        loads[name] = pltpu.make_async_copy(source, target, in_sems.at[i])
+        loads[name].start()
+
+    gain1 = g1_ref[...]
+    gain2 = g2_ref[...]
+    dg2_ref[...] = jnp.zeros_like(dg2_ref)
+    tokens = cot_ref.shape[0]
+    for name in ("cot", "mid", "down", "dn2"):
+        loads[name].wait()
+
+    @pl.loop(0, tokens // WIN)
+    def _(b):
+        rows = pl.ds(pl.multiple_of(b * WIN, WIN), WIN)
+        mid = mid_ref[rows, :].astype(F32)
+        res_ref[rows, :] = (mid + down_ref[rows, :]).astype(BF16)
+        xhat, scale = normalised(mid)
+        dn2 = dn2_ref[rows, :].astype(BF16).astype(F32)
+        dg2_ref[...] += jnp.sum(dn2 * xhat, axis=0, keepdims=True)
+        dmid = cot_ref[rows, :].astype(F32) + norm_pullback(xhat, scale, gain2, dn2)
+        dmid_ref[rows, :] = dmid.astype(BF16)
+
+    for band in range(BANDS):
+        for side in range(SIDES):
+            w = band * SIDES + side
+            res_buf[band, side] = res_ref[w * WIN:(w + 1) * WIN, :].reshape(WLAT, WLON, LEV, D)
+    res_copies = scatter_windows(0, res_buf, out_ref, lon_ref, lat_ref, corner_ref, sems.at[0])
+    for copy in res_copies:
+        copy.start()
+
+    loads["wout"].wait()
+
+    @pl.loop(0, tokens // ROWS)
+    def _(b):
+        rows = pl.ds(pl.multiple_of(b * ROWS, ROWS), ROWS)
+        datt_ref[rows, :] = mm_t(dmid_ref[rows, :], wout_ref[...]).astype(BF16)
+
+    loads["qkv"].wait()
+    loads["p"].wait()
+    att_back(0, tokens // WIN, datt_ref, qkv_ref, p_ref, dqkv_ref)
+
     dg1_ref[...] = jnp.zeros_like(dg1_ref)
-
-    @pl.loop(0, tokens // big)
+    loads["wqkv"].wait()
+    loads["x"].wait()
+
+    @pl.loop(0, tokens // ROWS)
     def _(b):
-        rows = pl.ds(pl.multiple_of(b * big, big), big)
+        rows = pl.ds(pl.multiple_of(b * ROWS, ROWS), ROWS)
         dn1 = mm_t(dqkv_ref[rows, :], wqkv_ref[...]).astype(BF16).astype(F32)
         xhat, scale = normalised(x_ref[rows, :].astype(F32))
         dg1_ref[...] += jnp.sum(dn1 * xhat, axis=0, keepdims=True)
@@ -341,6 +405,8 @@
     dx_copies = scatter_windows(1, dx_buf, grad_ref, lon_ref, lat_ref, corner_ref, sems.at[1])
     for copy in dx_copies:
         copy.start()
+    loads["att"].wait()
+    loads["n1"].wait()
     att_grads(1 - me_ref[0], n1_ref, dqkv_ref, att_ref, dmid_ref, dg1_ref[...], dg2_ref[...], send_ref)
     for copy in res_copies + dx_copies:
         copy.wait()
@@ -350,13 +416,41 @@
     att_grads(me_ref[0], n1_ref, dqkv_ref, att_ref, dmid_ref, dg1_ref[...], dg2_ref[...], keep_ref)
 
 
-def share_kernel(in_ref, out_ref):
-    total = in_ref[0].astype(F32)
-    for chip in range(1, in_ref.shape[0]):
-        total += in_ref[chip].astype(F32)
-    total = total.astype(BF16)
-    for chip in range(in_ref.shape[0]):
+def total_of(parts_ref, rows):
+    total = parts_ref[0, rows, :].astype(F32)
+    for chip in range(1, CHIPS_N):
+        total += parts_ref[chip, rows, :].astype(F32)
+    return total.astype(BF16)
+
+
+SHARE = FF // CHIPS_N
+MIXED = SLOTS + SHARE * D // 128
+
+
+def lane_blocks():
+    return [(slice(SLOTS + i * SHARE, SLOTS + (i + 1) * SHARE), slice(i * 128, (i + 1) * 128)) for i in range(D // 128)]
+
+
+def merge_kernel(parts_ref, keep_ref, got_ref, out_ref):
+    total = total_of(parts_ref, slice(0, SHARE))
+    for chip in range(CHIPS_N):
+        both = keep_ref[chip].astype(F32) + got_ref[chip].astype(F32)
+        out_ref[chip, 0:SLOTS, :] = both.astype(BF16)
+        for rows, lanes in lane_blocks():
+            out_ref[chip, rows, :] = total[:, lanes]
+
+
+def share_kernel(parts_ref, out_ref):
+    total = total_of(parts_ref, slice(0, SLOTS))
+    for chip in range(CHIPS_N):
         out_ref[chip] = total
+
+
+def compact_kernel(parts_ref, after_ref, done_ref):
+    del after_ref
+    for chip in range(CHIPS_N):
+        for rows, lanes in lane_blocks():
+            done_ref[chip * SHARE:(chip + 1) * SHARE, lanes] = parts_ref[chip, rows, :]
 
 
 def unpack_mlp_kernel(me_ref, mine_ref, theirs_ref, gup_ref, gdown_ref):
@@ -409,8 +503,8 @@
         copy.wait()
 
 
-def params():
-    return pltpu.CompilerParams(vmem_limit_bytes=LIMIT)
+def params(mib=32):
+    return pltpu.CompilerParams(vmem_limit_bytes=mib * 2**20)
 
 
 def cost(flops, moved):
@@ -426,6 +520,7 @@
 
 
 ANY = pl.BlockSpec(memory_space=pl.ANY)
+HB = pl.BlockSpec(memory_space=pltpu.HBM)
 
 
 def rim_shapes(rows, cols, levels):
@@ -441,7 +536,7 @@
         pack_kernel,
         name="pack",
         in_specs=[ANY] * 2,
-        out_specs=[ANY] * 3,
+        out_specs=[VM] * 3,
         out_shape=rim_shapes(*tokens.shape[:3]),
         scratch_shapes=[pltpu.SemaphoreType.DMA((2, 3))],
     )(tokens, cotangent)
@@ -451,7 +546,7 @@
     return pl.pallas_call(
         place_kernel,
         name="place",
-        in_specs=[ANY] * 5,
+        in_specs=[ANY] * 2 + [VM] * 3,
         out_specs=[ANY] * 2,
         out_shape=[shape(output.shape), shape(grad.shape)],
         input_output_aliases={0: 0, 1: 1},
@@ -463,124 +558,108 @@
 WINDOWED = (BANDS, SIDES, WLAT, WLON, LEV, D)
 
 
+def local(dims, dtype=BF16):
+    return pltpu.VMEM(dims, dtype)
+
+
+def held(*arrays):
+    return [pltpu.with_memory_space_constraint(array, pltpu.VMEM) for array in arrays]
+
+
+def far(*arrays):
+    return [pltpu.with_memory_space_constraint(array, pltpu.HBM) for array in arrays]
+
+
 def front(flag, tok, cot, lon, lat, corner, g1, wqkv, wout, g2):
     tokens = tok.size // D
     count = tokens // WIN
+    saved = [(tokens, D), (tokens, D), (tokens, 3 * D), (count, D // HD, WIN, WIN), (tokens, D), (tokens, D)]
     return pl.pallas_call(
         front_kernel,
         name="front",
-        in_specs=[SM] + [ANY] * 5 + [VM] * 4,
-        out_specs=[VM] * 8,
-        out_shape=[
-            shape((tokens, D)),
-            shape((tokens, D)),
-            shape((tokens, D)),
-            shape((tokens, 3 * D)),
-            shape((count, D // HD, WIN, WIN)),
-            shape((tokens, D)),
-            shape((tokens, D)),
-            shape((tokens, D)),
-        ],
+        in_specs=[SM] + [ANY] * 5 + [VM, HB, HB, VM],
+        out_specs=[HB] * 7 + [VM] * 2,
+        out_shape=[pltpu.HBM(dims, BF16) for dims in saved + [(tokens, D)]] + [local((tokens, D)), local((tokens, D))],
         scratch_shapes=[
             pltpu.VMEM(WINDOWED, BF16),
             pltpu.VMEM(WINDOWED, BF16),
+        ] + [pltpu.VMEM(dims, BF16) for dims in saved] + [
+            pltpu.VMEM((D, 3 * D), BF16),
+            pltpu.VMEM((D, D), BF16),
             pltpu.SemaphoreType.DMA((2, STRIPS)),
+            pltpu.SemaphoreType.DMA((SAVES + count,)),
+            pltpu.SemaphoreType.DMA((2,)),
         ],
         compiler_params=params(),
-        cost_estimate=cost(20 * 10**9, 10 * 2**20),
-    )(flag, tok, cot, lon, lat, corner, g1, wqkv, wout, g2)
-
-
-def mlp_specs(tokens, chunk):
-    steps = FF // chunk // 2
-    specs = {
-        "whole": pl.BlockSpec((tokens, D), lambda i, me: (0, 0)),
-        "gain": pl.BlockSpec((1, D), lambda i, me: (0, 0)),
-        "out": pl.BlockSpec((chunk, D), lambda i, me: (i, 0)),
-    }
-    for name, other in (("send", 1), ("keep", 0)):
-        def place(i, me, other=other):
-            return (me[0] if other == 0 else 1 - me[0]) * steps + i
-        specs[name] = [
-            pl.BlockSpec((D, chunk), lambda i, me, place=place: (0, place(i, me))),
-            pl.BlockSpec((chunk, D), lambda i, me, place=place: (place(i, me), 0)),
-        ]
-    return specs, steps
-
-
-def mlp_send(me, n2, cot, wup, wdown, chunk=512):
+        cost_estimate=cost(15 * 10**9, 10 * 2**20),
+    )(flag, tok, cot, lon, lat, corner, g1, *far(wqkv, wout), g2)
+
+
+def mlp(kind, me, n2, cot, wup, wdown, *carried):
     tokens = n2.shape[0]
-    specs, steps = mlp_specs(tokens, chunk)
-    whole, out = specs["whole"], specs["out"]
-    return pl.pallas_call(
-        mlp_send_kernel,
-        name="mlp_send",
-        grid_spec=pltpu.PrefetchScalarGridSpec(
-            num_scalar_prefetch=1,
-            grid=(steps,),
-            in_specs=[whole, whole] + specs["send"],
-            out_specs=[whole, whole, out, out],
-            scratch_shapes=[pltpu.VMEM((tokens, chunk), BF16), pltpu.VMEM((tokens, chunk), BF16)],
-        ),
-        out_shape=[shape((tokens, D), F32), shape((tokens, D), F32), shape((FF // 2, D)), shape((FF // 2, D))],
+    sums = [local((tokens, D), F32)] * 2
+    scratch = [pltpu.VMEM((tokens, CHUNK), BF16)] * 2
+    out_specs, aliases = [VM] * 3, {}
+    if kind == "send":
+        kernel, out_shape = send_kernel, sums + [shape((FF, D))]
+    elif kind == "first":
+        kernel, out_shape = keep_first_kernel, sums + [local((2 * CHUNK, D))]
+        aliases = {5: 0, 6: 1}
+    else:
+        kernel, out_shape = keep_second_kernel, [pltpu.HBM((tokens, D), F32)] * 2 + [pltpu.HBM((FF, D), BF16)]
+        out_specs = [HB, HB, VM]
+        scratch = scratch + [pltpu.VMEM((tokens, D), F32)] * 2 + [pltpu.SemaphoreType.DMA((2,))]
+    return pl.pallas_call(
+        kernel,
+        name="mlp_" + kind,
+        in_specs=[SM, VM, VM, VM, VM] + [VM] * len(carried),
+        out_specs=out_specs,
+        out_shape=out_shape,
+        scratch_shapes=scratch,
+        input_output_aliases=aliases,
         compiler_params=params(),
-        cost_estimate=cost(16 * 10**9, 10 * 2**20),
-    )(me, n2, cot, wup, wdown)
-
-
-def mlp_keep(me, n2, cot, wup, wdown, mid, g2, down, dn2, chunk=512):
-    tokens = n2.shape[0]
-    specs, steps = mlp_specs(tokens, chunk)
-    whole, out, gain = specs["whole"], specs["out"], specs["gain"]
-    return pl.pallas_call(
-        mlp_keep_kernel,
-        name="mlp_keep",
-        grid_spec=pltpu.PrefetchScalarGridSpec(
-            num_scalar_prefetch=1,
-            grid=(steps,),
-            in_specs=[whole, whole] + specs["keep"] + [whole, gain, whole, whole],
-            out_specs=[whole, whole, gain, out, out],
-            scratch_shapes=[
-                pltpu.VMEM((tokens, D), F32),
-                pltpu.VMEM((tokens, D), F32),
-                pltpu.VMEM((tokens, chunk), BF16),
-                pltpu.VMEM((tokens, chunk), BF16),
-            ],
-        ),
-        out_shape=[
-            shape((tokens, D)),
-            shape((tokens, D)),
-            shape((1, D), F32),
-            shape((FF // 2, D)),
-            shape((FF // 2, D)),
-        ],
-        compiler_params=params(),
-        cost_estimate=cost(16 * 10**9, 10 * 2**20),
-    )(me, n2, cot, wup, wdown, mid, g2, down, dn2)
-
-
-def back(me, dmid, n1, qkv, p, att, x, g1, wqkv, wout, dg2, res, field):
+        cost_estimate=cost((16 if kind == "send" else 8) * 10**9, 10 * 2**20),
+    )(me, *held(n2, cot, wup, wdown, *carried))
+
+
+def back(me, cot, mid, down, dn2, wout, qkv, p, wqkv, x, att, n1, g1, g2, field):
     tokens = x.shape[0]
+    count = tokens // WIN
     return pl.pallas_call(
         back_kernel,
         name="back",
-        in_specs=[SM] + [VM] * 11,
-        out_specs=[ANY] * 5 + [VM] * 3,
+        in_specs=[SM] + [HB] * 11 + [VM] * 2,
+        out_specs=[ANY] * 5 + [VM] * 7,
         out_shape=[shape(field), shape(field)] + rim_shapes(*field[:3]) + [
-            shape((tokens, 3 * D)),
-            shape((1, D), F32),
+            local((tokens, D)),
+            local((tokens, D)),
+            local((tokens, D)),
+            local((tokens, 3 * D)),
+            local((1, D), F32),
+            local((1, D), F32),
             shape((CHIPS_N, SLOTS, 128)),
         ],
         scratch_shapes=[
             pltpu.VMEM((tokens, D), BF16),
             pltpu.VMEM((tokens, D), BF16),
+            pltpu.VMEM((tokens, D), F32),
+            pltpu.VMEM((tokens, D), F32),
+            pltpu.VMEM((D, D), BF16),
+            pltpu.VMEM((tokens, 3 * D), BF16),
+            pltpu.VMEM((count, D // HD, WIN, WIN), BF16),
+            pltpu.VMEM((D, 3 * D), BF16),
+            pltpu.VMEM((tokens, D), BF16),
+            pltpu.VMEM((tokens, D), BF16),
+            pltpu.VMEM((tokens, D), BF16),
+            pltpu.VMEM((tokens, D), BF16),
             pltpu.VMEM(WINDOWED, BF16),
             pltpu.VMEM(WINDOWED, BF16),
+            pltpu.SemaphoreType.DMA((11,)),
             pltpu.SemaphoreType.DMA((2, STRIPS)),
         ],
-        compiler_params=params(),
+        compiler_params=params(40),
         cost_estimate=cost(30 * 10**9, 10 * 2**20),
-    )(me, dmid, n1, qkv, p, att, x, g1, wqkv, wout, dg2, res)
+    )(me, *far(cot, mid, down, dn2, wout, qkv, p, wqkv, x, att, n1), g1, g2)
 
 
 def keep_grads(me, n1, dqkv, att, dmid, dg1, dg2):
@@ -592,17 +671,29 @@
         out_shape=shape((CHIPS_N, SLOTS, 128)),
         compiler_params=params(),
         cost_estimate=cost(4 * 10**9, 4 * 2**20),
-    )(me, n1, dqkv, att, dmid, dg1, dg2)
+    )(me, *held(n1, dqkv, att, dmid, dg1, dg2))
+
+
+def simple(kernel, name, out_shape, *operands, moved=4 * 2**20, mib=56):
+    return pl.pallas_call(
+        kernel,
+        name=name,
+        in_specs=[VM] * len(operands),
+        out_specs=VM,
+        out_shape=out_shape,
+        compiler_params=params(mib),
+        cost_estimate=cost(10**9, moved),
+    )(*operands)
 
 
 def unpack_mlp(me, mine, theirs):
     return pl.pallas_call(
         unpack_mlp_kernel,
         name="unpack_mlp",
-        in_specs=[SM, VM, VM],
+        in_specs=[SM] + [VM] * 2,
         out_specs=[VM, VM],
         out_shape=[shape((D, FF), F32), shape((FF, D), F32)],
-        compiler_params=params(),
+        compiler_params=params(56),
         cost_estimate=cost(10**9, 12 * 2**20),
     )(me, mine, theirs)
 
@@ -644,22 +735,6 @@
     return lax.all_to_all(parts, CHIPS, 0, 0, tiled=True)
 
 
-def add_cores(keep, got):
-    return (keep.astype(F32) + got.astype(F32)).astype(BF16)
-
-
-def shared(parts):
-    return pl.pallas_call(
-        share_kernel,
-        name="share",
-        in_specs=[VM],
-        out_specs=VM,
-        out_shape=shape(parts.shape),
-        compiler_params=params(),
-        cost_estimate=cost(10**9, 2 * parts.size * 2),
-    )(parts)
-
-
 def shards(tokens, cotangent, norm_gain, w_qkv, w_out, mlp_gain, w_up, w_down):
     g1 = norm_gain.reshape(1, D)
     g2 = mlp_gain.reshape(1, D)
@@ -668,22 +743,24 @@
     me = lax.axis_index("c").astype(jnp.int32).reshape(1)
 
     rims = send_rims(*pack(tokens, cotangent), -1)
-    x, cot, n1, qkv, p, att, mid, n2 = front(flag, tokens, cotangent, *rims, g1, w_qkv, w_out, g2)
-    down, dn2, gup, gdown = mlp_send(me, n2, cot, w_up, w_down)
-    got = other_core(jnp.concatenate([gup, gdown]))
-    res, dmid, dg2, gup, gdown = mlp_keep(me, n2, cot, w_up, w_down, mid, g2, down, dn2)
-    mlp_part = add_cores(jnp.concatenate([gup, gdown]), got).reshape(CHIPS_N, -1, D)
-    mlp_part = exchange(mlp_part)
-    output, grad_tokens, lon, lat, corner, dqkv, dg1, send = back(
-        me, dmid, n1, qkv, p, att, x, g1, w_qkv, w_out, dg2, res, tokens.shape)
+    x, n1, qkv, p, att, mid, cot_far, cot, n2 = front(flag, tokens, cotangent, *rims, g1, w_qkv, w_out, g2)
+    fixed = (me, n2, cot, w_up, w_down)
+    down, dn2, grads = mlp("send", *fixed)
+    got = other_core(grads)
+    down, dn2, early = mlp("first", *fixed, down, dn2)
+    down, dn2, grads = mlp("second", *fixed, down, dn2, early, got)
+    sums = exchange(grads.reshape(CHIPS_N, SHARE, D))
+    output, grad_tokens, lon, lat, corner, att, n1, dmid, dqkv, dg1, dg2, send = back(
+        me, cot_far, mid, down, dn2, w_out, qkv, p, w_qkv, x, att, n1, g1, g2, tokens.shape)
     got = other_core(send)
     rims = send_rims(lon, lat, corner, 1)
     keep = keep_grads(me, n1, dqkv, att, dmid, dg1, dg2)
-    att_part = exchange(add_cores(keep, got))
     output, grad_tokens = place(output, grad_tokens, *rims)
-    mlp_mine = exchange(shared(mlp_part)).reshape(-1, D)
-    att_part, output, grad_tokens = lax.optimization_barrier((att_part, output, grad_tokens))
-    att_mine = exchange(shared(att_part))
+    mixed = exchange(simple(merge_kernel, "merge", pltpu.HBM((CHIPS_N, MIXED, 128), BF16), sums, keep, got))
+    mixed, output, grad_tokens = lax.optimization_barrier((mixed, output, grad_tokens))
+    share = simple(share_kernel, "share", pltpu.HBM((CHIPS_N, SLOTS, 128), BF16), mixed)
+    att_mine = exchange(share)
+    mlp_mine = simple(compact_kernel, "compact", shape((FF, D)), mixed, share)
     gup, gdown = unpack_mlp(me, mlp_mine, other_core(mlp_mine))
     att_mine, gup, gdown = lax.optimization_barrier((att_mine, gup, gdown))
     gqkv, gout, gains = unpack_att(me, att_mine, other_core(att_mine))

time: 302 us -> 217 us (0.72)
  Pallas kernels: 164 us -> 94.6 us
  blocking collectives: 39.6 us -> 0 us
  waiting for transfers between devices: 41.1 us -> 64.1 us
  starting transfers between devices: 44.6 us -> 52.1 us
  other arithmetic: 6.44 us -> 0 us
    pallas_call x8 -> x10, Pallas kernels: 130 us -> 73.7 us  [the longest x1 27.6 us: back(): pl.pallas_call(back_kernel, name='back', in_specs=[SM] + [HB] * 11 + [VM]...]
    all_to_all x1 -> x0, blocking collectives: 39.6 us -> none  [exchange(): return lax.all_to_all(parts, CHIPS, 0, 0, tiled=True)]
    ppermute x6, waiting for transfers between devices: 25.3 us -> 50 us  [send_rims(): moved.append(lax.ppermute(block, LAT + LON, route))]
    all_to_all x3, starting transfers between devices: 23.3 us -> 31 us  [exchange(): return lax.all_to_all(parts, CHIPS, 0, 0, tiled=True)]
    pallas_call x1, Pallas kernels: 23.9 us -> 16.8 us  [front(): pl.pallas_call(front_kernel, name='front', in_specs=[SM] + [ANY] * 5 + [V...]
    convert_element_type x2 -> x0, other arithmetic: 4.76 us -> none  [add_cores(): return (keep.astype(F32) + got.astype(F32)).astype(BF16)]
    pallas_call x1, Pallas kernels: 5.62 us -> 1.58 us  [keep_grads(): pl.pallas_call(keep_kernel, name='keep', in_specs=[SM] + [VM] * 6, out_sp...]
  transfers between devices with their start and end apart: 13 -> 13, of which waited for: 4 -> 4; matrix products, arithmetic and copies ran while one was open for 1% -> 0% of each run, Pallas kernels for 30% -> 20%
where the time goes in v3:
time: 217 us
  Pallas kernels  94.6 us (44%)
  waiting for transfers between devices  64.1 us (30%)
  starting transfers between devices  52.1 us (24%)
  local copies, waits for them, and re-layouts  5.15 us (2%)
    ppermute x6, waiting for transfers between devices, send_rims(): moved.append(lax.ppermute(block, LAT + LON, route))  50 us
    all_to_all x3, starting transfers between devices, exchange(): return lax.all_to_all(parts, CHIPS, 0, 0, tiled=True)  31 us
    pallas_call x1, Pallas kernels, back(): pl.pallas_call(back_kernel, name='back', in_specs=[SM] + [HB] * 11 + [VM]...  27.6 us
    pallas_call x3, Pallas kernels, mlp(): pl.pallas_call(kernel, name='mlp_' + kind, in_specs=[SM, VM, VM, VM, VM]...  23.8 us
    pallas_call x1, Pallas kernels, front(): pl.pallas_call(front_kernel, name='front', in_specs=[SM] + [ANY] * 5 + [V...  16.8 us
    ppermute x6, starting transfers between devices, send_rims(): moved.append(lax.ppermute(block, LAT + LON, route))  15.5 us
    pallas_call x3, Pallas kernels, simple(): pl.pallas_call(kernel, name=name, in_specs=[VM] * len(operands), out_spec...  11.8 us
    all_to_all x3, waiting for transfers between devices, exchange(): return lax.all_to_all(parts, CHIPS, 0, 0, tiled=True)  11.6 us
  transfers between devices with their start and end apart: 13, of which 4 were waited for; matrix products, arithmetic and copies ran while one was open for 0% of the time, Pallas kernels for 20%

profile of v3, /device:TPU:1, one launch (start us, length us, event | category | flops | bytes accessed | tf_op | source)
XLA Modules:
  0.0 216.8 jit_solution(11950071847485519097)
XLA Ops:
  0.7 2.3 %pack.1 = (bf16[2,21,6,2,512]{4,3,2,1,0:T(2,128)(2,1)}, bf16[2,3,18,2,512]{4,3,2,1,0:T(2,128)(2,1)}, bf16[2,3,6,2,512]{4,3,2,1,0:T(2,128)(2,1)}) custom-call(bf16[24,24,2,512]{3,2,1,0:T(2,128)(2,1)} %tok_ref.3, bf16[24,24,2,512]{3,2,1,0:T(2,128)(2,1)} %cot_ref.3), custom_call_target="tpu_custom_call" | custom-call | tf_op jit(solution)/shard_map/pack/pallas_call | solution.py:535
  4.5 3.9 %collective-permute-start.1 = (bf16[2,3,18,2,512]{4,3,2,1,0:T(2,128)(2,1)}, bf16[2,3,18,2,512]{4,3,2,1,0:T(2,128)(2,1)S(1)}, u32[]{:S(2)}, u32[]{:S(2)}) collective-permute-start(bf16[2,3,18,2,512]{4,3,2,1,0:T(2,128)(2,1)} %get-tuple-element.55), channel_id=1, source_target_pairs={{0,112},{1,113},{2,114},{3,115},{4,116},{5,117},{6,118},{7,119},{8... | collective-permute-start | bytes 663560 | tf_op jit(solution)/shard_map/ppermute | solution.py:726
  8.4 5.8 %collective-permute-start.2 = (bf16[2,3,6,2,512]{4,3,2,1,0:T(2,128)(2,1)}, bf16[2,3,6,2,512]{4,3,2,1,0:T(2,128)(2,1)S(1)}, u32[]{:S(2)}, u32[]{:S(2)}) collective-permute-start(bf16[2,3,6,2,512]{4,3,2,1,0:T(2,128)(2,1)} %get-tuple-element.56), channel_id=1, source_target_pairs={{0,127},{1,112},{2,113},{3,114},{4,115},{5,116},{6,117},{7,118},{8... | collective-permute-start | bytes 221192 | tf_op jit(solution)/shard_map/ppermute | solution.py:726
  14.1 2.3 %collective-permute-done.2.corner_ref = bf16[2,3,6,2,512]{4,3,2,1,0:T(2,128)(2,1)S(1)} collective-permute-done((bf16[2,3,6,2,512]{4,3,2,1,0:T(2,128)(2,1)}, bf16[2,3,6,2,512]{4,3,2,1,0:T(2,128)(2,1)S(1)}, u32[]{:S(2)}, u32[]{:S(2)}) %collective-permute-start.2) | collective-permute-done | bytes 73760 | tf_op jit(solution)/shard_map/ppermute | solution.py:726
  16.5 16.8 %front.1 = (bf16[1152,512]{1,0:T(8,128)(2,1)}, bf16[1152,512]{1,0:T(8,128)(2,1)}, bf16[1152,1536]{1,0:T(8,128)(2,1)}, bf16[8,8,144,144]{3,2,1,0:T(8,128)(2,1)}, ...) custom-call(s32[1]{0:T(128)} %bitcast.1.flag_ref, ...), custom_call_target="tpu_custom_call" | custom-call | flops 15000000512 | bytes 10485760 | tf_op jit(solution)/shard_map/front/pallas_call | solution.py:577
  33.4 10.7 %mlp_send.1 = (f32[1152,512]{1,0:T(8,128)S(1)}, f32[1152,512]{1,0:T(8,128)S(1)}, bf16[2048,512]{1,0:T(8,128)(2,1)S(1)}) custom-call(s32[1]{0:T(128)} %bitcast.me_ref, bf16[1152,512]{1,0:T(8,128)(2,1)S(1)} %get-tuple-element.57.n2_ref, bf16[1152,512]{1,0:T(8,128)(2,1)S(1)} %get-tuple-element.58.cot_ref, bf16[512,2048]{1,0:T(8,128)(2,1)S(1)} %copy-done.3, ...), custom_call_target="tpu_custom_call" | custom-call | flops 16000000000 | bytes 10485760 | tf_op jit(solution)/shard_map/mlp_send/pallas_call | solution.py:612
  44.1 3.4 %collective-permute-start.3 = (bf16[2048,512]{1,0:T(8,128)(2,1)S(1)}, bf16[2048,512]{1,0:T(8,128)(2,1)S(1)}, u32[]{:S(2)}, u32[]{:S(2)}) collective-permute-start(bf16[2048,512]{1,0:T(8,128)(2,1)S(1)} %get-tuple-element.64), channel_id=1, source_target_pairs={{0,1},{1,0},{2,3},{3,2},{4,5},{5,4},{6,7},{7,6},{8,9},{9,8},{10,11... | collective-permute-start | bytes 6291464 | tf_op jit(solution)/shard_map/ppermute | solution.py:731
  47.5 5.8 %mlp_first.1 = (f32[1152,512]{1,0:T(8,128)S(1)}, f32[1152,512]{1,0:T(8,128)S(1)}, bf16[1024,512]{1,0:T(8,128)(2,1)S(1)}) custom-call(s32[1]{0:T(128)} %bitcast.me_ref, bf16[1152,512]{1,0:T(8,128)(2,1)S(1)} %get-tuple-element.57.n2_ref, bf16[1152,512]{1,0:T(8,128)(2,1)S(1)} %get-tuple-element.58.cot_ref, ...), custom_call_target="tpu_custom_call", output_to_operand_aliasing={{0}: (5, {}), {1}: (6, {})} | custom-call | flops 8000000000 | bytes 10485760 | tf_op jit(solution)/shard_map/mlp_first/pallas_call | solution.py:612
  53.2 7.3 %mlp_second.1 = (f32[1152,512]{1,0:T(8,128)}, f32[1152,512]{1,0:T(8,128)}, bf16[2048,512]{1,0:T(8,128)(2,1)}) custom-call(s32[1]{0:T(128)} %bitcast.me_ref, bf16[1152,512]{1,0:T(8,128)(2,1)S(1)} %get-tuple-element.57.n2_ref, bf16[1152,512]{1,0:T(8,128)(2,1)S(1)} %get-tuple-element.58.cot_ref, bf16[512,2048]{1,0:T(8,128)(2,1)S(1)} %copy-done.3, ...), custom_call_target="tpu_custom_call" | custom-call | flops 8000000000 | bytes 10485760 | tf_op jit(solution)/shard_map/mlp_second/pallas_call | solution.py:612
  60.6 11.6 %all-to-all-start = ((bf16[64,32,512]{2,1,0:T(8,128)(2,1)}), bf16[64,32,512]{2,1,0:T(8,128)(2,1)S(1)}, u32[]{:S(2)}, u32[]{:S(2)}) async-start(bf16[64,32,512]{2,1,0:T(8,128)(2,1)} %bitcast.11), calls=%async_computation | async-start | bytes 4194304 | tf_op jit(solution)/shard_map/all_to_all | solution.py:735
  72.1 27.6 %back.1 = (bf16[24,24,2,512]{3,2,1,0:T(2,128)(2,1)}, bf16[24,24,2,512]{3,2,1,0:T(2,128)(2,1)}, bf16[2,21,6,2,512]{4,3,2,1,0:T(2,128)(2,1)S(1)}, bf16[2,3,18,2,51...) custom-call(s32[1]{0:T(128)} %bitcast.me_ref, ...), custom_call_target="tpu_custom_call" | custom-call | flops 30000001024 | bytes 10485760 | tf_op jit(solution)/shard_map/back/pallas_call | solution.py:628
  100.6 1.6 keep.1.keep_ref
  104.6 4.7 %merge.1 = bf16[64,200,128]{2,1,0:T(8,128)(2,1)} custom-call(bf16[64,32,512]{2,1,0:T(8,128)(2,1)} %copy-done.7, bf16[64,72,128]{2,1,0:T(8,128)(2,1)} %copy-done.2, bf16[64,72,128]{2,1,0:T(8,128)(2,1)} %collective-permute-done.4.got_ref), custom_call_target="tpu_custom_call" | custom-call | flops 1000000000 | bytes 4194304 | tf_op jit(solution)/shard_map/merge/pallas_call | solution.py:678
  109.3 10.0 %all-to-all-start.1 = ((bf16[64,200,128]{2,1,0:T(8,128)(2,1)}), bf16[64,200,128]{2,1,0:T(8,128)(2,1)}, u32[]{:S(2)}, u32[]{:S(2)}) async-start(bf16[64,200,128]{2,1,0:T(8,128)(2,1)} %merge.1), calls=%async_computation.1 | async-start | bytes 6553600 | tf_op jit(solution)/shard_map/all_to_all | solution.py:735
  119.3 1.8 collective-permute-start.5
  123.6 47.7 %collective-permute-done.7.corner_ref = bf16[2,3,6,2,512]{4,3,2,1,0:T(2,128)(2,1)S(1)} collective-permute-done((bf16[2,3,6,2,512]{4,3,2,1,0:T(2,128)(2,1)S(1)}, bf16[2,3,6,2,512]{4,3,2,1,0:T(2,128)(2,1)S(1)}, u32[]{:S(2)}, u32[]{:S(2)}) %collective-permute-start.7) | collective-permute-done | bytes 73760 | tf_op jit(solution)/shard_map/ppermute | solution.py:726
  172.2 2.1 place.1
  174.3 3.2 %share.1.after_ref = bf16[64,72,128]{2,1,0:T(8,128)(2,1)} custom-call(bf16[64,200,128]{2,1,0:T(8,128)(2,1)} %all-to-all-done.1.parts_ref), custom_call_target="tpu_custom_call" | custom-call | flops 1000000000 | bytes 4194304 | tf_op jit(solution)/shard_map/share/pallas_call | solution.py:678
  177.4 3.9 %compact.1.mine_ref = bf16[2048,512]{1,0:T(8,128)(2,1)} custom-call(bf16[64,200,128]{2,1,0:T(8,128)(2,1)} %all-to-all-done.1.parts_ref, bf16[64,72,128]{2,1,0:T(8,128)(2,1)} %share.1.after_ref), custom_call_target="tpu_custom_call" | custom-call | flops 1000000000 | bytes 4194304 | tf_op jit(solution)/shard_map/compact/pallas_call | solution.py:678
  181.4 9.4 %all-to-all-start.2 = ((bf16[64,72,128]{2,1,0:T(8,128)(2,1)}), bf16[64,72,128]{2,1,0:T(8,128)(2,1)S(1)}, u32[]{:S(2)}, u32[]{:S(2)}) async-start(bf16[64,72,128]{2,1,0:T(8,128)(2,1)} %share.1.after_ref), calls=%async_computation.2 | async-start | bytes 2359296 | tf_op jit(solution)/shard_map/all_to_all | solution.py:735
  192.1 6.0 %unpack_mlp.1 = (f32[512,2048]{1,0:T(8,128)}, f32[2048,512]{1,0:T(8,128)}) custom-call(s32[1]{0:T(128)} %bitcast.me_ref, bf16[2048,512]{1,0:T(8,128)(2,1)} %compact.1.mine_ref, bf16[2048,512]{1,0:T(8,128)(2,1)} %copy-done.8), custom_call_target="tpu_custom_call" | custom-call | flops 1000000000 | bytes 12582912 | tf_op jit(solution)/shard_map/unpack_mlp/pallas_call | solution.py:690
  198.2 11.6 %all-to-all-done.2.mine_ref = bf16[64,72,128]{2,1,0:T(8,128)(2,1)S(1)} async-done(((bf16[64,72,128]{2,1,0:T(8,128)(2,1)}), bf16[64,72,128]{2,1,0:T(8,128)(2,1)S(1)}, u32[]{:S(2)}, u32[]{:S(2)}) %all-to-all-start.2) | async-done | bytes 1179680 | tf_op jit(solution)/shard_map/all_to_all | solution.py:735
  211.2 2.5 %collective-permute-done.9.theirs_ref = bf16[64,72,128]{2,1,0:T(8,128)(2,1)S(1)} collective-permute-done((bf16[64,72,128]{2,1,0:T(8,128)(2,1)S(1)}, bf16[64,72,128]{2,1,0:T(8,128)(2,1)S(1)}, u32[]{:S(2)}, u32[]{:S(2)}) %collective-permute-start.9) | collective-permute-done | bytes 1179680 | tf_op jit(solution)/shard_map/ppermute | solution.py:731
  213.7 2.5 %unpack_att.1 = (f32[512,1536]{1,0:T(8,128)}, f32[512,512]{1,0:T(8,128)}, f32[16,512]{1,0:T(8,128)S(1)}) custom-call(s32[1]{0:T(128)} %bitcast.me_ref, bf16[64,72,128]{2,1,0:T(8,128)(2,1)S(1)} %all-to-all-done.2.mine_ref, bf16[64,72,128]{2,1,0:T(8,128)(2,1)S(1)} %collective-permute-done.9.theirs_ref), custom_call_target="tpu_custom_call" | custom-call | flops 1000000000 | bytes 6291456 | tf_op jit(solution)/shard_map/unpack_att/pallas_call | solution.py:702
  (40 shorter events, 11.4 us)
Async XLA Ops:
  0.6 15.8 %copy-start = (bf16[24,24,2,512]{3,2,1,0:T(2,128)(2,1)S(1)}, bf16[24,24,2,512]{3,2,1,0:T(2,128)(2,1)}, u32[]{:S(2)}) copy-start(bf16[24,24,2,512]{3,2,1,0:T(2,128)(2,1)} %tok_ref.3) | copy-start | bytes 3538948
  0.6 15.8 %copy-start.1 = (bf16[24,24,2,512]{3,2,1,0:T(2,128)(2,1)S(1)}, bf16[24,24,2,512]{3,2,1,0:T(2,128)(2,1)}, u32[]{:S(2)}) copy-start(bf16[24,24,2,512]{3,2,1,0:T(2,128)(2,1)} %cot_ref.3) | copy-start | bytes 3538948
  0.7 15.8 %copy-start.5 = (f32[512]{0:T(512)S(1)}, f32[512]{0:T(512)}, u32[]{:S(2)}) copy-start(f32[512]{0:T(512)} %param.10) | copy-start | bytes 6148
  0.7 15.8 %copy-start.6 = (f32[512]{0:T(512)S(1)}, f32[512]{0:T(512)}, u32[]{:S(2)}) copy-start(f32[512]{0:T(512)} %param.13) | copy-start | bytes 6148
  3.0 13.5 %collective-permute-start = (bf16[2,21,6,2,512]{4,3,2,1,0:T(2,128)(2,1)}, bf16[2,21,6,2,512]{4,3,2,1,0:T(2,128)(2,1)S(1)}, u32[]{:S(2)}, u32[]{:S(2)}) collective-permute-start(bf16[2,21,6,2,512]{4,3,2,1,0:T(2,128)(2,1)} %get-tuple-element.54), channel_id=1, source_target_pairs={{0,15},{1,0},{2,1},{3,2},{4,3},{5,4},{6,5},{7,6},{8,7},{9,8},{10,9... | collective-permute-start | bytes 1548296 | tf_op jit(solution)/shard_map/ppermute | solution.py:726
  4.5 12.0 %collective-permute-start.1 = (bf16[2,3,18,2,512]{4,3,2,1,0:T(2,128)(2,1)}, bf16[2,3,18,2,512]{4,3,2,1,0:T(2,128)(2,1)S(1)}, u32[]{:S(2)}, u32[]{:S(2)}) collective-permute-start(bf16[2,3,18,2,512]{4,3,2,1,0:T(2,128)(2,1)} %get-tuple-element.55), channel_id=1, source_target_pairs={{0,112},{1,113},{2,114},{3,115},{4,116},{5,117},{6,118},{7,119},{8... | collective-permute-start | bytes 663560 | tf_op jit(solution)/shard_map/ppermute | solution.py:726
  8.4 8.1 %collective-permute-start.2 = (bf16[2,3,6,2,512]{4,3,2,1,0:T(2,128)(2,1)}, bf16[2,3,6,2,512]{4,3,2,1,0:T(2,128)(2,1)S(1)}, u32[]{:S(2)}, u32[]{:S(2)}) collective-permute-start(bf16[2,3,6,2,512]{4,3,2,1,0:T(2,128)(2,1)} %get-tuple-element.56), channel_id=1, source_target_pairs={{0,127},{1,112},{2,113},{3,114},{4,115},{5,116},{6,117},{7,118},{8... | collective-permute-start | bytes 221192 | tf_op jit(solution)/shard_map/ppermute | solution.py:726
  16.5 16.8 %copy-start.3 = (bf16[512,2048]{1,0:T(8,128)(2,1)S(1)}, bf16[512,2048]{1,0:T(8,128)(2,1)}, u32[]{:S(2)}) copy-start(bf16[512,2048]{1,0:T(8,128)(2,1)} %wup_ref.5) | copy-start | bytes 6291460
  16.5 16.8 %copy-start.4 = (bf16[2048,512]{1,0:T(8,128)(2,1)S(1)}, bf16[2048,512]{1,0:T(8,128)(2,1)}, u32[]{:S(2)}) copy-start(bf16[2048,512]{1,0:T(8,128)(2,1)} %wdown_ref.5) | copy-start | bytes 6291460
  44.1 9.1 %collective-permute-start.3 = (bf16[2048,512]{1,0:T(8,128)(2,1)S(1)}, bf16[2048,512]{1,0:T(8,128)(2,1)S(1)}, u32[]{:S(2)}, u32[]{:S(2)}) collective-permute-start(bf16[2048,512]{1,0:T(8,128)(2,1)S(1)} %get-tuple-element.64), channel_id=1, source_target_pairs={{0,1},{1,0},{2,3},{3,2},{4,5},{5,4},{6,7},{7,6},{8,9},{9,8},{10,11... | collective-permute-start | bytes 6291464 | tf_op jit(solution)/shard_map/ppermute | solution.py:731
  60.6 42.7 %all-to-all-start = ((bf16[64,32,512]{2,1,0:T(8,128)(2,1)}), bf16[64,32,512]{2,1,0:T(8,128)(2,1)S(1)}, u32[]{:S(2)}, u32[]{:S(2)}) async-start(bf16[64,32,512]{2,1,0:T(8,128)(2,1)} %bitcast.11), calls=%async_computation | async-start | bytes 4194304 | tf_op jit(solution)/shard_map/all_to_all | solution.py:735
  99.8 3.5 %collective-permute-start.4 = (bf16[64,72,128]{2,1,0:T(8,128)(2,1)S(1)}, bf16[64,72,128]{2,1,0:T(8,128)(2,1)}, u32[]{:S(2)}, u32[]{:S(2)}) collective-permute-start(bf16[64,72,128]{2,1,0:T(8,128)(2,1)S(1)} %get-tuple-element.81), channel_id=1, source_target_pairs={{0,1},{1,0},{2,3},{3,2},{4,5},{5,4},{6,7},{7,6},{8,9},{9,8},{10,11... | collective-permute-start | bytes 3538952 | tf_op jit(solution)/shard_map/ppermute | solution.py:731
  102.2 1.0 copy-start.2
  103.3 1.3 copy-start.7
  109.3 65.0 %all-to-all-start.1 = ((bf16[64,200,128]{2,1,0:T(8,128)(2,1)}), bf16[64,200,128]{2,1,0:T(8,128)(2,1)}, u32[]{:S(2)}, u32[]{:S(2)}) async-start(bf16[64,200,128]{2,1,0:T(8,128)(2,1)} %merge.1), calls=%async_computation.1 | async-start | bytes 6553600 | tf_op jit(solution)/shard_map/all_to_all | solution.py:735
  119.3 52.0 %collective-permute-start.5 = (bf16[2,21,6,2,512]{4,3,2,1,0:T(2,128)(2,1)S(1)}, bf16[2,21,6,2,512]{4,3,2,1,0:T(2,128)(2,1)S(1)}, u32[]{:S(2)}, u32[]{:S(2)}) collective-permute-start(bf16[2,21,6,2,512]{4,3,2,1,0:T(2,128)(2,1)S(1)} %get-tuple-element.84), channel_id=1, source_target_pairs={{0,1},{1,2},{2,3},{3,4},{4,5},{5,6},{6,7},{7,8},{8,9},{9,10},{10,1... | collective-permute-start | bytes 1548296 | tf_op jit(solution)/shard_map/ppermute | solution.py:726
  121.2 50.1 %collective-permute-start.6 = (bf16[2,3,18,2,512]{4,3,2,1,0:T(2,128)(2,1)S(1)}, bf16[2,3,18,2,512]{4,3,2,1,0:T(2,128)(2,1)S(1)}, u32[]{:S(2)}, u32[]{:S(2)}) collective-permute-start(bf16[2,3,18,2,512]{4,3,2,1,0:T(2,128)(2,1)S(1)} %get-tuple-element.85), channel_id=1, source_target_pairs={{0,16},{1,17},{2,18},{3,19},{4,20},{5,21},{6,22},{7,23},{8,24},{9,... | collective-permute-start | bytes 663560 | tf_op jit(solution)/shard_map/ppermute | solution.py:726
  122.4 48.9 %collective-permute-start.7 = (bf16[2,3,6,2,512]{4,3,2,1,0:T(2,128)(2,1)S(1)}, bf16[2,3,6,2,512]{4,3,2,1,0:T(2,128)(2,1)S(1)}, u32[]{:S(2)}, u32[]{:S(2)}) collective-permute-start(bf16[2,3,6,2,512]{4,3,2,1,0:T(2,128)(2,1)S(1)} %get-tuple-element.86), channel_id=1, source_target_pairs={{0,17},{1,18},{2,19},{3,20},{4,21},{5,22},{6,23},{7,24},{8,25},{9,... | collective-permute-start | bytes 221192 | tf_op jit(solution)/shard_map/ppermute | solution.py:726
  171.3 0.7 copy-start.10
  171.3 0.9 copy-start.9
  181.4 9.4 %collective-permute-start.8 = (bf16[2048,512]{1,0:T(8,128)(2,1)}, bf16[2048,512]{1,0:T(8,128)(2,1)S(1)}, u32[]{:S(2)}, u32[]{:S(2)}) collective-permute-start(bf16[2048,512]{1,0:T(8,128)(2,1)} %compact.1.mine_ref), channel_id=1, source_target_pairs={{0,1},{1,0},{2,3},{3,2},{4,5},{5,4},{6,7},{7,6},{8,9},{9,8},{10,11... | collective-permute-start | bytes 6291464 | tf_op jit(solution)/shard_map/ppermute | solution.py:731
  181.4 28.4 %all-to-all-start.2 = ((bf16[64,72,128]{2,1,0:T(8,128)(2,1)}), bf16[64,72,128]{2,1,0:T(8,128)(2,1)S(1)}, u32[]{:S(2)}, u32[]{:S(2)}) async-start(bf16[64,72,128]{2,1,0:T(8,128)(2,1)} %share.1.after_ref), calls=%async_computation.2 | async-start | bytes 2359296 | tf_op jit(solution)/shard_map/all_to_all | solution.py:735
  190.8 1.4 copy-start.8
  209.8 3.9 %collective-permute-start.9 = (bf16[64,72,128]{2,1,0:T(8,128)(2,1)S(1)}, bf16[64,72,128]{2,1,0:T(8,128)(2,1)S(1)}, u32[]{:S(2)}, u32[]{:S(2)}) collective-permute-start(bf16[64,72,128]{2,1,0:T(8,128)(2,1)S(1)} %all-to-all-done.2.mine_ref), channel_id=1, source_target_pairs={{0,1},{1,0},{2,3},{3,2},{4,5},{5,4},{6,7},{7,6},{8,9},{9,8},{10,11... | collective-permute-start | bytes 3538952 | tf_op jit(solution)/shard_map/ppermute | solution.py:731
  (1 other events, 0.6 us)

commit v4 on v3

--- a/solution.py
+++ b/solution.py
@@ -140,7 +140,7 @@
     gain1 = g1_ref[...]
     gain2 = g2_ref[...]
 
-    @pl.loop(0, count)
+    @pl.loop(0, count, unroll=2)
     def _(w):
         rows = pl.ds(pl.multiple_of(w * WIN, WIN), WIN)
         xhat, _ = normalised(x_ref[rows, :].astype(F32))
@@ -166,7 +166,7 @@
     split = key_group != query_group
     low = lax.broadcasted_iota(jnp.int32, (WIN, PAIR), 1) < HD
 
-    @pl.loop(0, count)
+    @pl.loop(0, count, unroll=4)
     def _(w):
         rows = pl.ds(pl.multiple_of(w * WIN, WIN), WIN)
         cut = jnp.logical_and(flag_ref[0] == 1, w >= count - per_row)
@@ -280,11 +280,12 @@
 
 
 HALF = D // 2
-SLOTS = 72
 CHIPS_N = 64
-
-
-def att_grads(half, n1_ref, dqkv_ref, att_ref, dmid_ref, dg1, dg2, out_ref):
+GRADS = 64
+GAINS = 8
+
+
+def att_grads(half, n1_ref, dqkv_ref, att_ref, dmid_ref, out_ref):
     per = D // (CHIPS_N // 4)
     lanes = pl.ds(pl.multiple_of(half * HALF, HALF), HALF)
     for part in range(4):
@@ -298,17 +299,12 @@
         for block in range(2):
             piece = grad[:, block * 128:(block + 1) * 128].reshape(CHIPS_N // 4, per, 128)
             out_ref[first:first + CHIPS_N // 4, block * per:(block + 1) * per, :] = piece
-    out_ref[:, 2 * per:, :] = jnp.zeros((CHIPS_N, SLOTS - 2 * per, 128), BF16)
-    gain = jnp.where(half == 0, dg1, dg2)
-    for block in range(D // 128):
-        row = jnp.broadcast_to(gain[:, block * 128:(block + 1) * 128], (SLOTS - 2 * per, 128))
-        out_ref[block, 2 * per:, :] = row.astype(BF16)
 
 
 def att_back(first, last, datt_ref, qkv_ref, p_ref, dqkv_ref):
     low = lax.broadcasted_iota(jnp.int32, (WIN, PAIR), 1) < HD
 
-    @pl.loop(first, last)
+    @pl.loop(first, last, unroll=4)
     def _(w):
         rows = pl.ds(pl.multiple_of(w * WIN, WIN), WIN)
         for pair in range(D // PAIR):
@@ -333,29 +329,28 @@
             dqkv_ref[rows, 2 * D + pair * PAIR:2 * D + (pair + 1) * PAIR] = jnp.where(low, dvs[0], dvs[1]).astype(BF16)
 
 
-def back_kernel(me_ref, cot_hbm, mid_hbm, down_hbm, dn2_hbm, wout_hbm, qkv_hbm, p_hbm, wqkv_hbm, x_hbm, att_hbm, n1_hbm,
-                g1_ref, g2_ref,
-                out_ref, grad_ref, lon_ref, lat_ref, corner_ref,
-                att_ref, n1_ref, dmid_ref, dqkv_ref, dg1_ref, dg2_ref, send_ref,
-                cot_ref, mid_ref, down_ref, dn2_ref, wout_ref, qkv_ref, p_ref, wqkv_ref, x_ref,
-                datt_ref, dx_ref, res_ref, res_buf, dx_buf, in_sems, sems):
-    loads = {}
-    for i, (name, source, target) in enumerate((
-        ("cot", cot_hbm, cot_ref), ("mid", mid_hbm, mid_ref), ("down", down_hbm, down_ref), ("dn2", dn2_hbm, dn2_ref),
-        ("wout", wout_hbm, wout_ref), ("qkv", qkv_hbm, qkv_ref), ("p", p_hbm, p_ref), ("wqkv", wqkv_hbm, wqkv_ref),
-        ("x", x_hbm, x_ref), ("att", att_hbm, att_ref), ("n1", n1_hbm, n1_ref),
-    )):
-        loads[name] = pltpu.make_async_copy(source, target, in_sems.at[i])
-        loads[name].start()
-
-    gain1 = g1_ref[...]
+def start_loads(pairs, sems):
+    loads = []
+    for i, (source, target) in enumerate(pairs):
+        loads.append(pltpu.make_async_copy(source, target, sems.at[i]))
+        loads[-1].start()
+    return loads
+
+
+def back_kernel(cot_hbm, mid_hbm, down_hbm, dn2_hbm, wout_hbm, qkv_hbm, p_hbm, att_hbm, n1_hbm, g2_ref,
+                res_out, dmid_out, dqkv_out, dg2_ref, att_ref, n1_ref, dmid_ref, dqkv_ref,
+                cot_ref, mid_ref, down_ref, dn2_ref, wout_ref, qkv_ref, p_ref, datt_ref, res_ref, in_sems, sems):
+    loads = start_loads((
+        (cot_hbm, cot_ref), (mid_hbm, mid_ref), (down_hbm, down_ref), (dn2_hbm, dn2_ref),
+        (wout_hbm, wout_ref), (qkv_hbm, qkv_ref), (p_hbm, p_ref), (att_hbm, att_ref), (n1_hbm, n1_ref),
+    ), in_sems)
     gain2 = g2_ref[...]
     dg2_ref[...] = jnp.zeros_like(dg2_ref)
     tokens = cot_ref.shape[0]
-    for name in ("cot", "mid", "down", "dn2"):
-        loads[name].wait()
-
-    @pl.loop(0, tokens // WIN)
+    for load in loads[:4]:
+        load.wait()
+
+    @pl.loop(0, tokens // WIN, unroll=2)
     def _(b):
         rows = pl.ds(pl.multiple_of(b * WIN, WIN), WIN)
         mid = mid_ref[rows, :].astype(F32)
@@ -366,6 +361,38 @@
         dmid = cot_ref[rows, :].astype(F32) + norm_pullback(xhat, scale, gain2, dn2)
         dmid_ref[rows, :] = dmid.astype(BF16)
 
+    saves = [
+        pltpu.make_async_copy(res_ref, res_out, sems.at[0]),
+        pltpu.make_async_copy(dmid_ref, dmid_out, sems.at[1]),
+    ]
+    for copy in saves:
+        copy.start()
+    loads[4].wait()
+
+    @pl.loop(0, tokens // ROWS)
+    def _(b):
+        rows = pl.ds(pl.multiple_of(b * ROWS, ROWS), ROWS)
+        datt_ref[rows, :] = mm_t(dmid_ref[rows, :], wout_ref[...]).astype(BF16)
+
+    loads[5].wait()
+    loads[6].wait()
+    att_back(0, tokens // WIN, datt_ref, qkv_ref, p_ref, dqkv_ref)
+    saves.append(pltpu.make_async_copy(dqkv_ref, dqkv_out, sems.at[2]))
+    saves[-1].start()
+    for copy in loads[7:] + saves:
+        copy.wait()
+
+
+def tokens_kernel(dqkv_hbm, wqkv_hbm, x_hbm, dmid_hbm, res_hbm, g1_ref, after_ref,
+                  out_ref, grad_ref, lon_ref, lat_ref, corner_ref, dg1_ref,
+                  dqkv_ref, wqkv_ref, x_ref, dmid_ref, res_ref, dx_ref, res_buf, dx_buf, in_sems, sems):
+    loads = start_loads((
+        (res_hbm, res_ref), (dqkv_hbm, dqkv_ref), (wqkv_hbm, wqkv_ref), (x_hbm, x_ref), (dmid_hbm, dmid_ref),
+    ), in_sems)
+    gain1 = g1_ref[...]
+    tokens = x_ref.shape[0]
+    dg1_ref[...] = jnp.zeros_like(dg1_ref)
+    loads[0].wait()
     for band in range(BANDS):
         for side in range(SIDES):
             w = band * SIDES + side
@@ -373,21 +400,8 @@
     res_copies = scatter_windows(0, res_buf, out_ref, lon_ref, lat_ref, corner_ref, sems.at[0])
     for copy in res_copies:
         copy.start()
-
-    loads["wout"].wait()
-
-    @pl.loop(0, tokens // ROWS)
-    def _(b):
-        rows = pl.ds(pl.multiple_of(b * ROWS, ROWS), ROWS)
-        datt_ref[rows, :] = mm_t(dmid_ref[rows, :], wout_ref[...]).astype(BF16)
-
-    loads["qkv"].wait()
-    loads["p"].wait()
-    att_back(0, tokens // WIN, datt_ref, qkv_ref, p_ref, dqkv_ref)
-
-    dg1_ref[...] = jnp.zeros_like(dg1_ref)
-    loads["wqkv"].wait()
-    loads["x"].wait()
+    for load in loads[1:]:
+        load.wait()
 
     @pl.loop(0, tokens // ROWS)
     def _(b):
@@ -405,15 +419,13 @@
     dx_copies = scatter_windows(1, dx_buf, grad_ref, lon_ref, lat_ref, corner_ref, sems.at[1])
     for copy in dx_copies:
         copy.start()
-    loads["att"].wait()
-    loads["n1"].wait()
-    att_grads(1 - me_ref[0], n1_ref, dqkv_ref, att_ref, dmid_ref, dg1_ref[...], dg2_ref[...], send_ref)
     for copy in res_copies + dx_copies:
         copy.wait()
 
 
-def keep_kernel(me_ref, n1_ref, dqkv_ref, att_ref, dmid_ref, dg1_ref, dg2_ref, keep_ref):
-    att_grads(me_ref[0], n1_ref, dqkv_ref, att_ref, dmid_ref, dg1_ref[...], dg2_ref[...], keep_ref)
+SHARE = FF // CHIPS_N
+MLP = SHARE * D // 128
+ALL = GRADS + GAINS + MLP
 
 
 def total_of(parts_ref, rows):
@@ -423,57 +435,70 @@
     return total.astype(BF16)
 
 
-SHARE = FF // CHIPS_N
-MIXED = SLOTS + SHARE * D // 128
-
-
-def lane_blocks():
-    return [(slice(SLOTS + i * SHARE, SLOTS + (i + 1) * SHARE), slice(i * 128, (i + 1) * 128)) for i in range(D // 128)]
-
-
-def merge_kernel(parts_ref, keep_ref, got_ref, out_ref):
-    total = total_of(parts_ref, slice(0, SHARE))
+def half_kernel(half_ref, n1_ref, dqkv_ref, att_ref, dmid_ref, out_ref):
+    att_grads(half_ref[0], n1_ref, dqkv_ref, att_ref, dmid_ref, out_ref)
+
+
+def add_kernel(keep_ref, got_ref, out_ref):
     for chip in range(CHIPS_N):
-        both = keep_ref[chip].astype(F32) + got_ref[chip].astype(F32)
-        out_ref[chip, 0:SLOTS, :] = both.astype(BF16)
-        for rows, lanes in lane_blocks():
-            out_ref[chip, rows, :] = total[:, lanes]
-
-
-def share_kernel(parts_ref, out_ref):
-    total = total_of(parts_ref, slice(0, SLOTS))
-    for chip in range(CHIPS_N):
-        out_ref[chip] = total
-
-
-def compact_kernel(parts_ref, after_ref, done_ref):
+        out_ref[chip] = (keep_ref[chip].astype(F32) + got_ref[chip].astype(F32)).astype(BF16)
+
+
+def share_mlp_kernel(sums_ref, after_ref, tile_ref):
     del after_ref
-    for chip in range(CHIPS_N):
-        for rows, lanes in lane_blocks():
-            done_ref[chip * SHARE:(chip + 1) * SHARE, lanes] = parts_ref[chip, rows, :]
-
-
-def unpack_mlp_kernel(me_ref, mine_ref, theirs_ref, gup_ref, gdown_ref):
+    total = total_of(sums_ref, slice(0, SHARE))
+    for block in range(D // 128):
+        tile_ref[block * SHARE:(block + 1) * SHARE, :] = total[:, block * 128:(block + 1) * 128]
+
+
+def share_kernel(parts_hbm, tile_ref, dg1_ref, dg2_ref, out_ref, parts_ref, share_ref, sem, sems):
+    load = pltpu.make_async_copy(parts_hbm, parts_ref, sem)
+    load.start()
+    share_ref[GRADS + GAINS:, :] = tile_ref[...]
+    share_ref[GRADS:GRADS + GAINS, :] = jnp.concatenate(
+        [ref[:, block * 128:(block + 1) * 128] for ref in (dg1_ref, dg2_ref) for block in range(D // 128)]).astype(BF16)
+    load.wait()
+    share_ref[0:GRADS, :] = total_of(parts_ref, slice(0, GRADS))
+    copies = [pltpu.make_async_copy(share_ref, out_ref.at[chip], sems.at[chip]) for chip in range(CHIPS_N)]
+    for copy in copies:
+        copy.start()
+    for copy in copies:
+        copy.wait()
+
+
+def unpack_kernel(mine, half_ref, all_ref, gains_in, *refs):
+    (gup_hbm, gdown_hbm, gqkv_hbm, gout_hbm, gains_ref, gup_ref, gdown_ref, att_ref, sems) = refs if mine else refs[4:]
+    half = half_ref[0]
     wide = FF // 2
-    for ref, half in ((mine_ref, me_ref[0]), (theirs_ref, 1 - me_ref[0])):
+    copies = []
+
+    def send(source, target):
+        copies.append(pltpu.make_async_copy(source, target, sems.at[len(copies)]))
+        copies[-1].start()
+
+    blocks = [(slice(GRADS + GAINS + i * SHARE, GRADS + GAINS + (i + 1) * SHARE), i * 128) for i in range(D // 128)]
+    quarter = CHIPS_N // 4
+    for rows, lane in blocks:
+        gdown_ref[:, lane:lane + 128] = all_ref[2 * quarter:, rows, :].reshape(wide, 128).astype(F32)
+    send(gdown_ref, gdown_hbm.at[pl.ds(pl.multiple_of(half * wide, wide), wide), :])
+    for j in range(2):
+        for rows, lane in blocks:
+            piece = all_ref[j * quarter:(j + 1) * quarter, rows, :].reshape(D, 128)
+            gup_ref[:, j * D + lane:j * D + lane + 128] = piece.astype(F32)
+    send(gup_ref, gup_hbm.at[:, pl.ds(pl.multiple_of(half * wide, wide), wide)])
+    per = GRADS // 2
+    for part in range(4):
         for block in range(2):
-            lanes = pl.ds(pl.multiple_of(half * wide + block * D, D), D)
-            gup_ref[:, lanes] = ref[block * D:(block + 1) * D, :].astype(F32)
-        gdown_ref[pl.ds(pl.multiple_of(half * wide, wide), wide), :] = ref[2 * D:, :].astype(F32)
-
-
-def unpack_att_kernel(me_ref, mine_ref, theirs_ref, gqkv_ref, gout_ref, gains_ref):
-    quarter = CHIPS_N // 4
-    per = D // quarter
-    for ref, half in ((mine_ref, me_ref[0]), (theirs_ref, 1 - me_ref[0])):
-        for part in range(4):
-            for block in range(2):
-                piece = ref[part * quarter:(part + 1) * quarter, block * per:(block + 1) * per, :]
-                piece = piece.reshape(D, 128).astype(F32)
-                out, first = (gqkv_ref, part * D) if part < 3 else (gout_ref, 0)
-                out[:, pl.ds(pl.multiple_of(half * HALF + (first + block * 128), 128), 128)] = piece
-        for block in range(D // 128):
-            gains_ref[pl.ds(pl.multiple_of(half * 8, 8), 8), block * 128:(block + 1) * 128] = ref[block, 2 * per:, :].astype(F32)
+            piece = all_ref[part * quarter:(part + 1) * quarter, block * per:(block + 1) * per, :].reshape(D, 128)
+            att_ref[part, :, block * 128:(block + 1) * 128] = piece.astype(F32)
+        out, first = (gqkv_hbm, part * D) if part < 3 else (gout_hbm, 0)
+        send(att_ref.at[part], out.at[:, pl.ds(pl.multiple_of(half * HALF + first, HALF), HALF)])
+    gains = all_ref[0, GRADS:GRADS + GAINS, :].astype(F32)
+    for chip in range(1, CHIPS_N):
+        gains += all_ref[chip, GRADS:GRADS + GAINS, :].astype(F32)
+    gains_ref[...] = gains if mine else gains_in[...] + gains
+    for copy in copies:
+        copy.wait()
 
 
 def pack_kernel(tok_ref, cot_ref, lon_ref, lat_ref, corner_ref, sems):
@@ -489,8 +514,8 @@
         copy.wait()
 
 
-def place_kernel(out_in, grad_in, lon_ref, lat_ref, corner_ref, out_ref, grad_ref, sems):
-    del out_in, grad_in
+def place_kernel(out_in, grad_in, lon_ref, lat_ref, corner_ref, after_ref, out_ref, grad_ref, sems):
+    del out_in, grad_in, after_ref
     copies = []
     for which, ref in enumerate((out_ref, grad_ref)):
         below, right = pl.ds(HALF_LAT, ref.shape[0] - HALF_LAT), pl.ds(HALF_LON, ref.shape[1] - HALF_LON)
@@ -537,22 +562,22 @@
         name="pack",
         in_specs=[ANY] * 2,
         out_specs=[VM] * 3,
-        out_shape=rim_shapes(*tokens.shape[:3]),
+        out_shape=[local(rim.shape) for rim in rim_shapes(*tokens.shape[:3])],
         scratch_shapes=[pltpu.SemaphoreType.DMA((2, 3))],
     )(tokens, cotangent)
 
 
-def place(output, grad, lon, lat, corner):
+def place(output, grad, lon, lat, corner, after):
     return pl.pallas_call(
         place_kernel,
         name="place",
-        in_specs=[ANY] * 2 + [VM] * 3,
+        in_specs=[ANY] * 2 + [VM] * 3 + [ANY],
         out_specs=[ANY] * 2,
         out_shape=[shape(output.shape), shape(grad.shape)],
         input_output_aliases={0: 0, 1: 1},
         scratch_shapes=[pltpu.SemaphoreType.DMA((2, 3))],
         cost_estimate=cost(10**9, 2**21),
-    )(output, grad, lon, lat, corner)
+    )(output, grad, lon, lat, corner, after)
 
 
 WINDOWED = (BANDS, SIDES, WLAT, WLON, LEV, D)
@@ -622,92 +647,115 @@
     )(me, *held(n2, cot, wup, wdown, *carried))
 
 
-def back(me, cot, mid, down, dn2, wout, qkv, p, wqkv, x, att, n1, g1, g2, field):
-    tokens = x.shape[0]
+def back(cot, mid, down, dn2, wout, qkv, p, att, n1, g2):
+    tokens = cot.shape[0]
     count = tokens // WIN
+    halves = pltpu.VMEM((tokens, D), BF16)
+    full = pltpu.VMEM((tokens, D), F32)
     return pl.pallas_call(
         back_kernel,
         name="back",
-        in_specs=[SM] + [HB] * 11 + [VM] * 2,
-        out_specs=[ANY] * 5 + [VM] * 7,
-        out_shape=[shape(field), shape(field)] + rim_shapes(*field[:3]) + [
+        in_specs=[HB] * 9 + [VM],
+        out_specs=[HB] * 3 + [VM] * 5,
+        out_shape=[
+            pltpu.HBM((tokens, D), BF16),
+            pltpu.HBM((tokens, D), BF16),
+            pltpu.HBM((tokens, 3 * D), BF16),
+            shape((1, D), F32),
             local((tokens, D)),
             local((tokens, D)),
             local((tokens, D)),
             local((tokens, 3 * D)),
-            local((1, D), F32),
-            local((1, D), F32),
-            shape((CHIPS_N, SLOTS, 128)),
         ],
         scratch_shapes=[
-            pltpu.VMEM((tokens, D), BF16),
-            pltpu.VMEM((tokens, D), BF16),
-            pltpu.VMEM((tokens, D), F32),
-            pltpu.VMEM((tokens, D), F32),
+            halves,
+            halves,
+            full,
+            full,
             pltpu.VMEM((D, D), BF16),
             pltpu.VMEM((tokens, 3 * D), BF16),
             pltpu.VMEM((count, D // HD, WIN, WIN), BF16),
+            halves,
+            halves,
+            pltpu.SemaphoreType.DMA((9,)),
+            pltpu.SemaphoreType.DMA((3,)),
+        ],
+        compiler_params=params(40),
+        cost_estimate=cost(25 * 10**9, 10 * 2**20),
+    )(*far(cot, mid, down, dn2, wout, qkv, p, att, n1), g2)
+
+
+def token_grads(dqkv, wqkv, x, dmid, res, g1, after, field):
+    tokens = x.shape[0]
+    halves = pltpu.VMEM((tokens, D), BF16)
+    return pl.pallas_call(
+        tokens_kernel,
+        name="tokens",
+        in_specs=[HB] * 5 + [VM, ANY],
+        out_specs=[ANY] * 5 + [VM],
+        out_shape=[shape(field), shape(field)] + rim_shapes(*field[:3]) + [shape((1, D), F32)],
+        scratch_shapes=[
+            pltpu.VMEM((tokens, 3 * D), BF16),
             pltpu.VMEM((D, 3 * D), BF16),
-            pltpu.VMEM((tokens, D), BF16),
-            pltpu.VMEM((tokens, D), BF16),
-            pltpu.VMEM((tokens, D), BF16),
-            pltpu.VMEM((tokens, D), BF16),
+            halves,
+            halves,
+            halves,
+            halves,
             pltpu.VMEM(WINDOWED, BF16),
             pltpu.VMEM(WINDOWED, BF16),
-            pltpu.SemaphoreType.DMA((11,)),
+            pltpu.SemaphoreType.DMA((5,)),
             pltpu.SemaphoreType.DMA((2, STRIPS)),
         ],
-        compiler_params=params(40),
-        cost_estimate=cost(30 * 10**9, 10 * 2**20),
-    )(me, *far(cot, mid, down, dn2, wout, qkv, p, wqkv, x, att, n1), g1, g2)
-
-
-def keep_grads(me, n1, dqkv, att, dmid, dg1, dg2):
+        compiler_params=params(),
+        cost_estimate=cost(6 * 10**9, 10 * 2**20),
+    )(*far(dqkv, wqkv, x, dmid, res), g1, after)
+
+
+def half_grads(name, half, n1, dqkv, att, dmid):
     return pl.pallas_call(
-        keep_kernel,
-        name="keep",
-        in_specs=[SM] + [VM] * 6,
+        half_kernel,
+        name=name,
+        in_specs=[SM] + [VM] * 4,
         out_specs=VM,
-        out_shape=shape((CHIPS_N, SLOTS, 128)),
+        out_shape=local((CHIPS_N, GRADS, 128)),
         compiler_params=params(),
         cost_estimate=cost(4 * 10**9, 4 * 2**20),
-    )(me, *held(n1, dqkv, att, dmid, dg1, dg2))
-
-
-def simple(kernel, name, out_shape, *operands, moved=4 * 2**20, mib=56):
+    )(half, *held(n1, dqkv, att, dmid))
+
+
+def simple(kernel, name, out_shape, *operands, specs=None, scratch=(), mib=56):
     return pl.pallas_call(
         kernel,
         name=name,
-        in_specs=[VM] * len(operands),
-        out_specs=VM,
+        in_specs=specs or [VM] * len(operands),
+        out_specs=VM if not scratch else HB,
         out_shape=out_shape,
+        scratch_shapes=scratch,
         compiler_params=params(mib),
-        cost_estimate=cost(10**9, moved),
+        cost_estimate=cost(10**9, 4 * 2**20),
     )(*operands)
 
 
-def unpack_mlp(me, mine, theirs):
+def unpack(half, gathered, carried=None):
+    mine = carried is None
+    outs = [pltpu.HBM((D, FF), F32), pltpu.HBM((FF, D), F32), pltpu.HBM((D, 3 * D), F32), pltpu.HBM((D, D), F32)]
+    gains = jnp.zeros((GAINS, 128), F32) if mine else carried[4]
     return pl.pallas_call(
-        unpack_mlp_kernel,
-        name="unpack_mlp",
-        in_specs=[SM] + [VM] * 2,
-        out_specs=[VM, VM],
-        out_shape=[shape((D, FF), F32), shape((FF, D), F32)],
-        compiler_params=params(56),
-        cost_estimate=cost(10**9, 12 * 2**20),
-    )(me, mine, theirs)
-
-
-def unpack_att(me, mine, theirs):
-    return pl.pallas_call(
-        unpack_att_kernel,
-        name="unpack_att",
-        in_specs=[SM, VM, VM],
-        out_specs=[VM] * 3,
-        out_shape=[shape((D, 3 * D), F32), shape((D, D), F32), shape((16, D), F32)],
-        compiler_params=params(),
-        cost_estimate=cost(10**9, 6 * 2**20),
-    )(me, mine, theirs)
+        functools.partial(unpack_kernel, mine),
+        name="unpack_mine" if mine else "unpack_theirs",
+        in_specs=[SM, VM, VM] + ([] if mine else [HB] * 4),
+        out_specs=[HB] * 4 + [VM],
+        out_shape=outs + [shape((GAINS, 128), F32)],
+        scratch_shapes=[
+            pltpu.VMEM((D, FF // 2), F32),
+            pltpu.VMEM((FF // 2, D), F32),
+            pltpu.VMEM((4, D, HALF), F32),
+            pltpu.SemaphoreType.DMA((6,)),
+        ],
+        input_output_aliases={} if mine else {3: 0, 4: 1, 5: 2, 6: 3},
+        compiler_params=params(40),
+        cost_estimate=cost(10**9, 10 * 2**20),
+    )(half, gathered, gains, *([] if mine else far(*carried[:4])))
 
 
 LAT = ("x", "zl")
@@ -750,21 +798,32 @@
     down, dn2, early = mlp("first", *fixed, down, dn2)
     down, dn2, grads = mlp("second", *fixed, down, dn2, early, got)
     sums = exchange(grads.reshape(CHIPS_N, SHARE, D))
-    output, grad_tokens, lon, lat, corner, att, n1, dmid, dqkv, dg1, dg2, send = back(
-        me, cot_far, mid, down, dn2, w_out, qkv, p, w_qkv, x, att, n1, g1, g2, tokens.shape)
-    got = other_core(send)
+    res, dmid_far, dqkv_far, dg2, att, n1, dmid, dqkv = back(cot_far, mid, down, dn2, w_out, qkv, p, att, n1, g2)
+    got = other_core(half_grads("send", 1 - me, n1, dqkv, att, dmid))
+    keep = half_grads("keep", me, n1, dqkv, att, dmid)
+    added = simple(add_kernel, "add", pltpu.HBM((CHIPS_N, GRADS, 128), BF16), *held(keep, got), mib=32)
+    att_sums = exchange(added)
+    tile = simple(share_mlp_kernel, "share_mlp", shape((MLP, 128)), sums, added, specs=[VM, ANY])
+    output, grad_tokens, lon, lat, corner, dg1 = token_grads(
+        dqkv_far, w_qkv, x, dmid_far, res, g1, added, tokens.shape)
+    att_sums, tile, dg1 = lax.optimization_barrier((att_sums, tile, dg1))
     rims = send_rims(lon, lat, corner, 1)
-    keep = keep_grads(me, n1, dqkv, att, dmid, dg1, dg2)
-    output, grad_tokens = place(output, grad_tokens, *rims)
-    mixed = exchange(simple(merge_kernel, "merge", pltpu.HBM((CHIPS_N, MIXED, 128), BF16), sums, keep, got))
-    mixed, output, grad_tokens = lax.optimization_barrier((mixed, output, grad_tokens))
-    share = simple(share_kernel, "share", pltpu.HBM((CHIPS_N, SLOTS, 128), BF16), mixed)
-    att_mine = exchange(share)
-    mlp_mine = simple(compact_kernel, "compact", shape((FF, D)), mixed, share)
-    gup, gdown = unpack_mlp(me, mlp_mine, other_core(mlp_mine))
-    att_mine, gup, gdown = lax.optimization_barrier((att_mine, gup, gdown))
-    gqkv, gout, gains = unpack_att(me, att_mine, other_core(att_mine))
-    return (output, grad_tokens, gains[0], gqkv, gout, gains[8], gup, gdown)
+    shares = simple(
+        share_kernel, "share", pltpu.HBM((CHIPS_N, ALL, 128), BF16), *far(att_sums), tile, dg1, dg2,
+        specs=[HB, VM, VM, VM],
+        scratch=[
+            pltpu.VMEM((CHIPS_N, GRADS, 128), BF16),
+            pltpu.VMEM((ALL, 128), BF16),
+            pltpu.SemaphoreType.DMA,
+            pltpu.SemaphoreType.DMA((CHIPS_N,)),
+        ])
+    gathered = exchange(shares)
+    theirs = other_core(gathered)
+    grads = unpack(1 - me, theirs, unpack(me, gathered))
+    output, grad_tokens = place(output, grad_tokens, *rims, grads[4])
+    gup, gdown, gqkv, gout, gains = grads
+    gains = gains.reshape(2, D)
+    return (output, grad_tokens, gains[0], gqkv, gout, gains[1], gup, gdown)
 
 
 def solution(mesh):

time: 217 us -> 196 us (0.903)
  waiting for transfers between devices: 64.1 us -> 15 us
  blocking collectives: 0 us -> 45.2 us
  starting transfers between devices: 52.1 us -> 43 us
  Pallas kernels: 94.6 us -> 87.1 us
    all_to_all x0 -> x1, blocking collectives: none -> 45.2 us  [exchange(): return lax.all_to_all(parts, CHIPS, 0, 0, tiled=True)]
    ppermute x6, waiting for transfers between devices: 50 us -> 8.5 us  [send_rims(): moved.append(lax.ppermute(block, LAT + LON, route))]
    all_to_all x3 -> x2, starting transfers between devices: 31 us -> 21.9 us  [exchange(): return lax.all_to_all(parts, CHIPS, 0, 0, tiled=True)]
    all_to_all x3 -> x2, waiting for transfers between devices: 11.6 us -> 5.7 us  [exchange(): return lax.all_to_all(parts, CHIPS, 0, 0, tiled=True)]
    pallas_call x1, Pallas kernels: 16.8 us -> 12.7 us  [front(): pl.pallas_call(front_kernel, name='front', in_specs=[SM] + [ANY] * 5 + [V...]
    pallas_call x8 -> x10, Pallas kernels: 51.7 us -> 49.2 us  [the longest x1 21.6 us: back(): pl.pallas_call(back_kernel, name='back', in_specs=[HB] * 9 + [VM], out_sp...]
    ppermute x4 -> x3, starting transfers between devices: 5.66 us -> 7.57 us  [other_core(): return lax.ppermute(block, 'c', [(0, 1), (1, 0)])]
    unnamed x24 -> x30, local copies, waits for them, and re-layouts: 4.57 us -> 3.25 us
  transfers between devices with their start and end apart: 13 -> 11, of which waited for: 4 -> 5; matrix products, arithmetic and copies ran while one was open for 0% -> 0% of each run, Pallas kernels for 20% -> 24%
where the time goes in v4:
time: 196 us; the launch traced here: 195 us
  Pallas kernels  87.1 us (44%)
  blocking collectives  45.2 us (23%)
  starting transfers between devices  43 us (22%)
  waiting for transfers between devices  15 us (8%)
  local copies, waits for them, and re-layouts  3.84 us (2%)
    all_to_all x1, blocking collectives, exchange(): return lax.all_to_all(parts, CHIPS, 0, 0, tiled=True)  45.2 us
    pallas_call x3, Pallas kernels, mlp(): pl.pallas_call(kernel, name='mlp_' + kind, in_specs=[SM, VM, VM, VM, VM]...  23.7 us
    all_to_all x2, starting transfers between devices, exchange(): return lax.all_to_all(parts, CHIPS, 0, 0, tiled=True)  21.9 us
    pallas_call x1, Pallas kernels, back(): pl.pallas_call(back_kernel, name='back', in_specs=[HB] * 9 + [VM], out_sp...  21.6 us
    ppermute x6, starting transfers between devices, send_rims(): moved.append(lax.ppermute(block, LAT + LON, route))  13.5 us
    pallas_call x1, Pallas kernels, front(): pl.pallas_call(front_kernel, name='front', in_specs=[SM] + [ANY] * 5 + [V...  12.7 us
    ppermute x6, waiting for transfers between devices, send_rims(): moved.append(lax.ppermute(block, LAT + LON, route))  8.5 us
    pallas_call x1, Pallas kernels, token_grads(): pl.pallas_call(tokens_kernel, name='tokens', in_specs=[HB] * 5 + [VM, ANY...  8.33 us
  transfers between devices with their start and end apart: 11, of which 5 were waited for; matrix products, arithmetic and copies ran while one was open for 0% of the time, Pallas kernels for 24%

profile of v4, /device:TPU:1, one launch (start us, length us, event | category | flops | bytes accessed | tf_op | source)
XLA Modules:
  0.0 195.3 jit_solution(5776048940053859808)
XLA Ops:
  4.3 3.9 %collective-permute-start.1 = (bf16[2,3,18,2,512]{4,3,2,1,0:T(2,128)(2,1)S(1)}, bf16[2,3,18,2,512]{4,3,2,1,0:T(2,128)(2,1)S(1)}, u32[]{:S(2)}, u32[]{:S(2)}) collective-permute-start(bf16[2,3,18,2,512]{4,3,2,1,0:T(2,128)(2,1)S(1)} %get-tuple-element.59), channel_id=1, source_target_pairs={{0,112},{1,113},{2,114},{3,115},{4,116},{5,117},{6,118},{7,119},{8... | collective-permute-start | bytes 663560 | tf_op jit(solution)/shard_map/ppermute | solution.py:774
  8.2 5.8 %collective-permute-start.2 = (bf16[2,3,6,2,512]{4,3,2,1,0:T(2,128)(2,1)S(1)}, bf16[2,3,6,2,512]{4,3,2,1,0:T(2,128)(2,1)S(1)}, u32[]{:S(2)}, u32[]{:S(2)}) collective-permute-start(bf16[2,3,6,2,512]{4,3,2,1,0:T(2,128)(2,1)S(1)} %get-tuple-element.60), channel_id=1, source_target_pairs={{0,127},{1,112},{2,113},{3,114},{4,115},{5,116},{6,117},{7,118},{8... | collective-permute-start | bytes 221192 | tf_op jit(solution)/shard_map/ppermute | solution.py:774
  14.0 2.0 %collective-permute-done.2.corner_ref = bf16[2,3,6,2,512]{4,3,2,1,0:T(2,128)(2,1)S(1)} collective-permute-done((bf16[2,3,6,2,512]{4,3,2,1,0:T(2,128)(2,1)S(1)}, bf16[2,3,6,2,512]{4,3,2,1,0:T(2,128)(2,1)S(1)}, u32[]{:S(2)}, u32[]{:S(2)}) %collective-permute-start.2) | collective-permute-done | bytes 73760 | tf_op jit(solution)/shard_map/ppermute | solution.py:774
  16.1 12.7 %front.1 = (bf16[1152,512]{1,0:T(8,128)(2,1)}, bf16[1152,512]{1,0:T(8,128)(2,1)}, bf16[1152,1536]{1,0:T(8,128)(2,1)}, bf16[8,8,144,144]{3,2,1,0:T(8,128)(2,1)}, ...) custom-call(s32[1]{0:T(128)} %bitcast.flag_ref, ...), custom_call_target="tpu_custom_call" | custom-call | flops 15000000512 | bytes 10485760 | tf_op jit(solution)/shard_map/front/pallas_call | solution.py:602
  28.8 10.8 %mlp_send.1 = (f32[1152,512]{1,0:T(8,128)S(1)}, f32[1152,512]{1,0:T(8,128)S(1)}, bf16[2048,512]{1,0:T(8,128)(2,1)S(1)}) custom-call(s32[1]{0:T(128)} %bitcast.3.me_ref.half_ref, bf16[1152,512]{1,0:T(8,128)(2,1)S(1)} %get-tuple-element.63.n2_ref, bf16[1152,512]{1,0:T(8,128)(2,1)S(1)} %get-tuple-element.64.cot_ref, bf16[512,2048]{1,0:T(8,128)(2,1)S(1)} %copy-done.6, ...), custom_call_target="tpu_custom_call" | custom-call | flops 16000000000 | bytes 10485760 | tf_op jit(solution)/shard_map/mlp_send/pallas_call | solution.py:637
  39.5 3.6 %collective-permute-start.3 = (bf16[2048,512]{1,0:T(8,128)(2,1)S(1)}, bf16[2048,512]{1,0:T(8,128)(2,1)S(1)}, u32[]{:S(2)}, u32[]{:S(2)}) collective-permute-start(bf16[2048,512]{1,0:T(8,128)(2,1)S(1)} %get-tuple-element.70), channel_id=1, source_target_pairs={{0,1},{1,0},{2,3},{3,2},{4,5},{5,4},{6,7},{7,6},{8,9},{9,8},{10,11... | collective-permute-start | bytes 6291464 | tf_op jit(solution)/shard_map/ppermute | solution.py:779
  43.1 5.7 %mlp_first.1 = (f32[1152,512]{1,0:T(8,128)S(1)}, f32[1152,512]{1,0:T(8,128)S(1)}, bf16[1024,512]{1,0:T(8,128)(2,1)S(1)}) custom-call(s32[1]{0:T(128)} %bitcast.3.me_ref.half_ref, bf16[1152,512]{1,0:T(8,128)(2,1)S(1)} %get-tuple-element.63.n2_ref, bf16[1152,512]{1,0:T(8,128)(2,1)S(1)} %get-tuple-element.64.cot_ref, ...), custom_call_target="tpu_custom_call", output_to_operand_aliasing={{0}: (5, {}), {1}: (6, {})} | custom-call | flops 8000000000 | bytes 10485760 | tf_op jit(solution)/shard_map/mlp_first/pallas_call | solution.py:637
  48.8 7.3 %mlp_second.1 = (f32[1152,512]{1,0:T(8,128)}, f32[1152,512]{1,0:T(8,128)}, bf16[2048,512]{1,0:T(8,128)(2,1)}) custom-call(s32[1]{0:T(128)} %bitcast.3.me_ref.half_ref, bf16[1152,512]{1,0:T(8,128)(2,1)S(1)} %get-tuple-element.63.n2_ref, bf16[1152,512]{1,0:T(8,128)(2,1)S(1)} %get-tuple-element.64.cot_ref, bf16[512,2048]{1,0:T(8,128)(2,1)S(1)} %copy-done.6, ...), custom_call_target="tpu_custom_call" | custom-call | flops 8000000000 | bytes 10485760 | tf_op jit(solution)/shard_map/mlp_second/pallas_call | solution.py:637
  56.1 12.0 %all-to-all-start.1 = ((bf16[64,32,512]{2,1,0:T(8,128)(2,1)}), bf16[64,32,512]{2,1,0:T(8,128)(2,1)}, u32[]{:S(2)}, u32[]{:S(2)}) async-start(bf16[64,32,512]{2,1,0:T(8,128)(2,1)} %bitcast.13), calls=%async_computation.1 | async-start | bytes 4194304 | tf_op jit(solution)/shard_map/all_to_all | solution.py:783
  68.1 21.6 %back.1 = (bf16[1152,512]{1,0:T(8,128)(2,1)}, bf16[1152,512]{1,0:T(8,128)(2,1)}, bf16[1152,1536]{1,0:T(8,128)(2,1)}, f32[1,512]{1,0:T(1,128)S(1)}, bf16[1152,512...) custom-call(bf16[1152,512]{1,0:T(8,128)(2,1)} %get-tuple-element.61., ...), custom_call_target="tpu_custom_call" | custom-call | flops 24999999488 | bytes 10485760 | tf_op jit(solution)/shard_map/back/pallas_call | solution.py:655
  89.7 1.6 send.1
  92.1 1.6 keep.1.keep_ref
  95.8 10.0 %all-to-all-start = ((bf16[64,64,128]{2,1,0:T(8,128)(2,1)}), bf16[64,64,128]{2,1,0:T(8,128)(2,1)S(1)}, u32[]{:S(2)}, u32[]{:S(2)}) async-start(bf16[64,64,128]{2,1,0:T(8,128)(2,1)} %add.5.after_ref), calls=%async_computation | async-start | bytes 2097152 | tf_op jit(solution)/shard_map/all_to_all | solution.py:783
  105.8 8.3 %tokens.1 = (bf16[24,24,2,512]{3,2,1,0:T(2,128)(2,1)}, bf16[24,24,2,512]{3,2,1,0:T(2,128)(2,1)}, bf16[2,21,6,2,512]{4,3,2,1,0:T(2,128)(2,1)S(1)}, bf16[2,3,18,2,...) custom-call(bf16[1152,1536]{1,0:T(8,128)(2,1)} %get-tuple-element.77.dqkv_hbm, ...), custom_call_target="tpu_custom_call" | custom-call | flops 6000000000 | bytes 10485760 | tf_op jit(solution)/shard_map/tokens/pallas_call | solution.py:691
  114.7 2.5 %share_mlp.1.tile_ref = bf16[128,128]{1,0:T(8,128)(2,1)} custom-call(bf16[64,32,512]{2,1,0:T(8,128)(2,1)} %all-to-all-done.1.sums_ref, bf16[64,64,128]{2,1,0:T(8,128)(2,1)} %add.5.after_ref), custom_call_target="tpu_custom_call" | custom-call | flops 1000000000 | bytes 4194304 | tf_op jit(solution)/shard_map/share_mlp/pallas_call | solution.py:727
  117.2 5.5 %all-to-all-done.parts_hbm = bf16[64,64,128]{2,1,0:T(8,128)(2,1)S(1)} async-done(((bf16[64,64,128]{2,1,0:T(8,128)(2,1)}), bf16[64,64,128]{2,1,0:T(8,128)(2,1)S(1)}, u32[]{:S(2)}, u32[]{:S(2)}) %all-to-all-start) | async-done | bytes 1048608 | tf_op jit(solution)/shard_map/all_to_all | solution.py:783
  123.7 4.4 %share.1 = bf16[64,200,128]{2,1,0:T(8,128)(2,1)} custom-call(bf16[64,64,128]{2,1,0:T(8,128)(2,1)} %copy-done.11, bf16[128,128]{1,0:T(8,128)(2,1)} %share_mlp.1.tile_ref, f32[1,512]{1,0:T(1,128)} %copy-done.5, f32[1,512]{1,0:T(1,128)} %copy-done.4), custom_call_target="tpu_custom_call" | custom-call | flops 1000000000 | bytes 4194304 | tf_op jit(solution)/shard_map/share/pallas_call | solution.py:727
  128.1 45.2 %all_to_all.15.all_ref = bf16[64,200,128]{2,1,0:T(8,128)(2,1)S(1)} all-to-all(bf16[64,200,128]{2,1,0:T(8,128)(2,1)} %share.1), channel_id=1, replica_groups=mesh['x'=4,'zl'=2,'zh'=2,'y'=4,'c'=2] {'x','zl','zh','y'}, dimensions={0} | all-to-all | bytes 6553600 | tf_op jit(solution)/shard_map/all_to_all | solution.py:783
  173.4 3.1 %collective-permute-start.8 = (bf16[64,200,128]{2,1,0:T(8,128)(2,1)S(1)}, bf16[64,200,128]{2,1,0:T(8,128)(2,1)S(1)}, u32[]{:S(2)}, u32[]{:S(2)}) collective-permute-start(bf16[64,200,128]{2,1,0:T(8,128)(2,1)S(1)} %all_to_all.15.all_ref), channel_id=1, source_target_pairs={{0,1},{1,0},{2,3},{3,2},{4,5},{5,4},{6,7},{7,6},{8,9},{9,8},{10,11... | collective-permute-start | bytes 9830408 | tf_op jit(solution)/shard_map/ppermute | solution.py:779
  177.1 1.9 collective-permute-start.7
  179.0 3.0 %unpack_mine.1 = (f32[512,2048]{1,0:T(8,128)}, f32[2048,512]{1,0:T(8,128)}, f32[512,1536]{1,0:T(8,128)}, f32[512,512]{1,0:T(8,128)}, f32[8,128]{1,0:T(8,128)S(1)}) custom-call(s32[1]{0:T(128)} %bitcast.3.me_ref.half_ref, bf16[64,200,128]{2,1,0:T(8,128)(2,1)S(1)} %all_to_all.15.all_ref, f32[8,128]{1,0:T(8,128)S(1)} %broadcast_in_dim.3.gains_in), custom_call_target="tpu_custom_call" | custom-call | flops 1000000000 | bytes 10485760 | tf_op jit(solution)/shard_map/unpack_mine/pallas_call | solution.py:743
  182.0 3.0 %unpack_theirs.1 = (f32[512,2048]{1,0:T(8,128)}, f32[2048,512]{1,0:T(8,128)}, f32[512,1536]{1,0:T(8,128)}, f32[512,512]{1,0:T(8,128)}, f32[8,128]{1,0:T(8,128)S(1)}) custom-call(s32[1]{0:T(128)S(6)} %sub.4.half_ref, ...), custom_call_target="tpu_custom_call", output_to_operand_aliasing={{0}: (3, {}), {1}: (4, {}), {2}: (5, {}), {3}: (6, {})} | custom-call | flops 1000000000 | bytes 10485760 | tf_op jit(solution)/shard_map/unpack_theirs/pallas_call | solution.py:743
  185.6 6.5 %collective-permute-done.7.corner_ref = bf16[2,3,6,2,512]{4,3,2,1,0:T(2,128)(2,1)S(1)} collective-permute-done((bf16[2,3,6,2,512]{4,3,2,1,0:T(2,128)(2,1)S(1)}, bf16[2,3,6,2,512]{4,3,2,1,0:T(2,128)(2,1)S(1)}, u32[]{:S(2)}, u32[]{:S(2)}) %collective-permute-start.7) | collective-permute-done | bytes 73760 | tf_op jit(solution)/shard_map/ppermute | solution.py:774
  193.0 2.1 %place.1 = (bf16[24,24,2,512]{3,2,1,0:T(2,128)(2,1)}, bf16[24,24,2,512]{3,2,1,0:T(2,128)(2,1)}) custom-call(bf16[24,24,2,512]{3,2,1,0:T(2,128)(2,1)} %get-tuple-element.85.out_in, bf16[24,24,2,512]{3,2,1,0:T(2,128)(2,1)} %get-tuple-element.86.grad_in, bf16[2,21,6,2,512]{4,3,2,1,0:T(2,128)(2,1)} %copy-done.12, ...), custom_call_target="tpu_custom_call", output_to_operand_aliasing={{0}: (0, {}), {1}: (1, {})} | custom-call | flops 1000000000 | bytes 2097152 | tf_op jit(solution)/shard_map/place/pallas_call | solution.py:571
  (46 shorter events, 10.2 us)
Async XLA Ops:
  0.6 15.4 %copy-start = (bf16[24,24,2,512]{3,2,1,0:T(2,128)(2,1)S(1)}, bf16[24,24,2,512]{3,2,1,0:T(2,128)(2,1)}, u32[]{:S(2)}) copy-start(bf16[24,24,2,512]{3,2,1,0:T(2,128)(2,1)} %tok_ref.3) | copy-start | bytes 3538948
  0.6 15.4 %copy-start.1 = (bf16[24,24,2,512]{3,2,1,0:T(2,128)(2,1)S(1)}, bf16[24,24,2,512]{3,2,1,0:T(2,128)(2,1)}, u32[]{:S(2)}) copy-start(bf16[24,24,2,512]{3,2,1,0:T(2,128)(2,1)} %cot_ref.3) | copy-start | bytes 3538948
  0.7 15.4 %copy-start.10 = (f32[512]{0:T(512)S(1)}, f32[512]{0:T(512)}, u32[]{:S(2)}) copy-start(f32[512]{0:T(512)} %param.10) | copy-start | bytes 6148
  0.7 15.4 %copy-start.9 = (f32[512]{0:T(512)S(1)}, f32[512]{0:T(512)}, u32[]{:S(2)}) copy-start(f32[512]{0:T(512)} %param.13) | copy-start | bytes 6148
  2.1 0.8 copy-start.8
  2.9 13.1 %collective-permute-start = (bf16[2,21,6,2,512]{4,3,2,1,0:T(2,128)(2,1)}, bf16[2,21,6,2,512]{4,3,2,1,0:T(2,128)(2,1)S(1)}, u32[]{:S(2)}, u32[]{:S(2)}) collective-permute-start(bf16[2,21,6,2,512]{4,3,2,1,0:T(2,128)(2,1)} %copy-done.8), channel_id=1, source_target_pairs={{0,15},{1,0},{2,1},{3,2},{4,3},{5,4},{6,5},{7,6},{8,7},{9,8},{10,9... | collective-permute-start | bytes 1548296 | tf_op jit(solution)/shard_map/ppermute | solution.py:774
  4.3 11.7 %collective-permute-start.1 = (bf16[2,3,18,2,512]{4,3,2,1,0:T(2,128)(2,1)S(1)}, bf16[2,3,18,2,512]{4,3,2,1,0:T(2,128)(2,1)S(1)}, u32[]{:S(2)}, u32[]{:S(2)}) collective-permute-start(bf16[2,3,18,2,512]{4,3,2,1,0:T(2,128)(2,1)S(1)} %get-tuple-element.59), channel_id=1, source_target_pairs={{0,112},{1,113},{2,114},{3,115},{4,116},{5,117},{6,118},{7,119},{8... | collective-permute-start | bytes 663560 | tf_op jit(solution)/shard_map/ppermute | solution.py:774
  8.2 7.8 %collective-permute-start.2 = (bf16[2,3,6,2,512]{4,3,2,1,0:T(2,128)(2,1)S(1)}, bf16[2,3,6,2,512]{4,3,2,1,0:T(2,128)(2,1)S(1)}, u32[]{:S(2)}, u32[]{:S(2)}) collective-permute-start(bf16[2,3,6,2,512]{4,3,2,1,0:T(2,128)(2,1)S(1)} %get-tuple-element.60), channel_id=1, source_target_pairs={{0,127},{1,112},{2,113},{3,114},{4,115},{5,116},{6,117},{7,118},{8... | collective-permute-start | bytes 221192 | tf_op jit(solution)/shard_map/ppermute | solution.py:774
  16.0 12.7 %copy-start.6 = (bf16[512,2048]{1,0:T(8,128)(2,1)S(1)}, bf16[512,2048]{1,0:T(8,128)(2,1)}, u32[]{:S(2)}) copy-start(bf16[512,2048]{1,0:T(8,128)(2,1)} %wup_ref.5) | copy-start | bytes 6291460
  16.0 12.7 %copy-start.7 = (bf16[2048,512]{1,0:T(8,128)(2,1)S(1)}, bf16[2048,512]{1,0:T(8,128)(2,1)}, u32[]{:S(2)}) copy-start(bf16[2048,512]{1,0:T(8,128)(2,1)} %wdown_ref.5) | copy-start | bytes 6291460
  39.5 9.3 %collective-permute-start.3 = (bf16[2048,512]{1,0:T(8,128)(2,1)S(1)}, bf16[2048,512]{1,0:T(8,128)(2,1)S(1)}, u32[]{:S(2)}, u32[]{:S(2)}) collective-permute-start(bf16[2048,512]{1,0:T(8,128)(2,1)S(1)} %get-tuple-element.70), channel_id=1, source_target_pairs={{0,1},{1,0},{2,3},{3,2},{4,5},{5,4},{6,7},{7,6},{8,9},{9,8},{10,11... | collective-permute-start | bytes 6291464 | tf_op jit(solution)/shard_map/ppermute | solution.py:779
  56.1 39.7 %all-to-all-start.1 = ((bf16[64,32,512]{2,1,0:T(8,128)(2,1)}), bf16[64,32,512]{2,1,0:T(8,128)(2,1)}, u32[]{:S(2)}, u32[]{:S(2)}) async-start(bf16[64,32,512]{2,1,0:T(8,128)(2,1)} %bitcast.13), calls=%async_computation.1 | async-start | bytes 4194304 | tf_op jit(solution)/shard_map/all_to_all | solution.py:783
  89.7 1.6 copy-start.4
  91.3 3.1 %collective-permute-start.4 = (bf16[64,64,128]{2,1,0:T(8,128)(2,1)S(1)}, bf16[64,64,128]{2,1,0:T(8,128)(2,1)S(1)}, u32[]{:S(2)}, u32[]{:S(2)}) collective-permute-start(bf16[64,64,128]{2,1,0:T(8,128)(2,1)S(1)} %send.1), channel_id=1, source_target_pairs={{0,1},{1,0},{2,3},{3,2},{4,5},{5,4},{6,7},{7,6},{8,9},{9,8},{10,11... | collective-permute-start | bytes 3145736 | tf_op jit(solution)/shard_map/ppermute | solution.py:779
  95.6 10.2 %copy-start.2 = (bf16[64,64,128]{2,1,0:T(8,128)(2,1)S(1)}, bf16[64,64,128]{2,1,0:T(8,128)(2,1)}, u32[]{:S(2)}) copy-start(bf16[64,64,128]{2,1,0:T(8,128)(2,1)} %add.5.after_ref) | copy-start | bytes 3145732
  95.8 26.9 %all-to-all-start = ((bf16[64,64,128]{2,1,0:T(8,128)(2,1)}), bf16[64,64,128]{2,1,0:T(8,128)(2,1)S(1)}, u32[]{:S(2)}, u32[]{:S(2)}) async-start(bf16[64,64,128]{2,1,0:T(8,128)(2,1)} %add.5.after_ref), calls=%async_computation | async-start | bytes 2097152 | tf_op jit(solution)/shard_map/all_to_all | solution.py:783
  122.7 1.0 copy-start.11
  173.4 8.6 %collective-permute-start.8 = (bf16[64,200,128]{2,1,0:T(8,128)(2,1)S(1)}, bf16[64,200,128]{2,1,0:T(8,128)(2,1)S(1)}, u32[]{:S(2)}, u32[]{:S(2)}) collective-permute-start(bf16[64,200,128]{2,1,0:T(8,128)(2,1)S(1)} %all_to_all.15.all_ref), channel_id=1, source_target_pairs={{0,1},{1,0},{2,3},{3,2},{4,5},{5,4},{6,7},{7,6},{8,9},{9,8},{10,11... | collective-permute-start | bytes 9830408 | tf_op jit(solution)/shard_map/ppermute | solution.py:779
  176.5 15.6 %collective-permute-start.5 = (bf16[2,21,6,2,512]{4,3,2,1,0:T(2,128)(2,1)S(1)}, bf16[2,21,6,2,512]{4,3,2,1,0:T(2,128)(2,1)S(1)}, u32[]{:S(2)}, u32[]{:S(2)}) collective-permute-start(bf16[2,21,6,2,512]{4,3,2,1,0:T(2,128)(2,1)S(1)} %get-tuple-element.87), channel_id=1, source_target_pairs={{0,1},{1,2},{2,3},{3,4},{4,5},{5,6},{6,7},{7,8},{8,9},{9,10},{10,1... | collective-permute-start | bytes 1548296 | tf_op jit(solution)/shard_map/ppermute | solution.py:774
  177.1 15.0 %collective-permute-start.6 = (bf16[2,3,18,2,512]{4,3,2,1,0:T(2,128)(2,1)S(1)}, bf16[2,3,18,2,512]{4,3,2,1,0:T(2,128)(2,1)S(1)}, u32[]{:S(2)}, u32[]{:S(2)}) collective-permute-start(bf16[2,3,18,2,512]{4,3,2,1,0:T(2,128)(2,1)S(1)} %get-tuple-element.88), channel_id=1, source_target_pairs={{0,16},{1,17},{2,18},{3,19},{4,20},{5,21},{6,22},{7,23},{8,24},{9,... | collective-permute-start | bytes 663560 | tf_op jit(solution)/shard_map/ppermute | solution.py:774
  177.1 15.0 %collective-permute-start.7 = (bf16[2,3,6,2,512]{4,3,2,1,0:T(2,128)(2,1)S(1)}, bf16[2,3,6,2,512]{4,3,2,1,0:T(2,128)(2,1)S(1)}, u32[]{:S(2)}, u32[]{:S(2)}) collective-permute-start(bf16[2,3,6,2,512]{4,3,2,1,0:T(2,128)(2,1)S(1)} %get-tuple-element.89), channel_id=1, source_target_pairs={{0,17},{1,18},{2,19},{3,20},{4,21},{5,22},{6,23},{7,24},{8,25},{9,... | collective-permute-start | bytes 221192 | tf_op jit(solution)/shard_map/ppermute | solution.py:774
  185.0 7.1 %copy-start.3 = (f32[8,128]{1,0:T(8,128)}, f32[8,128]{1,0:T(8,128)S(1)}, u32[]{:S(2)}) copy-start(f32[8,128]{1,0:T(8,128)S(1)} %get-tuple-element.101.after_ref) | copy-start | bytes 12292
  192.1 0.7 copy-start.13
  192.1 0.9 copy-start.12
  (2 other events, 1.2 us)
